TPU v7x, 512 devices: a whole 4x8x8 slice. The times are simulated.
512 devices in a mesh: row: 16 (over z_lo, x), col: 32 (over z_hi, y, core).
Axes of the slice: x: 4, y: 8, z: 8 (z_hi: 2, z_lo: 4; z = z_hi * 4 + z_lo), core: 2. Of those that a mesh axis runs over, the one named last changes fastest.
Arguments:
- features: bfloat16 [65536, 256], P(('col', 'row')), may hold values from -6 to 6
- weight: bfloat16 [256, 256], replicated, may hold values from -0.375 to 0.375
- cotangent: bfloat16 [65536, 256], P(('row', 'col')), may hold values from -6 to 6
- blocks: bfloat16 [16, 32, 96, 128, 128], P('row', 'col'), may hold values from -0.078125 to 0.078125
- block_pos: int32 [16, 32, 96], P('row', 'col'), may hold values from 0 to 511, as said below
- counts: int32 [16, 32], P('row', 'col'), may hold values from 1 to 96, as said below
Outputs:
- output: bfloat16 [65536, 256], P(('row', 'col'))
- input_grad: bfloat16 [65536, 256], P(('col', 'row'))
- weight_grad: float32 [256, 256], replicated
Inputs may be any that keep to these rules, and one draw needn't show every extreme that they name: `block_pos`: within one tile the first counts[r, c] slots name distinct positions; the later slots carry no block. `counts`: some tile lists all 96 slots in every draw; loads differ widely between tiles.
All inputs are finite; a program needn't handle non-finite values.
Results may differ from a plain program's by a relative error of at most 0.029.
Values may be sent and summed in bfloat16 or wider, within the bound.
No kernel may reach another device: no remote copies, remote signals or barrier semaphores. Data moves between devices by JAX's collectives and lax.ppermute only.
A program may use at most 128 MiB of HBM per device.

v0:
```python
import math

import jax
import jax.numpy as jnp
from jax import lax
from jax.sharding import PartitionSpec as P


def slope_of(pre):
    sigma = jax.nn.sigmoid(pre)
    return sigma * (1.0 + pre * (1.0 - sigma))


def member_table(index, valid, extent):
    return jnp.where(
        (index[None, :] == jnp.arange(extent, dtype=jnp.int32)[:, None]) & valid[None, :], 1.0, 0.0
    ).astype(jnp.float32)


def spread(members, products):
    return jnp.einsum("bk,kif->bif", members, products, precision=lax.Precision.HIGHEST)


def shards(features, weight, cotangent, blocks, block_pos, counts):
    rows_dev, width = features.shape
    tile = blocks[0, 0]
    place = block_pos[0, 0]
    count = counts[0, 0]
    slots, side = (tile.shape[0], tile.shape[1])
    height = lax.axis_size("col") * rows_dev // side
    breadth = lax.axis_size("row") * rows_dev // side
    valid = jnp.arange(slots, dtype=jnp.int32) < count
    target = place // breadth
    anchor = place % breadth
    column_nodes = lax.all_gather(features, "row", axis=0, tiled=True).reshape(breadth, side, width)
    picked = jnp.take(column_nodes, anchor, axis=0)
    products = jnp.einsum("kij,kjf->kif", tile, picked, preferred_element_type=jnp.float32)
    partial_value = spread(member_table(target, valid, height), products).reshape(
        height * side, width
    )
    share = lax.psum_scatter(
        partial_value.astype(jnp.bfloat16), "col", scatter_dimension=0, tiled=True
    )
    pre = jnp.dot(share, weight, preferred_element_type=jnp.float32)
    output = jax.nn.silu(pre).astype(jnp.bfloat16)
    slopes = (cotangent.astype(jnp.float32) * slope_of(pre)).astype(jnp.bfloat16)
    row_slopes = lax.all_gather(slopes, "col", axis=0, tiled=True)
    local_grad = lax.dot_general(
        share, slopes, (((0,), (0,)), ((), ())), preferred_element_type=jnp.float32
    )
    weight_grad = lax.psum(local_grad, ("row", "col"))
    nodes_total = rows_dev * lax.axis_size("row") * lax.axis_size("col")
    weight_grad = weight_grad * (1.0 / math.sqrt(nodes_total))
    grouped = row_slopes.reshape(height, side, width)
    picked_back = jnp.take(grouped, target, axis=0)
    products_back = jnp.einsum(
        "kji,kjf->kif", tile, picked_back, preferred_element_type=jnp.float32
    )
    partial_back = spread(member_table(anchor, valid, breadth), products_back).reshape(
        breadth * side, width
    )
    back = lax.psum_scatter(
        partial_back.astype(jnp.bfloat16), "row", scatter_dimension=0, tiled=True
    )
    input_grad = jnp.dot(back, weight.T, preferred_element_type=jnp.float32).astype(jnp.bfloat16)
    return (output, input_grad, weight_grad)


def solution(mesh):
    placed = (
        P(("col", "row"), None),
        P(),
        P(("row", "col"), None),
        P("row", "col", None, None, None),
        P("row", "col", None),
        P("row", "col"),
    )
    return jax.shard_map(
        shards,
        mesh=mesh,
        in_specs=placed,
        out_specs=(P(("row", "col"), None), P(("col", "row"), None), P()),
        check_vma=False,
    )
```

profile of v0, /device:TPU:6, one launch (start us, length us, event | category | flops | bytes accessed | tf_op | source)
XLA Modules:
  0.0 721.3 jit_solution(7425514510913558549)
XLA Ops:
  7.2 0.0 copy-start
  7.2 0.0 all-gather.3.cloned.1.call-start
  7.2 0.7 all-gather.3.cloned.1.call-update
  7.9 0.0 reduce-scatter.3.cloned.1.call-start
  8.8 0.7 fusion.37
  9.4 0.7 compare_and_fusion
  10.1 84.0 %all-gather.3.cloned.1.call-done = bf16[2048,256]{1,0:T(8,128)(2,1)} async-done(((bf16[128,256]{1,0:T(8,128)(2,1)}), bf16[2048,256]{1,0:T(8,128)(2,1)}) %all-gather.3.cloned.1.call-update) | async-done | bytes 1048592 | tf_op jit(solution)/shard_map/all_gather | solution.py:35
  94.1 7.1 gather_fusion
  101.3 0.0 copy-done
  101.3 9.3 %fusion.6 = f32[96,256,128]{2,1,0:T(8,128)} fusion(bf16[96,128,256]{2,1,0:T(8,128)(2,1)} %gather_fusion, pred[96]{0:T(512)(128)(4,1)S(1)} %get-tuple-element.11, bf16[1,1,96,128,128]{4,3,2,1,0:T(8,128)(2,1)S(1)} %copy-done), kind=kOutput, calls=%fused_computation.8 | convolution fusion | flops 808452096 | bytes 22020192 | tf_op jit(solution)/shard_map/kij,kjf->kif/dot_general | solution.py:37
  110.5 12.7 %copy.11 = f32[96,256,128]{1,0,2:T(8,128)} copy(f32[96,256,128]{2,1,0:T(8,128)} %fusion.6) | data formatting | bytes 25165824 | tf_op jit(solution)/shard_map/kij,kjf->kif/dot_general | solution.py:37
  123.3 9.0 %fusion.14 = bf16[32,128,256]{2,0,1:T(8,128)(2,1)S(1)} fusion(f32[96,256,128]{1,0,2:T(8,128)} %copy.11, s32[96]{0:T(128)S(1)} %get-tuple-element.4, pred[96]{0:T(512)(128)(4,1)S(1)} %get-tuple-element.13), kind=kOutput, calls=%fused_computation.16 | convolution fusion | flops 1209017344 | bytes 14680544 | tf_op jit(solution)/shard_map/bk,kif->bif/dot_general | solution.py:21
  132.2 0.0 copy-start.1
  132.2 0.0 copy-start.2
  132.2 2.5 copy.9
  134.8 0.0 reduce-scatter.3.cloned.1.call-update
  134.8 0.0 all-gather.5.cloned.1.call-start
  134.8 138.9 %reduce-scatter.3.cloned.1.call-done = bf16[128,256]{1,0:T(8,128)(2,1)} async-done(((bf16[4096,256]{1,0:T(8,128)(2,1)}), bf16[128,256]{1,0:T(8,128)(2,1)}) %reduce-scatter.3.cloned.1.call-update) | async-done | bytes 65552 | tf_op jit(solution)/shard_map/reduce_scatter | solution.py:41
  273.7 0.0 copy-done.1
  273.7 0.0 copy-done.2
  273.7 1.7 multiply_convert_fusion
  275.5 0.0 all-gather.5.cloned.1.call-update
  275.5 0.0 all-reduce.2.cloned.1.call-start
  275.5 1.8 fusion.44
  277.3 0.0 all-reduce.2.cloned.1.call-update
  277.4 0.2 reduce-scatter.5.cloned.1.call-start
  277.6 90.0 %all-gather.5.cloned.1.call-done = bf16[4096,256]{1,0:T(8,128)(2,1)} async-done(((bf16[128,256]{1,0:T(8,128)(2,1)}), bf16[4096,256]{1,0:T(8,128)(2,1)}) %all-gather.5.cloned.1.call-update) | async-done | bytes 2097168 | tf_op jit(solution)/shard_map/all_gather | solution.py:47
  367.6 7.5 %gather_fusion.1 = bf16[96,128,256]{2,1,0:T(8,128)(2,1)} fusion(bf16[32,128,256]{2,1,0:T(8,128)(2,1)} %bitcast.72, s32[1024]{0:T(1024)S(1)} %pad_clamp_fusion), kind=kCustom, calls=%fused_computation.1 | custom fusion | bytes 12583296 | tf_op jit(solution)/shard_map/jit(_take)/gather | solution.py:55
  375.1 9.3 %fusion.4 = f32[96,256,128]{2,1,0:T(8,128)} fusion(bf16[96,128,256]{2,1,0:T(8,128)(2,1)} %gather_fusion.1, pred[96]{0:T(512)(128)(4,1)S(1)} %get-tuple-element.3, bf16[1,1,96,128,128]{4,3,2,1,0:T(8,128)(2,1)S(1)} %copy-done), kind=kOutput, calls=%fused_computation.6 | convolution fusion | flops 808452096 | bytes 22020192 | tf_op jit(solution)/shard_map/kji,kjf->kif/dot_general | solution.py:56
  384.3 12.7 %copy.12 = f32[96,256,128]{1,0,2:T(8,128)} copy(f32[96,256,128]{2,1,0:T(8,128)} %fusion.4) | data formatting | bytes 25165824 | tf_op jit(solution)/shard_map/kji,kjf->kif/dot_general | solution.py:56
  397.1 8.6 %fusion.17 = bf16[16,128,256]{2,0,1:T(8,128)(2,1)S(1)} fusion(f32[96,256,128]{1,0,2:T(8,128)} %copy.12, s32[96]{0:T(128)S(1)} %get-tuple-element.12, pred[96]{0:T(512)(128)(4,1)S(1)} %get-tuple-element.13), kind=kOutput, calls=%fused_computation.17 | convolution fusion | flops 604508672 | bytes 13631968 | tf_op jit(solution)/shard_map/bk,kif->bif/dot_general | solution.py:21
  405.6 1.3 copy.10
  407.0 0.0 reduce-scatter.5.cloned.1.call-update
  407.0 225.9 %all-reduce.2.cloned.1.call-done = f32[256,256]{1,0:T(8,128)} async-done(((f32[256,256]{1,0:T(8,128)}), f32[256,256]{1,0:T(8,128)}) %all-reduce.2.cloned.1.call-update) | async-done | bytes 262160 | tf_op jit(solution)/shard_map/psum | solution.py:51
  632.9 1.7 broadcast_multiply_fusion
  634.6 78.5 %reduce-scatter.5.cloned.1.call-done = bf16[128,256]{1,0:T(8,128)(2,1)} async-done(((bf16[2048,256]{1,0:T(8,128)(2,1)}), bf16[128,256]{1,0:T(8,128)(2,1)}) %reduce-scatter.5.cloned.1.call-update) | async-done | bytes 65552 | tf_op jit(solution)/shard_map/reduce_scatter | solution.py:62
  713.1 1.7 convolution_convert_fusion
  (2 shorter events, 0.0 us)
Async XLA Ops:
  7.2 94.1 %copy-start = (bf16[1,1,96,128,128]{4,3,2,1,0:T(8,128)(2,1)S(1)}, bf16[1,1,96,128,128]{4,3,2,1,0:T(8,128)(2,1)}, u32[]{:S(2)}) copy-start(bf16[1,1,96,128,128]{4,3,2,1,0:T(8,128)(2,1)} %param.9) | copy-start | bytes 9437188
  7.2 86.9 %all-gather.3.cloned.1.call-start = ((), (), s32[]{:S(2)}) async-start(), calls=%async_computation.2 | async-start | bytes 1114112 | tf_op jit(solution)/shard_map/all_gather | solution.py:35
  7.9 265.8 %reduce-scatter.3.cloned.1.call-start = ((), (), s32[]{:S(2)}) async-start(), calls=%async_computation.3 | async-start | bytes 2162688 | tf_op jit(solution)/shard_map/reduce_scatter | solution.py:41
  132.2 141.5 %copy-start.1 = (bf16[256,256]{1,0:T(8,128)(2,1)S(1)}, bf16[256,256]{1,0:T(8,128)(2,1)}, u32[]{:S(2)}) copy-start(bf16[256,256]{1,0:T(8,128)(2,1)} %param.7) | copy-start | bytes 393220
  132.2 141.5 %copy-start.2 = (bf16[128,256]{1,0:T(8,128)(2,1)S(1)}, bf16[128,256]{1,0:T(8,128)(2,1)}, u32[]{:S(2)}) copy-start(bf16[128,256]{1,0:T(8,128)(2,1)} %param.8) | copy-start | bytes 196612
  134.8 232.8 %all-gather.5.cloned.1.call-start = ((), (), s32[]{:S(2)}) async-start(), calls=%async_computation.4 | async-start | bytes 2162688 | tf_op jit(solution)/shard_map/all_gather | solution.py:47
  275.5 357.4 %all-reduce.2.cloned.1.call-start = ((), (), s32[]{:S(2)}) async-start(), calls=%async_computation.6 | async-start | bytes 524288 | tf_op jit(solution)/shard_map/psum | solution.py:51
  277.4 435.7 %reduce-scatter.5.cloned.1.call-start = ((), (), s32[]{:S(2)}) async-start(), calls=%async_computation.5 | async-start | bytes 1114112 | tf_op jit(solution)/shard_map/reduce_scatter | solution.py:62
Sparse Core Ops, SparseCore 0:
  10.1 83.9 all-gather.2
  134.9 138.7 reduce-scatter.2
  278.2 89.3 all-gather.4
  373.7 259.1 all-reduce.1
  635.6 77.4 reduce-scatter.4
where the time goes:
time: 731 us; the launch traced here: 721 us
  waiting for transfers between devices  618 us (85%)
  local copies, waits for them, and re-layouts  44 us (6%)
  matrix products  41.3 us (6%)
  between operations  14.6 us (2%)
    psum x1, waiting for transfers between devices, shards(): weight_grad = lax.psum(local_grad, ('row', 'col'))  226 us
    reduce_scatter x1, waiting for transfers between devices, shards(): lax.psum_scatter(partial_value.astype(jnp.bfloat16), 'col', scatter_dimen...  139 us
    all_gather x1, waiting for transfers between devices, shards(): row_slopes = lax.all_gather(slopes, 'col', axis=0, tiled=True)  90 us
    all_gather x1, waiting for transfers between devices, shards(): lax.all_gather(features, 'row', axis=0, tiled=True)  84 us
    reduce_scatter x1, waiting for transfers between devices, shards(): lax.psum_scatter(partial_back.astype(jnp.bfloat16), 'row', scatter_dimens...  78.5 us
    dot_general x2, matrix products, spread(): jnp.einsum('bk,kif->bif', members, products, precision=lax.Precision.HIGH...  17.5 us
  transfers between devices with their start and end apart: 5, of which 5 were waited for; matrix products, arithmetic and copies ran while one was open for 6% of the time, Pallas kernels for 0%

commit v1 on v0

v1 whole, which is shorter than its diff:
```python
import functools
import math

import jax
import jax.numpy as jnp
from jax import lax
from jax.experimental import pallas as pl
from jax.experimental.pallas import tpu as pltpu
from jax.sharding import Mesh
from jax.sharding import PartitionSpec as P

BF = jnp.bfloat16
F32 = jnp.float32
GROUP = 4
VMEM = pl.BlockSpec(memory_space=pltpu.VMEM)
SMEM = pl.BlockSpec(memory_space=pltpu.SMEM)
LIMIT = pltpu.CompilerParams(vmem_limit_bytes=48 * 1024 * 1024)


def dot(a, b, dims=(((1,), (0,)), ((), ()))):
    return lax.dot_general(a, b, dims, preferred_element_type=F32)


def forward_kernel(place, info, blocks, nodes, keep, send, acc):
    acc[...] = jnp.zeros_like(acc)
    count, core = info[0], info[1]

    def step(i, _):
        products = []
        for g in range(GROUP):
            k = i * GROUP + g
            p = place[k]
            t, a = p // 16, p % 16
            source = nodes[(a % 4) * 4 + a // 4]
            slot = ((t % 2) ^ core) * 16 + t // 2
            products.append((jnp.where(k < count, slot, 32), dot(blocks[k], source)))
        for slot, product in products:
            acc[slot] += product
        return 0

    lax.fori_loop(0, pl.cdiv(count, GROUP), step, 0)
    keep[...] = acc[0:16].astype(BF)
    send[...] = acc[16:32].astype(BF)


def middle_kernel(parts, weight, cotangent, output, spread):
    total = parts[0].astype(F32)
    for s in range(1, 16):
        total += parts[s].astype(F32)
    share = total.astype(BF)
    pre = dot(share, weight[...])
    sigma = 1.0 / (1.0 + jnp.exp(-pre))
    output[...] = (pre * sigma).astype(BF)
    slope = sigma * (1.0 + pre * (1.0 - sigma))
    slopes32 = cotangent[...].astype(F32) * slope
    slopes = slopes32.astype(BF)
    turned = slopes.astype(F32).T.astype(BF)
    grad = dot(share.astype(F32).T.astype(BF), slopes).astype(BF)
    for s in range(16):
        spread[s, 0:256, :] = turned
        spread[s, 256:272, :] = grad[16 * s : 16 * s + 16, 0:128]
        spread[s, 272:288, :] = grad[16 * s : 16 * s + 16, 128:256]


def split(value):
    high = value.astype(BF)
    return high, (value - high.astype(F32)).astype(BF)


def backward_kernel(place, info, blocks, own, other, out, acc):
    acc[...] = jnp.zeros_like(acc)
    count, core = info[0], info[1]

    def step(i, _):
        products = []
        for g in range(GROUP):
            k = i * GROUP + g
            p = place[k]
            t, a = p // 16, p % 16
            h = t // 2
            source = jnp.where(t % 2 == core, own[h, 0:256, :], other[h, 0:256, :])
            slot = (a % 4) * 4 + a // 4
            products.append((jnp.where(k < count, slot, 16), dot(source, blocks[k])))
        for slot, product in products:
            acc[slot] += product
        return 0

    lax.fori_loop(0, pl.cdiv(count, GROUP), step, 0)
    grad = jnp.zeros((32, 128), F32)
    for s in range(16):
        grad += own[s, 256:288, :].astype(F32) + other[s, 256:288, :].astype(F32)
    high, low = split(grad)
    for x in range(4):
        for z in range(4):
            out[x, 256 * z : 256 * z + 256, :] = acc[4 * x + z].astype(BF)
        out[x, 1024:1056, :] = high
        out[x, 1056:1088, :] = low


def fold_kernel(parts, out):
    for z in range(4):
        rows = slice(256 * z, 256 * z + 256)
        total = parts[0, rows, :].astype(F32)
        for x in range(1, 4):
            total += parts[x, rows, :].astype(F32)
        out[z, 0:256, :] = total.astype(BF)
    grad = jnp.zeros((32, 128), F32)
    for x in range(4):
        grad += parts[x, 1024:1056, :].astype(F32) + parts[x, 1056:1088, :].astype(F32)
    high, low = split(grad)
    for z in range(4):
        out[z, 256:288, :] = high
        out[z, 288:320, :] = low


def last_kernel(scale, parts, weight, input_grad, grad_out):
    total = parts[0, 0:256, :].astype(F32)
    for z in range(1, 4):
        total += parts[z, 0:256, :].astype(F32)
    back = total.astype(BF).astype(F32).T.astype(BF)
    input_grad[...] = dot(back, weight[...], (((1,), (1,)), ((), ()))).astype(BF)
    grad = jnp.zeros((32, 128), F32)
    for z in range(4):
        grad += parts[z, 256:288, :].astype(F32) + parts[z, 288:320, :].astype(F32)
    grad = grad * scale
    for s in range(16):
        grad_out[s, :, 0:128] = grad[0:16]
        grad_out[s, :, 128:256] = grad[16:32]


def call(kernel, shapes, kinds, scratch=(), flops=0, size=0):
    return pl.pallas_call(
        kernel,
        out_shape=[jax.ShapeDtypeStruct(s, d) for s, d in shapes],
        in_specs=kinds,
        out_specs=[VMEM] * len(shapes),
        scratch_shapes=list(scratch),
        compiler_params=LIMIT,
        cost_estimate=pl.CostEstimate(flops=flops, bytes_accessed=size, transcendentals=0),
    )


def exchange(value, axes):
    return lax.all_to_all(value, axes, 0, 0, tiled=True)


def swap(value):
    return lax.ppermute(value, "c", [(0, 1), (1, 0)])


def shards(features, weight, cotangent, blocks, block_pos, counts):
    tile = blocks[0, 0]
    place = block_pos[0, 0]
    info = jnp.stack([counts[0, 0], lax.axis_index("c").astype(jnp.int32)])
    nodes_total = 65536

    lines = exchange(jnp.broadcast_to(features[None], (4, 128, 256)), "zl")
    nodes = exchange(jnp.broadcast_to(lines[None], (4, 4, 128, 256)), "x").reshape(16, 128, 256)
    keep, send = call(
        forward_kernel,
        [((16, 128, 256), BF)] * 2,
        [SMEM, SMEM, VMEM, VMEM],
        [pltpu.VMEM((33, 128, 256), F32)],
        flops=8 * 10**8,
        size=6 * 2**20,
    )(place, info, tile, nodes)
    pair = (keep.astype(F32) + swap(send).astype(F32)).astype(BF)
    parts = exchange(pair, ("zh", "y"))
    output, spread = call(
        middle_kernel,
        [((128, 256), BF), ((16, 288, 128), BF)],
        [VMEM, VMEM, VMEM],
    )(parts, weight, cotangent)
    own = exchange(spread, ("zh", "y"))
    other = swap(own)
    (back,) = call(
        backward_kernel,
        [((4, 1088, 128), BF)],
        [SMEM, SMEM, VMEM, VMEM, VMEM],
        [pltpu.VMEM((17, 256, 128), F32)],
        flops=8 * 10**8,
        size=6 * 2**20,
    )(place, info, tile, own, other)
    (folded,) = call(fold_kernel, [((4, 320, 128), BF)], [VMEM])(exchange(back, "x"))
    input_grad, grad = call(
        functools.partial(last_kernel, 1.0 / math.sqrt(nodes_total)),
        [((128, 256), BF), ((16, 16, 256), F32)],
        [VMEM, VMEM],
    )(exchange(folded, "zl"), weight)
    weight_grad = exchange(grad, ("zh", "y")).reshape(256, 256)
    return (output, input_grad, weight_grad)


def solution(mesh):
    names = ("zl", "x", "zh", "y", "c")
    row, col = names[:2], names[2:]
    fine = Mesh(mesh.devices.reshape(4, 4, 2, 8, 2), names)
    return jax.shard_map(
        shards,
        mesh=fine,
        in_specs=(
            P(col + row, None),
            P(),
            P(row + col, None),
            P(row, col, None, None, None),
            P(row, col, None),
            P(row, col),
        ),
        out_specs=(P(row + col, None), P(col + row, None), P()),
        check_vma=False,
    )
```

time: 731 us -> 196 us (0.27)
  waiting for transfers between devices: 618 us -> 15.5 us
  blocking collectives: 0 us -> 154 us
  local copies, waits for them, and re-layouts: 44 us -> 2.65 us
  matrix products: 41.3 us -> 0 us
  between operations: 14.6 us -> 1.35 us
  Pallas kernels: 0 us -> 10.7 us
  starting transfers between devices: 0.38 us -> 8.73 us
    psum x1 -> x0, waiting for transfers between devices: 226 us -> none  [shards(): weight_grad = lax.psum(local_grad, ('row', 'col'))]
    reduce_scatter x2 -> x0, waiting for transfers between devices: 217 us -> none  [the longest x1 139 us: shards(): lax.psum_scatter(partial_value.astype(jnp.bfloat16), 'col', scatter_dimen...]
    all_gather x2 -> x0, waiting for transfers between devices: 174 us -> none  [the longest x1 90 us: shards(): row_slopes = lax.all_gather(slopes, 'col', axis=0, tiled=True)]
    all_to_all x0 -> x6, blocking collectives: none -> 154 us  [exchange(): return lax.all_to_all(value, axes, 0, 0, tiled=True)]
    dot_general x7 -> x0, matrix products: 41.3 us -> none  [the longest x2 17.5 us: spread(): jnp.einsum('bk,kif->bif', members, products, precision=lax.Precision.HIGH...]
    dot_general x2 -> x0, local copies, waits for them, and re-layouts: 25.4 us -> none  [the longest x1 12.7 us: shards(): jnp.einsum('kji,kjf->kif', tile, picked_back, preferred_element_type=jnp....]
    gather x2 -> x0, local copies, waits for them, and re-layouts: 14.7 us -> none  [the longest x1 7.52 us: shards(): picked_back = jnp.take(grouped, target, axis=0)]
    pallas_call x0 -> x5, Pallas kernels: none -> 10.7 us  [the longest x1 4.5 us: shards(): call(forward_kernel, [((16, 128, 256), BF)] * 2, [SMEM, SMEM, VMEM, VMEM]...]
  transfers between devices with their start and end apart: 5 -> 3, of which waited for: 5 -> 3; matrix products, arithmetic and copies ran while one was open for 6% -> 0% of each run, Pallas kernels for 0% -> 0%
where the time goes in v1:
time: 196 us; the launch traced here: 193 us
  blocking collectives  154 us (79%)
  waiting for transfers between devices  15.5 us (8%)
  Pallas kernels  10.7 us (5%)
  starting transfers between devices  8.73 us (4%)
  local copies, waits for them, and re-layouts  2.65 us (1%)
    all_to_all x6, blocking collectives, exchange(): return lax.all_to_all(value, axes, 0, 0, tiled=True)  154 us
    all_to_all x1, waiting for transfers between devices, exchange(): return lax.all_to_all(value, axes, 0, 0, tiled=True)  10.1 us
    ppermute x2, waiting for transfers between devices, swap(): return lax.ppermute(value, 'c', [(0, 1), (1, 0)])  5.44 us
    all_to_all x1, starting transfers between devices, exchange(): return lax.all_to_all(value, axes, 0, 0, tiled=True)  4.9 us
    pallas_call x1, Pallas kernels, shards(): call(forward_kernel, [((16, 128, 256), BF)] * 2, [SMEM, SMEM, VMEM, VMEM]...  4.5 us
    pallas_call x1, Pallas kernels, shards(): call(backward_kernel, [((4, 1088, 128), BF)], [SMEM, SMEM, VMEM, VMEM, VM...  4.3 us
  transfers between devices with their start and end apart: 3, of which 3 were waited for; matrix products, arithmetic and copies ran while one was open for 0% of the time, Pallas kernels for 0%

profile of v1, /device:TPU:6, one launch (start us, length us, event | category | flops | bytes accessed | tf_op | source)
XLA Modules:
  0.0 193.4 jit_solution(4112467396483333682)
XLA Ops:
  0.6 0.9 broadcast_in_dim.4
  1.5 15.9 %all_to_all.35 = bf16[4,128,256]{2,1,0:T(8,128)(2,1)S(1)} all-to-all(bf16[4,128,256]{2,1,0:T(8,128)(2,1)S(1)} %broadcast_in_dim.4), channel_id=1, replica_groups=mesh['zl'=4,'x'=4,'zh'=2,'y'=8,'c'=2] {'zl'}, dimensions={0} | all-to-all | bytes 524288 | tf_op jit(solution)/shard_map/all_to_all | solution.py:144
  17.4 1.1 broadcast_in_dim.5
  18.5 0.0 copy-start.2
  18.5 4.9 %all-to-all-start.1 = ((bf16[4,4,128,256]{3,2,1,0:T(8,128)(2,1)}), bf16[4,4,128,256]{3,2,1,0:T(8,128)(2,1)S(1)}, u32[]{:S(2)}, u32[]{:S(2)}) async-start(bf16[4,4,128,256]{3,2,1,0:T(8,128)(2,1)} %broadcast_in_dim.5), calls=%async_computation.1 | async-start | bytes 2097152 | tf_op jit(solution)/shard_map/all_to_all | solution.py:144
  24.0 0.1 pad_add_fusion.info
  24.1 10.1 %all-to-all-done.1 = bf16[4,4,128,256]{3,2,1,0:T(8,128)(2,1)S(1)} async-done(((bf16[4,4,128,256]{3,2,1,0:T(8,128)(2,1)}), bf16[4,4,128,256]{3,2,1,0:T(8,128)(2,1)S(1)}, u32[]{:S(2)}, u32[]{:S(2)}) %all-to-all-start.1) | async-done | bytes 1048608 | tf_op jit(solution)/shard_map/all_to_all | solution.py:144
  34.2 0.0 copy-done.2
  34.2 4.5 %shard_map.85 = (bf16[16,128,256]{2,1,0:T(8,128)(2,1)S(1)}, bf16[16,128,256]{2,1,0:T(8,128)(2,1)S(1)}) custom-call(s32[96]{0:T(128)S(1)} %bitcast.8, s32[2]{0:T(128)S(1)} %pad_add_fusion.info, bf16[96,128,128]{2,1,0:T(8,128)(2,1)} %bitcast.10, bf16[16,128,256]{2,1,0:T(8,128)(2,1)S(1)} %bitcast.7), custom_call_target="tpu_custom_call" | custom-call | flops 800000000 | bytes 6291456 | tf_op jit(solution)/shard_map/pallas_call | solution.py:159
  38.7 1.9 collective-permute-start
  40.6 2.6 %collective-permute-done = bf16[16,128,256]{2,1,0:T(8,128)(2,1)S(1)} collective-permute-done((bf16[16,128,256]{2,1,0:T(8,128)(2,1)S(1)}, bf16[16,128,256]{2,1,0:T(8,128)(2,1)S(1)}, u32[]{:S(2)}, u32[]{:S(2)}) %collective-permute-start) | collective-permute-done | bytes 1048608 | tf_op jit(solution)/shard_map/ppermute | solution.py:148
  43.2 0.3 add_convert_fusion
  43.6 0.0 copy-start
  43.6 0.0 copy-start.1
  43.6 47.3 %all_to_all.36.parts = bf16[16,128,256]{2,1,0:T(8,128)(2,1)S(1)} all-to-all(bf16[16,128,256]{2,1,0:T(8,128)(2,1)S(1)} %add_convert_fusion), channel_id=1, replica_groups=mesh['zl'=4,'x'=4,'zh'=2,'y'=8,'c'=2] {'zh','y'}, dimensions={0} | all-to-all | bytes 2097152 | tf_op jit(solution)/shard_map/all_to_all | solution.py:144
  90.9 0.0 copy-done
  90.9 0.0 copy-done.1
  90.9 0.9 shard_map.86
  91.8 39.6 %all_to_all.37.own = bf16[16,288,128]{2,1,0:T(8,128)(2,1)S(1)} all-to-all(bf16[16,288,128]{2,1,0:T(8,128)(2,1)S(1)} %get-tuple-element.12), channel_id=1, replica_groups=mesh['zl'=4,'x'=4,'zh'=2,'y'=8,'c'=2] {'zh','y'}, dimensions={0} | all-to-all | bytes 2359296 | tf_op jit(solution)/shard_map/all_to_all | solution.py:144
  131.5 1.9 collective-permute-start.1
  133.4 2.8 %collective-permute-done.1.other = bf16[16,288,128]{2,1,0:T(8,128)(2,1)S(1)} collective-permute-done((bf16[16,288,128]{2,1,0:T(8,128)(2,1)S(1)}, bf16[16,288,128]{2,1,0:T(8,128)(2,1)S(1)}, u32[]{:S(2)}, u32[]{:S(2)}) %collective-permute-start.1) | collective-permute-done | bytes 1179680 | tf_op jit(solution)/shard_map/ppermute | solution.py:148
  136.2 4.3 %shard_map.87 = bf16[4,1088,128]{2,1,0:T(8,128)(2,1)S(1)} custom-call(s32[96]{0:T(128)S(1)} %bitcast.9, s32[2]{0:T(128)S(1)} %pad_add_fusion.info, bf16[96,128,128]{2,1,0:T(8,128)(2,1)} %bitcast.11, bf16[16,288,128]{2,1,0:T(8,128)(2,1)S(1)} %all_to_all.37.own, bf16[16,288,128]{2,1,0:T(8,128)(2,1)S(1)} %collective-permute-done.1.other), custom_call_target="tpu_custom_call" | custom-call | flops 800000000 | bytes 6291456 | tf_op jit(solution)/shard_map/pallas_call | solution.py:176
  140.5 18.3 %all_to_all.38.parts = bf16[4,1088,128]{2,1,0:T(8,128)(2,1)S(1)} all-to-all(bf16[4,1088,128]{2,1,0:T(8,128)(2,1)S(1)} %shard_map.87), channel_id=1, replica_groups=mesh['zl'=4,'x'=4,'zh'=2,'y'=8,'c'=2] {'x'}, dimensions={0} | all-to-all | bytes 2228224 | tf_op jit(solution)/shard_map/all_to_all | solution.py:144
  158.8 0.1 shard_map.88
  159.0 13.5 %all_to_all.39.parts = bf16[4,320,128]{2,1,0:T(8,128)(2,1)S(1)} all-to-all(bf16[4,320,128]{2,1,0:T(8,128)(2,1)S(1)} %shard_map.88), channel_id=1, replica_groups=mesh['zl'=4,'x'=4,'zh'=2,'y'=8,'c'=2] {'zl'}, dimensions={0} | all-to-all | bytes 655360 | tf_op jit(solution)/shard_map/all_to_all | solution.py:144
  172.5 0.9 shard_map.89
  173.3 19.4 %all_to_all.40 = f32[16,16,256]{2,1,0:T(8,128)S(1)} all-to-all(f32[16,16,256]{2,1,0:T(8,128)S(1)} %get-tuple-element.14), channel_id=1, replica_groups=mesh['zl'=4,'x'=4,'zh'=2,'y'=8,'c'=2] {'zh','y'}, dimensions={0} | all-to-all | bytes 524288 | tf_op jit(solution)/shard_map/all_to_all | solution.py:144
  192.7 0.7 copy.11
Async XLA Ops:
  18.5 15.7 %copy-start.2 = (s32[1,1,96]{2,1,0:T(1,128)S(1)}, s32[1,1,96]{2,1,0:T(1,128)}, u32[]{:S(2)}) copy-start(s32[1,1,96]{2,1,0:T(1,128)} %param.10) | copy-start | bytes 1156
  18.5 15.7 %all-to-all-start.1 = ((bf16[4,4,128,256]{3,2,1,0:T(8,128)(2,1)}), bf16[4,4,128,256]{3,2,1,0:T(8,128)(2,1)S(1)}, u32[]{:S(2)}, u32[]{:S(2)}) async-start(bf16[4,4,128,256]{3,2,1,0:T(8,128)(2,1)} %broadcast_in_dim.5), calls=%async_computation.1 | async-start | bytes 2097152 | tf_op jit(solution)/shard_map/all_to_all | solution.py:144
  38.7 4.6 %collective-permute-start = (bf16[16,128,256]{2,1,0:T(8,128)(2,1)S(1)}, bf16[16,128,256]{2,1,0:T(8,128)(2,1)S(1)}, u32[]{:S(2)}, u32[]{:S(2)}) collective-permute-start(bf16[16,128,256]{2,1,0:T(8,128)(2,1)S(1)} %get-tuple-element.10), channel_id=1, source_target_pairs={{0,1},{1,0},{2,3},{3,2},{4,5},{5,4},{6,7},{7,6},{8,9},{9,8},{10,11... | collective-permute-start | bytes 3145736 | tf_op jit(solution)/shard_map/ppermute | solution.py:148
  43.6 47.3 %copy-start = (bf16[256,256]{1,0:T(8,128)(2,1)S(1)}, bf16[256,256]{1,0:T(8,128)(2,1)}, u32[]{:S(2)}) copy-start(bf16[256,256]{1,0:T(8,128)(2,1)} %weight.3) | copy-start | bytes 393220
  43.6 47.3 %copy-start.1 = (bf16[128,256]{1,0:T(8,128)(2,1)S(1)}, bf16[128,256]{1,0:T(8,128)(2,1)}, u32[]{:S(2)}) copy-start(bf16[128,256]{1,0:T(8,128)(2,1)} %cotangent.1) | copy-start | bytes 196612
  131.5 4.7 %collective-permute-start.1 = (bf16[16,288,128]{2,1,0:T(8,128)(2,1)S(1)}, bf16[16,288,128]{2,1,0:T(8,128)(2,1)S(1)}, u32[]{:S(2)}, u32[]{:S(2)}) collective-permute-start(bf16[16,288,128]{2,1,0:T(8,128)(2,1)S(1)} %all_to_all.37.own), channel_id=1, source_target_pairs={{0,1},{1,0},{2,3},{3,2},{4,5},{5,4},{6,7},{7,6},{8,9},{9,8},{10,11... | collective-permute-start | bytes 3538952 | tf_op jit(solution)/shard_map/ppermute | solution.py:148

commit v2 on v1

v2 whole, which is shorter than its diff:
```python
import functools
import math

import jax
import jax.numpy as jnp
from jax import lax
from jax.experimental import pallas as pl
from jax.experimental.pallas import tpu as pltpu
from jax.sharding import Mesh
from jax.sharding import PartitionSpec as P

BF = jnp.bfloat16
F32 = jnp.float32
GROUP = 16
SLOTS = 112
VMEM = pl.BlockSpec(memory_space=pltpu.VMEM)
SMEM = pl.BlockSpec(memory_space=pltpu.SMEM)
LIMIT = pltpu.CompilerParams(vmem_limit_bytes=48 * 1024 * 1024)


def dot(a, b, dims=(((1,), (0,)), ((), ()))):
    return lax.dot_general(a, b, dims, preferred_element_type=F32)


def plan_kernel(place, info, lists, groups):
    count, core, xi, zi = info[0], info[1], info[2], info[3]

    def write(at, k, t, source, half, target):
        for f, value in enumerate((k, t, source, half, target)):
            lists[f * 2 * SLOTS + at] = value

    def step(k, held):
        p = place[k]
        t, a = p >> 4, p & 15
        z, x = a >> 2, a & 3
        half = t >> 1
        source = (((xi - x) & 3) << 2) + ((zi - z) & 3)
        target = (((x - xi) & 3) << 2) + ((z - zi) & 3)
        mine, theirs = held
        away = (t & 1) ^ core
        write(jnp.where(away == 0, mine, SLOTS + theirs), k, half, source, half, target)
        return mine + 1 - away, theirs + away

    mine, theirs = lax.fori_loop(0, count, step, (jnp.int32(0), jnp.int32(0)))
    for i, n in enumerate((mine, theirs)):
        for g in range(GROUP):
            write(i * SLOTS + n + g, 0, 16, 0, 0, 16)
        groups[i] = (n + GROUP - 1) // GROUP


def entry(lists, which, field, j):
    return lists[field * 2 * SLOTS + which * SLOTS + j]


def forward_kernel(which, lists, groups, blocks, g0, g1, g2, g3, out, nodes, acc):
    for i, part in enumerate((g0, g1, g2, g3)):
        nodes[4 * i : 4 * i + 4] = part[...]
    acc[...] = jnp.zeros_like(acc)

    def step(i, _):
        products = []
        for g in range(GROUP):
            j = i * GROUP + g
            product = dot(blocks[entry(lists, which, 0, j)], nodes[entry(lists, which, 2, j)])
            products.append((entry(lists, which, 1, j), product))
        for slot, product in products:
            acc[slot] += product
        return 0

    lax.fori_loop(0, groups[which], step, 0)
    out[...] = acc[0:16].astype(BF)


def middle_kernel(parts, weight, cotangent, output, spread):
    total = parts[0].astype(F32)
    for s in range(1, 16):
        total += parts[s].astype(F32)
    share = total.astype(BF)
    pre = dot(share, weight[...])
    sigma = 1.0 / (1.0 + jnp.exp(-pre))
    output[...] = (pre * sigma).astype(BF)
    slope = sigma * (1.0 + pre * (1.0 - sigma))
    slopes32 = cotangent[...].astype(F32) * slope
    slopes = slopes32.astype(BF)
    turned = slopes.astype(F32).T.astype(BF)
    grad = dot(share.astype(F32).T.astype(BF), slopes).astype(BF)
    for s in range(16):
        spread[s, 0:256, :] = turned
        spread[s, 256:272, :] = grad[16 * s : 16 * s + 16, 0:128]
        spread[s, 272:288, :] = grad[16 * s : 16 * s + 16, 128:256]


def split(value):
    high = value.astype(BF)
    return high, (value - high.astype(F32)).astype(BF)


def back_products(which, lists, groups, blocks, source, acc):
    def step(i, _):
        products = []
        for g in range(GROUP):
            j = i * GROUP + g
            product = dot(source[entry(lists, which, 3, j), 0:256, :], blocks[entry(lists, which, 0, j)])
            products.append((entry(lists, which, 4, j), product))
        for slot, product in products:
            acc[slot] += product
        return 0

    lax.fori_loop(0, groups[which], step, 0)


def backward_own_kernel(lists, groups, blocks, own, acc):
    acc[...] = jnp.zeros_like(acc)
    back_products(0, lists, groups, blocks, own, acc)


def backward_other_kernel(lists, groups, blocks, own, other, begun, b0, b1, b2, b3, acc):
    acc[...] = begun[...]
    back_products(1, lists, groups, blocks, other, acc)
    grad = jnp.zeros((32, 128), F32)
    for s in range(16):
        grad += own[s, 256:288, :].astype(F32) + other[s, 256:288, :].astype(F32)
    high, low = split(grad)
    for x, out in enumerate((b0, b1, b2, b3)):
        for z in range(4):
            out[256 * z : 256 * z + 256, :] = acc[4 * x + z].astype(BF)
        out[1024:1056, :] = high
        out[1056:1088, :] = low


def ordered_sum(me, parts, row, scratch):
    for k, part in enumerate(parts):
        high, low = part[row : row + 32, :], part[row + 32 : row + 64, :]
        scratch[(me - k) & 3] = high.astype(F32) + low.astype(F32)
    return scratch[0] + scratch[1] + scratch[2] + scratch[3]


def fold_kernel(info, b0, b1, b2, b3, f0, f1, f2, f3, scratch):
    parts = (b0, b1, b2, b3)
    high, low = split(ordered_sum(info[2], parts, 1024, scratch))
    for z, out in enumerate((f0, f1, f2, f3)):
        rows = slice(256 * z, 256 * z + 256)
        total = parts[0][rows, :].astype(F32)
        for part in parts[1:]:
            total += part[rows, :].astype(F32)
        out[0:256, :] = total.astype(BF)
        out[256:288, :] = high
        out[288:320, :] = low


def last_kernel(scale, info, f0, f1, f2, f3, weight, input_grad, grad_out, scratch):
    parts = (f0, f1, f2, f3)
    grad = ordered_sum(info[3], parts, 256, scratch) * scale
    for s in range(16):
        grad_out[s, :, 0:128] = grad[0:16]
        grad_out[s, :, 128:256] = grad[16:32]
    total = parts[0][0:256, :].astype(F32)
    for part in parts[1:]:
        total += part[0:256, :].astype(F32)
    back = total.astype(BF).astype(F32).T.astype(BF)
    input_grad[...] = dot(back, weight[...], (((1,), (1,)), ((), ()))).astype(BF)


def call(kernel, outs, kinds, scratch=(), flops=0, size=0):
    return pl.pallas_call(
        kernel,
        out_shape=[jax.ShapeDtypeStruct(s, d) for s, d, _ in outs],
        in_specs=kinds,
        out_specs=[k for _, _, k in outs],
        scratch_shapes=list(scratch),
        compiler_params=LIMIT,
        cost_estimate=pl.CostEstimate(flops=flops, bytes_accessed=size, transcendentals=0),
    )


def exchange(value, axes):
    return lax.all_to_all(value, axes, 0, 0, tiled=True)


def swap(value):
    return lax.ppermute(value, "c", [(0, 1), (1, 0)])


def rotate(value, axis, k):
    return lax.ppermute(value, axis, [(i, (i + k) % 4) for i in range(4)])


def shards(features, weight, cotangent, blocks, block_pos, counts):
    tile = blocks[0, 0]
    index = [lax.axis_index(a).astype(jnp.int32) for a in ("c", "x", "zl")]
    info = jnp.stack([counts[0, 0]] + index)
    nodes_total = 65536
    heavy = dict(flops=8 * 10**8, size=6 * 2**20)
    i32 = jnp.int32

    lists, groups = call(
        plan_kernel,
        [((10 * SLOTS,), i32, SMEM), ((2,), i32, SMEM)],
        [SMEM, SMEM],
        size=2**20,
    )(block_pos[0, 0], info)

    line = jnp.stack([features] + [rotate(features, "zl", k) for k in (1, 2, 3)])
    plane = [line] + [rotate(line, "x", k) for k in (1, 2, 3)]
    send, keep = [
        call(
            functools.partial(forward_kernel, which),
            [((16, 128, 256), BF, VMEM)],
            [SMEM, SMEM] + [VMEM] * 5,
            [pltpu.VMEM((16, 128, 256), BF), pltpu.VMEM((17, 128, 256), F32)],
            **heavy,
        )(lists, groups, tile, *plane)[0]
        for which in (1, 0)
    ]
    pair = (keep.astype(F32) + swap(send).astype(F32)).astype(BF)
    parts = exchange(pair, ("zh", "y"))
    output, spread = call(
        middle_kernel,
        [((128, 256), BF, VMEM), ((16, 288, 128), BF, VMEM)],
        [VMEM, VMEM, VMEM],
    )(parts, weight, cotangent)
    own = exchange(spread, ("zh", "y"))
    other = swap(own)
    (begun,) = call(
        backward_own_kernel,
        [((17, 256, 128), F32, VMEM)],
        [SMEM, SMEM, VMEM, VMEM],
        **heavy,
    )(lists, groups, tile, own)
    back = call(
        backward_other_kernel,
        [((1088, 128), BF, VMEM)] * 4,
        [SMEM, SMEM] + [VMEM] * 4,
        [pltpu.VMEM((17, 256, 128), F32)],
        **heavy,
    )(lists, groups, tile, own, other, begun)
    back = [back[0]] + [rotate(back[k], "x", k) for k in (1, 2, 3)]
    folded = call(
        fold_kernel,
        [((320, 128), BF, VMEM)] * 4,
        [SMEM] + [VMEM] * 4,
        [pltpu.VMEM((4, 32, 128), F32)],
    )(info, *back)
    folded = [folded[0]] + [rotate(folded[k], "zl", k) for k in (1, 2, 3)]
    input_grad, grad = call(
        functools.partial(last_kernel, 1.0 / math.sqrt(nodes_total)),
        [((128, 256), BF, VMEM), ((16, 16, 256), F32, VMEM)],
        [SMEM] + [VMEM] * 5,
        [pltpu.VMEM((4, 32, 128), F32)],
    )(info, *folded, weight)
    weight_grad = exchange(grad, ("zh", "y")).reshape(256, 256)
    return (output, input_grad, weight_grad)


def solution(mesh):
    names = ("zl", "x", "zh", "y", "c")
    row, col = names[:2], names[2:]
    fine = Mesh(mesh.devices.reshape(4, 4, 2, 8, 2), names)
    return jax.shard_map(
        shards,
        mesh=fine,
        in_specs=(
            P(col + row, None),
            P(),
            P(row + col, None),
            P(row, col, None, None, None),
            P(row, col, None),
            P(row, col),
        ),
        out_specs=(P(row + col, None), P(col + row, None), P()),
        check_vma=False,
    )
```

time: 196 us -> 194 us (0.990)
  blocking collectives: 154 us -> 101 us
  starting transfers between devices: 8.73 us -> 47.2 us
  waiting for transfers between devices: 15.5 us -> 25.7 us
  Pallas kernels: 10.7 us -> 13.8 us
    all_to_all x6 -> x3, blocking collectives: 154 us -> 101 us  [exchange(): return lax.all_to_all(value, axes, 0, 0, tiled=True)]
    ppermute x0 -> x12, starting transfers between devices: none -> 43.4 us  [rotate(): return lax.ppermute(value, axis, [(i, (i + k) % 4) for i in range(4)])]
    ppermute x0 -> x12, waiting for transfers between devices: none -> 24.2 us  [rotate(): return lax.ppermute(value, axis, [(i, (i + k) % 4) for i in range(4)])]
    all_to_all x1 -> x0, waiting for transfers between devices: 10.1 us -> none  [exchange(): return lax.all_to_all(value, axes, 0, 0, tiled=True)]
    all_to_all x1 -> x0, starting transfers between devices: 4.9 us -> none  [exchange(): return lax.all_to_all(value, axes, 0, 0, tiled=True)]
    ppermute x2, waiting for transfers between devices: 5.44 us -> 1.53 us  [swap(): return lax.ppermute(value, 'c', [(0, 1), (1, 0)])]
    unnamed x7 -> x9, local copies, waits for them, and re-layouts: 0.72 us -> 3.26 us
    pallas_call x4 -> x7, Pallas kernels: 9.86 us -> 12.4 us  [the longest x2 3.19 us: shards(): call(functools.partial(forward_kernel, which), [((16, 128, 256), BF, VMEM...]
  transfers between devices with their start and end apart: 3 -> 14, of which waited for: 3 -> 10; matrix products, arithmetic and copies ran while one was open for 0% -> 0% of each run, Pallas kernels for 0% -> 3%
where the time goes in v2:
time: 194 us; the launch traced here: 193 us
  blocking collectives  101 us (52%)
  starting transfers between devices  47.2 us (24%)
  waiting for transfers between devices  25.7 us (13%)
  Pallas kernels  13.8 us (7%)
  local copies, waits for them, and re-layouts  3.26 us (2%)
    all_to_all x3, blocking collectives, exchange(): return lax.all_to_all(value, axes, 0, 0, tiled=True)  101 us
    ppermute x12, starting transfers between devices, rotate(): return lax.ppermute(value, axis, [(i, (i + k) % 4) for i in range(4)])  43.4 us
    ppermute x12, waiting for transfers between devices, rotate(): return lax.ppermute(value, axis, [(i, (i + k) % 4) for i in range(4)])  24.2 us
  transfers between devices with their start and end apart: 14, of which 10 were waited for; matrix products, arithmetic and copies ran while one was open for 0% of the time, Pallas kernels for 3%

profile of v2, /device:TPU:6, one launch (start us, length us, event | category | flops | bytes accessed | tf_op | source)
XLA Modules:
  0.0 193.3 jit_solution(781098634816180718)
XLA Ops:
  0.6 4.3 %collective-permute-start = (bf16[128,256]{1,0:T(8,128)(2,1)}, bf16[128,256]{1,0:T(8,128)(2,1)S(1)}, u32[]{:S(2)}, u32[]{:S(2)}) collective-permute-start(bf16[128,256]{1,0:T(8,128)(2,1)} %param.6), channel_id=1, source_target_pairs={{0,128},{128,256},{256,384},{384,0},{1,129},{129,257},{257,385},{3... | collective-permute-start | bytes 196616 | tf_op jit(solution)/shard_map/ppermute | solution.py:185
  4.9 5.5 %collective-permute-start.2 = (bf16[128,256]{1,0:T(8,128)(2,1)}, bf16[128,256]{1,0:T(8,128)(2,1)S(1)}, u32[]{:S(2)}, u32[]{:S(2)}) collective-permute-start(bf16[128,256]{1,0:T(8,128)(2,1)} %param.6), channel_id=1, source_target_pairs={{0,384},{128,0},{256,128},{384,256},{1,385},{129,1},{257,129},{385... | collective-permute-start | bytes 196616 | tf_op jit(solution)/shard_map/ppermute | solution.py:185
  10.5 2.5 %collective-permute-start.1 = (bf16[128,256]{1,0:T(8,128)(2,1)}, bf16[128,256]{1,0:T(8,128)(2,1)S(1)}, u32[]{:S(2)}, u32[]{:S(2)}) collective-permute-start(bf16[128,256]{1,0:T(8,128)(2,1)} %param.6), channel_id=1, source_target_pairs={{0,256},{128,384},{256,0},{384,128},{1,257},{129,385},{257,1},{385... | collective-permute-start | bytes 196616 | tf_op jit(solution)/shard_map/ppermute | solution.py:185
  12.9 0.0 collective-permute-done
  13.0 0.0 collective-permute-done.2
  13.0 4.8 %collective-permute-done.1 = bf16[128,256]{1,0:T(8,128)(2,1)S(1)} collective-permute-done((bf16[128,256]{1,0:T(8,128)(2,1)}, bf16[128,256]{1,0:T(8,128)(2,1)S(1)}, u32[]{:S(2)}, u32[]{:S(2)}) %collective-permute-start.1) | collective-permute-done | bytes 65568 | tf_op jit(solution)/shard_map/ppermute | solution.py:185
  17.7 0.9 pad_maximum_fusion.g0
  18.6 2.7 %collective-permute-start.5 = (bf16[4,128,256]{2,1,0:T(8,128)(2,1)S(1)}, bf16[4,128,256]{2,1,0:T(8,128)(2,1)S(1)}, u32[]{:S(2)}, u32[]{:S(2)}) collective-permute-start(bf16[4,128,256]{2,1,0:T(8,128)(2,1)S(1)} %pad_maximum_fusion.g0), channel_id=1, source_target_pairs={{0,96},{32,0},{64,32},{96,64},{1,97},{33,1},{65,33},{97,65},{2,98}... | collective-permute-start | bytes 786440 | tf_op jit(solution)/shard_map/ppermute | solution.py:185
  21.4 6.2 %collective-permute-start.4 = (bf16[4,128,256]{2,1,0:T(8,128)(2,1)S(1)}, bf16[4,128,256]{2,1,0:T(8,128)(2,1)S(1)}, u32[]{:S(2)}, u32[]{:S(2)}) collective-permute-start(bf16[4,128,256]{2,1,0:T(8,128)(2,1)S(1)} %pad_maximum_fusion.g0), channel_id=1, source_target_pairs={{0,64},{32,96},{64,0},{96,32},{1,65},{33,97},{65,1},{97,33},{2,66}... | collective-permute-start | bytes 786440 | tf_op jit(solution)/shard_map/ppermute | solution.py:185
  27.6 1.9 collective-permute-start.3
  30.2 0.1 pad_add_fusion.info
  30.2 0.7 copy-done.3
  30.9 2.0 %shard_map.85 = (s32[1120]{0:T(1024)S(1)}, s32[2]{0:T(128)S(1)}) custom-call(s32[96]{0:T(128)S(1)} %bitcast.16, s32[4]{0:T(128)S(1)} %pad_add_fusion.info), custom_call_target="tpu_custom_call" | custom-call | bytes 1048576 | tf_op jit(solution)/shard_map/pallas_call | solution.py:196
  32.9 0.0 collective-permute-done.5.g3
  32.9 1.8 collective-permute-done.4.g2
  34.6 2.5 %collective-permute-done.3.g1 = bf16[4,128,256]{2,1,0:T(8,128)(2,1)S(1)} collective-permute-done((bf16[4,128,256]{2,1,0:T(8,128)(2,1)S(1)}, bf16[4,128,256]{2,1,0:T(8,128)(2,1)S(1)}, u32[]{:S(2)}, u32[]{:S(2)}) %collective-permute-start.3) | collective-permute-done | bytes 262176 | tf_op jit(solution)/shard_map/ppermute | solution.py:185
  37.1 1.9 copy-done
  39.0 1.8 shard_map.87
  40.9 1.9 collective-permute-start.6
  42.8 1.4 shard_map.86
  44.2 0.0 copy-start.1
  44.2 0.0 copy-start.2
  44.2 1.2 collective-permute-done.6
  45.4 0.3 add_convert_fusion
  45.8 42.7 %all_to_all.15.parts = bf16[16,128,256]{2,1,0:T(8,128)(2,1)S(1)} all-to-all(bf16[16,128,256]{2,1,0:T(8,128)(2,1)S(1)} %add_convert_fusion), channel_id=1, replica_groups=mesh['zl'=4,'x'=4,'zh'=2,'y'=8,'c'=2] {'zh','y'}, dimensions={0} | all-to-all | bytes 2097152 | tf_op jit(solution)/shard_map/all_to_all | solution.py:177
  88.5 0.0 copy-done.1
  88.5 0.9 shard_map.88
  89.4 39.6 %all_to_all.16.own = bf16[16,288,128]{2,1,0:T(8,128)(2,1)S(1)} all-to-all(bf16[16,288,128]{2,1,0:T(8,128)(2,1)S(1)} %get-tuple-element.20), channel_id=1, replica_groups=mesh['zl'=4,'x'=4,'zh'=2,'y'=8,'c'=2] {'zh','y'}, dimensions={0} | all-to-all | bytes 2359296 | tf_op jit(solution)/shard_map/all_to_all | solution.py:177
  129.1 1.9 collective-permute-start.7
  131.0 2.5 %shard_map.89.begun = f32[17,256,128]{2,1,0:T(8,128)S(1)} custom-call(s32[1120]{0:T(1024)S(1)} %get-tuple-element.17.lists, s32[2]{0:T(128)S(1)} %get-tuple-element.18.groups, bf16[96,128,128]{2,1,0:T(8,128)(2,1)} %bitcast.12, bf16[16,288,128]{2,1,0:T(8,128)(2,1)S(1)} %all_to_all.16.own), custom_call_target="tpu_custom_call" | custom-call | flops 800000000 | bytes 6291456 | tf_op jit(solution)/shard_map/pallas_call | solution.py:224
  133.5 0.3 collective-permute-done.7.other
  133.8 3.1 %shard_map.90 = (bf16[1088,128]{1,0:T(8,128)(2,1)S(1)}, bf16[1088,128]{1,0:T(8,128)(2,1)S(1)}, bf16[1088,128]{1,0:T(8,128)(2,1)S(1)}, bf16[1088,128]{1,0:T(8,128)(2,1)S(1)}) custom-call(s32[1120]{0:T(1024)S(1)} %get-tuple-element.17.lists, s32[2]{0:T(128)S(1)} %get-tuple-element.18.groups, bf16[96,128,128]{2,1,0:T(8,128)(2,1)} %bitcast.13, ...), custom_call_target="tpu_custom_call" | custom-call | flops 800000000 | bytes 6291456 | tf_op jit(solution)/shard_map/pallas_call | solution.py:230
  136.9 4.1 %collective-permute-start.8 = (bf16[1088,128]{1,0:T(8,128)(2,1)S(1)}, bf16[1088,128]{1,0:T(8,128)(2,1)S(1)}, u32[]{:S(2)}, u32[]{:S(2)}) collective-permute-start(bf16[1088,128]{1,0:T(8,128)(2,1)S(1)} %get-tuple-element.22), channel_id=1, source_target_pairs={{0,32},{32,64},{64,96},{96,0},{1,33},{33,65},{65,97},{97,1},{2,34}... | collective-permute-start | bytes 835592 | tf_op jit(solution)/shard_map/ppermute | solution.py:185
  141.0 3.2 %collective-permute-start.9 = (bf16[1088,128]{1,0:T(8,128)(2,1)S(1)}, bf16[1088,128]{1,0:T(8,128)(2,1)S(1)}, u32[]{:S(2)}, u32[]{:S(2)}) collective-permute-start(bf16[1088,128]{1,0:T(8,128)(2,1)S(1)} %get-tuple-element.23), channel_id=1, source_target_pairs={{0,64},{32,96},{64,0},{96,32},{1,65},{33,97},{65,1},{97,33},{2,66}... | collective-permute-start | bytes 835592 | tf_op jit(solution)/shard_map/ppermute | solution.py:185
  144.2 3.3 %collective-permute-start.10 = (bf16[1088,128]{1,0:T(8,128)(2,1)S(1)}, bf16[1088,128]{1,0:T(8,128)(2,1)S(1)}, u32[]{:S(2)}, u32[]{:S(2)}) collective-permute-start(bf16[1088,128]{1,0:T(8,128)(2,1)S(1)} %get-tuple-element.24), channel_id=1, source_target_pairs={{0,96},{32,0},{64,32},{96,64},{1,97},{33,1},{65,33},{97,65},{2,98}... | collective-permute-start | bytes 835592 | tf_op jit(solution)/shard_map/ppermute | solution.py:185
  147.6 0.6 collective-permute-done.8.b1
  148.2 5.8 %collective-permute-done.9.b2 = bf16[1088,128]{1,0:T(8,128)(2,1)S(1)} collective-permute-done((bf16[1088,128]{1,0:T(8,128)(2,1)S(1)}, bf16[1088,128]{1,0:T(8,128)(2,1)S(1)}, u32[]{:S(2)}, u32[]{:S(2)}) %collective-permute-start.9) | collective-permute-done | bytes 278560 | tf_op jit(solution)/shard_map/ppermute | solution.py:185
  154.0 4.9 %collective-permute-done.10.b3 = bf16[1088,128]{1,0:T(8,128)(2,1)S(1)} collective-permute-done((bf16[1088,128]{1,0:T(8,128)(2,1)S(1)}, bf16[1088,128]{1,0:T(8,128)(2,1)S(1)}, u32[]{:S(2)}, u32[]{:S(2)}) %collective-permute-start.10) | collective-permute-done | bytes 278560 | tf_op jit(solution)/shard_map/ppermute | solution.py:185
  158.9 0.7 shard_map.91
  159.6 2.0 %collective-permute-start.11 = (bf16[320,128]{1,0:T(8,128)(2,1)S(1)}, bf16[320,128]{1,0:T(8,128)(2,1)S(1)}, u32[]{:S(2)}, u32[]{:S(2)}) collective-permute-start(bf16[320,128]{1,0:T(8,128)(2,1)S(1)} %get-tuple-element.26), channel_id=1, source_target_pairs={{0,128},{128,256},{256,384},{384,0},{1,129},{129,257},{257,385},{3... | collective-permute-start | bytes 245768 | tf_op jit(solution)/shard_map/ppermute | solution.py:185
  161.6 4.6 %collective-permute-start.12 = (bf16[320,128]{1,0:T(8,128)(2,1)S(1)}, bf16[320,128]{1,0:T(8,128)(2,1)S(1)}, u32[]{:S(2)}, u32[]{:S(2)}) collective-permute-start(bf16[320,128]{1,0:T(8,128)(2,1)S(1)} %get-tuple-element.27), channel_id=1, source_target_pairs={{0,256},{128,384},{256,0},{384,128},{1,257},{129,385},{257,1},{385... | collective-permute-start | bytes 245768 | tf_op jit(solution)/shard_map/ppermute | solution.py:185
  166.2 3.0 %collective-permute-start.13 = (bf16[320,128]{1,0:T(8,128)(2,1)S(1)}, bf16[320,128]{1,0:T(8,128)(2,1)S(1)}, u32[]{:S(2)}, u32[]{:S(2)}) collective-permute-start(bf16[320,128]{1,0:T(8,128)(2,1)S(1)} %get-tuple-element.28), channel_id=1, source_target_pairs={{0,384},{128,0},{256,128},{384,256},{1,385},{129,1},{257,129},{385... | collective-permute-start | bytes 245768 | tf_op jit(solution)/shard_map/ppermute | solution.py:185
  169.2 0.0 collective-permute-done.11.f1
  169.2 2.2 %collective-permute-done.12.f2 = bf16[320,128]{1,0:T(8,128)(2,1)S(1)} collective-permute-done((bf16[320,128]{1,0:T(8,128)(2,1)S(1)}, bf16[320,128]{1,0:T(8,128)(2,1)S(1)}, u32[]{:S(2)}, u32[]{:S(2)}) %collective-permute-start.12) | collective-permute-done | bytes 81952 | tf_op jit(solution)/shard_map/ppermute | solution.py:185
  171.3 1.7 collective-permute-done.13.f3
  173.0 1.4 shard_map.92
  174.4 18.2 %all_to_all.17 = f32[16,16,256]{2,1,0:T(8,128)S(1)} all-to-all(f32[16,16,256]{2,1,0:T(8,128)S(1)} %get-tuple-element.30), channel_id=1, replica_groups=mesh['zl'=4,'x'=4,'zh'=2,'y'=8,'c'=2] {'zh','y'}, dimensions={0} | all-to-all | bytes 524288 | tf_op jit(solution)/shard_map/all_to_all | solution.py:177
  192.6 0.7 copy.11
  (3 shorter events, 0.0 us)
Async XLA Ops:
  0.6 12.3 %collective-permute-start = (bf16[128,256]{1,0:T(8,128)(2,1)}, bf16[128,256]{1,0:T(8,128)(2,1)S(1)}, u32[]{:S(2)}, u32[]{:S(2)}) collective-permute-start(bf16[128,256]{1,0:T(8,128)(2,1)} %param.6), channel_id=1, source_target_pairs={{0,128},{128,256},{256,384},{384,0},{1,129},{129,257},{257,385},{3... | collective-permute-start | bytes 196616 | tf_op jit(solution)/shard_map/ppermute | solution.py:185
  4.9 8.0 %collective-permute-start.2 = (bf16[128,256]{1,0:T(8,128)(2,1)}, bf16[128,256]{1,0:T(8,128)(2,1)S(1)}, u32[]{:S(2)}, u32[]{:S(2)}) collective-permute-start(bf16[128,256]{1,0:T(8,128)(2,1)} %param.6), channel_id=1, source_target_pairs={{0,384},{128,0},{256,128},{384,256},{1,385},{129,1},{257,129},{385... | collective-permute-start | bytes 196616 | tf_op jit(solution)/shard_map/ppermute | solution.py:185
  10.5 7.3 %collective-permute-start.1 = (bf16[128,256]{1,0:T(8,128)(2,1)}, bf16[128,256]{1,0:T(8,128)(2,1)S(1)}, u32[]{:S(2)}, u32[]{:S(2)}) collective-permute-start(bf16[128,256]{1,0:T(8,128)(2,1)} %param.6), channel_id=1, source_target_pairs={{0,256},{128,384},{256,0},{384,128},{1,257},{129,385},{257,1},{385... | collective-permute-start | bytes 196616 | tf_op jit(solution)/shard_map/ppermute | solution.py:185
  18.6 14.3 %collective-permute-start.5 = (bf16[4,128,256]{2,1,0:T(8,128)(2,1)S(1)}, bf16[4,128,256]{2,1,0:T(8,128)(2,1)S(1)}, u32[]{:S(2)}, u32[]{:S(2)}) collective-permute-start(bf16[4,128,256]{2,1,0:T(8,128)(2,1)S(1)} %pad_maximum_fusion.g0), channel_id=1, source_target_pairs={{0,96},{32,0},{64,32},{96,64},{1,97},{33,1},{65,33},{97,65},{2,98}... | collective-permute-start | bytes 786440 | tf_op jit(solution)/shard_map/ppermute | solution.py:185
  21.4 13.3 %collective-permute-start.4 = (bf16[4,128,256]{2,1,0:T(8,128)(2,1)S(1)}, bf16[4,128,256]{2,1,0:T(8,128)(2,1)S(1)}, u32[]{:S(2)}, u32[]{:S(2)}) collective-permute-start(bf16[4,128,256]{2,1,0:T(8,128)(2,1)S(1)} %pad_maximum_fusion.g0), channel_id=1, source_target_pairs={{0,64},{32,96},{64,0},{96,32},{1,65},{33,97},{65,1},{97,33},{2,66}... | collective-permute-start | bytes 786440 | tf_op jit(solution)/shard_map/ppermute | solution.py:185
  27.6 9.6 %collective-permute-start.3 = (bf16[4,128,256]{2,1,0:T(8,128)(2,1)S(1)}, bf16[4,128,256]{2,1,0:T(8,128)(2,1)S(1)}, u32[]{:S(2)}, u32[]{:S(2)}) collective-permute-start(bf16[4,128,256]{2,1,0:T(8,128)(2,1)S(1)} %pad_maximum_fusion.g0), channel_id=1, source_target_pairs={{0,32},{32,64},{64,96},{96,0},{1,33},{33,65},{65,97},{97,1},{2,34}... | collective-permute-start | bytes 786440 | tf_op jit(solution)/shard_map/ppermute | solution.py:185
  30.2 0.7 copy-start.3
  37.1 1.9 copy-start
  40.9 4.6 %collective-permute-start.6 = (bf16[16,128,256]{2,1,0:T(8,128)(2,1)S(1)}, bf16[16,128,256]{2,1,0:T(8,128)(2,1)S(1)}, u32[]{:S(2)}, u32[]{:S(2)}) collective-permute-start(bf16[16,128,256]{2,1,0:T(8,128)(2,1)S(1)} %shard_map.87), channel_id=1, source_target_pairs={{0,1},{1,0},{2,3},{3,2},{4,5},{5,4},{6,7},{7,6},{8,9},{9,8},{10,11... | collective-permute-start | bytes 3145736 | tf_op jit(solution)/shard_map/ppermute | solution.py:181
  44.2 44.3 %copy-start.1 = (bf16[256,256]{1,0:T(8,128)(2,1)S(1)}, bf16[256,256]{1,0:T(8,128)(2,1)}, u32[]{:S(2)}) copy-start(bf16[256,256]{1,0:T(8,128)(2,1)} %weight.3) | copy-start | bytes 393220
  44.2 44.3 %copy-start.2 = (bf16[128,256]{1,0:T(8,128)(2,1)S(1)}, bf16[128,256]{1,0:T(8,128)(2,1)}, u32[]{:S(2)}) copy-start(bf16[128,256]{1,0:T(8,128)(2,1)} %cotangent.1) | copy-start | bytes 196612
  129.1 4.7 %collective-permute-start.7 = (bf16[16,288,128]{2,1,0:T(8,128)(2,1)S(1)}, bf16[16,288,128]{2,1,0:T(8,128)(2,1)S(1)}, u32[]{:S(2)}, u32[]{:S(2)}) collective-permute-start(bf16[16,288,128]{2,1,0:T(8,128)(2,1)S(1)} %all_to_all.16.own), channel_id=1, source_target_pairs={{0,1},{1,0},{2,3},{3,2},{4,5},{5,4},{6,7},{7,6},{8,9},{9,8},{10,11... | collective-permute-start | bytes 3538952 | tf_op jit(solution)/shard_map/ppermute | solution.py:181
  136.9 11.3 %collective-permute-start.8 = (bf16[1088,128]{1,0:T(8,128)(2,1)S(1)}, bf16[1088,128]{1,0:T(8,128)(2,1)S(1)}, u32[]{:S(2)}, u32[]{:S(2)}) collective-permute-start(bf16[1088,128]{1,0:T(8,128)(2,1)S(1)} %get-tuple-element.22), channel_id=1, source_target_pairs={{0,32},{32,64},{64,96},{96,0},{1,33},{33,65},{65,97},{97,1},{2,34}... | collective-permute-start | bytes 835592 | tf_op jit(solution)/shard_map/ppermute | solution.py:185
  141.0 13.0 %collective-permute-start.9 = (bf16[1088,128]{1,0:T(8,128)(2,1)S(1)}, bf16[1088,128]{1,0:T(8,128)(2,1)S(1)}, u32[]{:S(2)}, u32[]{:S(2)}) collective-permute-start(bf16[1088,128]{1,0:T(8,128)(2,1)S(1)} %get-tuple-element.23), channel_id=1, source_target_pairs={{0,64},{32,96},{64,0},{96,32},{1,65},{33,97},{65,1},{97,33},{2,66}... | collective-permute-start | bytes 835592 | tf_op jit(solution)/shard_map/ppermute | solution.py:185
  144.2 14.6 %collective-permute-start.10 = (bf16[1088,128]{1,0:T(8,128)(2,1)S(1)}, bf16[1088,128]{1,0:T(8,128)(2,1)S(1)}, u32[]{:S(2)}, u32[]{:S(2)}) collective-permute-start(bf16[1088,128]{1,0:T(8,128)(2,1)S(1)} %get-tuple-element.24), channel_id=1, source_target_pairs={{0,96},{32,0},{64,32},{96,64},{1,97},{33,1},{65,33},{97,65},{2,98}... | collective-permute-start | bytes 835592 | tf_op jit(solution)/shard_map/ppermute | solution.py:185
  159.6 9.6 %collective-permute-start.11 = (bf16[320,128]{1,0:T(8,128)(2,1)S(1)}, bf16[320,128]{1,0:T(8,128)(2,1)S(1)}, u32[]{:S(2)}, u32[]{:S(2)}) collective-permute-start(bf16[320,128]{1,0:T(8,128)(2,1)S(1)} %get-tuple-element.26), channel_id=1, source_target_pairs={{0,128},{128,256},{256,384},{384,0},{1,129},{129,257},{257,385},{3... | collective-permute-start | bytes 245768 | tf_op jit(solution)/shard_map/ppermute | solution.py:185
  161.6 9.8 %collective-permute-start.12 = (bf16[320,128]{1,0:T(8,128)(2,1)S(1)}, bf16[320,128]{1,0:T(8,128)(2,1)S(1)}, u32[]{:S(2)}, u32[]{:S(2)}) collective-permute-start(bf16[320,128]{1,0:T(8,128)(2,1)S(1)} %get-tuple-element.27), channel_id=1, source_target_pairs={{0,256},{128,384},{256,0},{384,128},{1,257},{129,385},{257,1},{385... | collective-permute-start | bytes 245768 | tf_op jit(solution)/shard_map/ppermute | solution.py:185
  166.2 6.8 %collective-permute-start.13 = (bf16[320,128]{1,0:T(8,128)(2,1)S(1)}, bf16[320,128]{1,0:T(8,128)(2,1)S(1)}, u32[]{:S(2)}, u32[]{:S(2)}) collective-permute-start(bf16[320,128]{1,0:T(8,128)(2,1)S(1)} %get-tuple-element.28), channel_id=1, source_target_pairs={{0,384},{128,0},{256,128},{384,256},{1,385},{129,1},{257,129},{385... | collective-permute-start | bytes 245768 | tf_op jit(solution)/shard_map/ppermute | solution.py:185

commit v3 on v2

v3 whole, which is shorter than its diff:
```python
import functools
import math

import jax
import jax.numpy as jnp
from jax import lax
from jax.experimental import pallas as pl
from jax.experimental.pallas import tpu as pltpu
from jax.sharding import Mesh
from jax.sharding import PartitionSpec as P

BF = jnp.bfloat16
F32 = jnp.float32
GROUP = 16
SLOTS = 112
VMEM = pl.BlockSpec(memory_space=pltpu.VMEM)
SMEM = pl.BlockSpec(memory_space=pltpu.SMEM)
LIMIT = pltpu.CompilerParams(vmem_limit_bytes=20 * 1024 * 1024)


def dot(a, b, dims=(((1,), (0,)), ((), ()))):
    return lax.dot_general(a, b, dims, preferred_element_type=F32)


def plan_kernel(place, info, blocks, lists, groups):
    count, core, xi, zi = info[0], info[1], info[2], info[3]

    def write(at, k, t, source, half, target):
        for f, value in enumerate((k, t, source, half, target)):
            lists[f * 2 * SLOTS + at] = value

    def step(k, held):
        p = place[k]
        t, a = p >> 4, p & 15
        z, x = a >> 2, a & 3
        half = t >> 1
        source = (((xi - x) & 3) << 2) + ((zi - z) & 3)
        target = (((x - xi) & 3) << 2) + ((z - zi) & 3)
        mine, theirs = held
        away = (t & 1) ^ core
        write(jnp.where(away == 0, mine, SLOTS + theirs), k, half, source, half, target)
        return mine + 1 - away, theirs + away

    mine, theirs = lax.fori_loop(0, count, step, (jnp.int32(0), jnp.int32(0)))
    for i, n in enumerate((mine, theirs)):
        for g in range(GROUP):
            write(i * SLOTS + n + g, 0, 16, 0, 0, 16)
        groups[i] = (n + GROUP - 1) // GROUP


def entry(lists, which, field, j):
    return lists[field * 2 * SLOTS + which * SLOTS + j]


def products_into(acc, lists, groups, which, target, product):
    def step(i, _):
        products = []
        for g in range(GROUP):
            j = i * GROUP + g
            products.append((entry(lists, which, target, j), product(j)))
        for slot, value in products:
            acc[slot] += value
        return 0

    lax.fori_loop(0, groups[which], step, 0)


def line_kernel(f0, f1, f2, f3, line0, line1):
    for k, part in enumerate((f0, f1, f2, f3)):
        line0[k] = part[:, 0:128]
        line1[k] = part[:, 128:256]


def forward_products(which, lists, groups, blocks, parts, out, nodes, acc):
    for i, part in enumerate(parts):
        nodes[4 * i : 4 * i + 4] = part[...]
    acc[...] = jnp.zeros_like(acc)

    def product(j):
        return dot(blocks[entry(lists, which, 0, j)], nodes[entry(lists, which, 2, j)])

    products_into(acc, lists, groups, which, 1, product)
    out[...] = acc[0:16].astype(BF)


def forward_kernel(which, lists, groups, blocks, g0, g1, g2, g3, out, nodes, acc):
    forward_products(which, lists, groups, blocks, (g0, g1, g2, g3), out, nodes, acc)


def forward_gate_kernel(which, lists, groups, blocks, g0, g1, g2, g3, later, out, now, nodes, acc):
    now[...] = later[...]
    forward_products(which, lists, groups, blocks, (g0, g1, g2, g3), out, nodes, acc)


def middle_kernel(parts0, parts1, weight, cotangent, output, spread0, spread1):
    shares = []
    for parts in (parts0, parts1):
        total = parts[0].astype(F32)
        for s in range(1, 16):
            total += parts[s].astype(F32)
        shares.append(total.astype(BF))
    share = jnp.concatenate(shares, axis=1)
    pre = dot(share, weight[...])
    sigma = 1.0 / (1.0 + jnp.exp(-pre))
    output[...] = (pre * sigma).astype(BF)
    slope = sigma * (1.0 + pre * (1.0 - sigma))
    slopes = (cotangent[...].astype(F32) * slope).astype(BF)
    turned = slopes.astype(F32).T.astype(BF)
    grad = dot(share.astype(F32).T.astype(BF), slopes).astype(BF)
    for s in range(16):
        spread0[s, 0:128, :] = turned[0:128]
        spread0[s, 128:144, :] = grad[16 * s : 16 * s + 16, 0:128]
        spread0[s, 144:160, :] = grad[16 * s : 16 * s + 16, 128:256]
        spread1[s] = turned[128:256]


def split(value):
    high = value.astype(BF)
    return high, (value - high.astype(F32)).astype(BF)


def back_products(which, lists, groups, blocks, source, acc):
    def product(j):
        return dot(source[entry(lists, which, 3, j), 0:128, :], blocks[entry(lists, which, 0, j)])

    products_into(acc, lists, groups, which, 4, product)


def backward_own_kernel(lists, groups, blocks, own, acc):
    acc[...] = jnp.zeros_like(acc)
    back_products(0, lists, groups, blocks, own, acc)


def backward_other_kernel(lists, groups, blocks, own, other, begun, b0, b1, b2, b3, acc):
    acc[...] = begun[...]
    back_products(1, lists, groups, blocks, other, acc)
    for x, out in enumerate((b0, b1, b2, b3)):
        for z in range(4):
            out[128 * z : 128 * z + 128, :] = acc[4 * x + z].astype(BF)
    if own.shape[1] > 128:
        grad = jnp.zeros((32, 128), F32)
        for s in range(16):
            grad += own[s, 128:160, :].astype(F32) + other[s, 128:160, :].astype(F32)
        high, low = split(grad)
        for out in (b0, b1, b2, b3):
            out[512:544, :] = high
            out[544:576, :] = low


def ordered_sum(me, parts, row, scratch):
    for k, part in enumerate(parts):
        high, low = part[row : row + 32, :], part[row + 32 : row + 64, :]
        scratch[(me - k) & 3] = high.astype(F32) + low.astype(F32)
    return scratch[0] + scratch[1] + scratch[2] + scratch[3]


def fold_kernel(info, b0, b1, b2, b3, f0, f1, f2, f3, scratch):
    parts, outs = (b0, b1, b2, b3), (f0, f1, f2, f3)
    for z, out in enumerate(outs):
        rows = slice(128 * z, 128 * z + 128)
        total = parts[0][rows, :].astype(F32)
        for part in parts[1:]:
            total += part[rows, :].astype(F32)
        out[0:128, :] = total.astype(BF)
    if b0.shape[0] > 512:
        high, low = split(ordered_sum(info[2], parts, 512, scratch))
        for out in outs:
            out[128:160, :] = high
            out[160:192, :] = low


def fold_gate_kernel(info, b0, b1, b2, b3, later, f0, f1, f2, f3, now, scratch):
    now[...] = later[...]
    fold_kernel(info, b0, b1, b2, b3, f0, f1, f2, f3, scratch)


def grad_kernel(scale, info, f0, f1, f2, f3, grad_out, scratch):
    grad = ordered_sum(info[3], (f0, f1, f2, f3), 128, scratch) * scale
    for s in range(16):
        grad_out[s, :, 0:128] = grad[0:16]
        grad_out[s, :, 128:256] = grad[16:32]


def last_kernel(f0, f1, f2, f3, h0, h1, h2, h3, weight, input_grad):
    backs = []
    for parts in ((f0, f1, f2, f3), (h0, h1, h2, h3)):
        total = parts[0][0:128, :].astype(F32)
        for part in parts[1:]:
            total += part[0:128, :].astype(F32)
        backs.append(total.astype(BF).astype(F32).T.astype(BF))
    back = jnp.concatenate(backs, axis=1)
    input_grad[...] = dot(back, weight[...], (((1,), (1,)), ((), ()))).astype(BF)


def call(kernel, outs, kinds, scratch=(), flops=0, size=0):
    return pl.pallas_call(
        kernel,
        out_shape=[jax.ShapeDtypeStruct(s, d) for s, d, _ in outs],
        in_specs=kinds,
        out_specs=[k for _, _, k in outs],
        scratch_shapes=list(scratch),
        compiler_params=LIMIT,
        cost_estimate=pl.CostEstimate(flops=flops, bytes_accessed=size, transcendentals=0),
    )


def exchange(value, axes):
    return lax.all_to_all(value, axes, 0, 0, tiled=True)


def swap(value):
    return lax.ppermute(value, "c", [(0, 1), (1, 0)])


def rotate(value, axis, k):
    return lax.ppermute(value, axis, [(i, (i + k) % 4) for i in range(4)])


def shards(features, weight, cotangent, blocks, block_pos, counts):
    tile = blocks[0, 0]
    index = [lax.axis_index(a).astype(jnp.int32) for a in ("c", "x", "zl")]
    info = jnp.stack([counts[0, 0]] + index)
    nodes_total = 65536
    heavy = dict(flops=4 * 10**8, size=4 * 2**20)
    i32 = jnp.int32
    rounds = (1, 2, 3)

    lists, groups = call(
        plan_kernel,
        [((10 * SLOTS,), i32, SMEM), ((2,), i32, SMEM)],
        [SMEM, SMEM, VMEM],
        size=2**20,
    )(block_pos[0, 0], info, tile)

    line = [features] + [rotate(features, "zl", k) for k in rounds]
    line0, line1 = call(line_kernel, [((4, 128, 128), BF, VMEM)] * 2, [VMEM] * 4)(*line)
    kept = ((16, 128, 128), BF, VMEM)
    scratch = [pltpu.VMEM((16, 128, 128), BF), pltpu.VMEM((17, 128, 128), F32)]
    kinds = [SMEM, SMEM] + [VMEM] * 5

    def forward(which, plane):
        body = functools.partial(forward_kernel, which)
        return call(body, [kept], kinds, scratch, **heavy)(lists, groups, tile, *plane)[0]

    plane = [line0] + [rotate(line0, "x", k) for k in rounds]
    send, line1 = call(
        functools.partial(forward_gate_kernel, 1),
        [kept, ((4, 128, 128), BF, VMEM)],
        kinds + [VMEM],
        scratch,
        **heavy,
    )(lists, groups, tile, *plane, line1)
    plane1 = [line1] + [rotate(line1, "x", k) for k in rounds]
    sent = swap(send)
    pair = (forward(0, plane).astype(F32) + sent.astype(F32)).astype(BF)
    parts0 = exchange(pair, ("zh", "y"))
    sent = swap(forward(1, plane1))
    pair = (forward(0, plane1).astype(F32) + sent.astype(F32)).astype(BF)
    parts1 = exchange(pair, ("zh", "y"))
    output, spread0, spread1 = call(
        middle_kernel,
        [((128, 256), BF, VMEM), ((16, 160, 128), BF, VMEM), ((16, 128, 128), BF, VMEM)],
        [VMEM] * 4,
    )(parts0, parts1, weight, cotangent)

    def backward(own):
        other = swap(own)
        (begun,) = call(
            backward_own_kernel,
            [((17, 128, 128), F32, VMEM)],
            [SMEM, SMEM, VMEM, VMEM],
            **heavy,
        )(lists, groups, tile, own)
        rows = 512 + (64 if own.shape[1] > 128 else 0)
        back = call(
            backward_other_kernel,
            [((rows, 128), BF, VMEM)] * 4,
            [SMEM, SMEM] + [VMEM] * 4,
            [pltpu.VMEM((17, 128, 128), F32)],
            **heavy,
        )(lists, groups, tile, own, other, begun)
        return [back[0]] + [rotate(back[k], "x", k) for k in rounds]

    small = [pltpu.VMEM((4, 32, 128), F32)]
    own0 = exchange(spread0, ("zh", "y"))
    own1 = exchange(spread1, ("zh", "y"))
    *fold0, own1 = call(
        fold_gate_kernel,
        [((192, 128), BF, VMEM)] * 4 + [((16, 128, 128), BF, VMEM)],
        [SMEM] + [VMEM] * 5,
        small,
    )(info, *backward(own0), own1)
    fold0[1:] = [rotate(fold0[k], "zl", k) for k in rounds]
    fold1 = call(fold_kernel, [((128, 128), BF, VMEM)] * 4, [SMEM] + [VMEM] * 4, small)(info, *backward(own1))
    fold1 = [fold1[0]] + [rotate(fold1[k], "zl", k) for k in rounds]
    folds = (fold0, fold1)
    (grad,) = call(
        functools.partial(grad_kernel, 1.0 / math.sqrt(nodes_total)),
        [((16, 16, 256), F32, VMEM)],
        [SMEM] + [VMEM] * 4,
        [pltpu.VMEM((4, 32, 128), F32)],
    )(info, *folds[0])
    weight_grad = exchange(grad, ("zh", "y")).reshape(256, 256)
    (input_grad,) = call(
        last_kernel,
        [((128, 256), BF, VMEM)],
        [VMEM] * 9,
    )(*folds[0], *folds[1], weight)
    return (output, input_grad, weight_grad)


def solution(mesh):
    names = ("zl", "x", "zh", "y", "c")
    row, col = names[:2], names[2:]
    fine = Mesh(mesh.devices.reshape(4, 4, 2, 8, 2), names)
    return jax.shard_map(
        shards,
        mesh=fine,
        in_specs=(
            P(col + row, None),
            P(),
            P(row + col, None),
            P(row, col, None, None, None),
            P(row, col, None),
            P(row, col),
        ),
        out_specs=(P(row + col, None), P(col + row, None), P()),
        check_vma=False,
    )
```

time: 194 us -> 234 us (1.21); the launches traced: 193 us -> 230 us
  starting transfers between devices: 47.2 us -> 111 us
  blocking collectives: 101 us -> 60.4 us
  Pallas kernels: 13.8 us -> 20.9 us
  local copies, waits for them, and re-layouts: 3.26 us -> 7.72 us
    all_to_all x3 -> x2, blocking collectives: 101 us -> 60.4 us  [exchange(): return lax.all_to_all(value, axes, 0, 0, tiled=True)]
    ppermute x12 -> x21, starting transfers between devices: 43.4 us -> 73.8 us  [rotate(): return lax.ppermute(value, axis, [(i, (i + k) % 4) for i in range(4)])]
    all_to_all x0 -> x3, starting transfers between devices: none -> 29.5 us  [exchange(): return lax.all_to_all(value, axes, 0, 0, tiled=True)]
    pallas_call x7 -> x14, Pallas kernels: 11.8 us -> 19 us  [the longest x3 4.17 us: forward(): call(body, [kept], kinds, scratch, **heavy)(lists, groups, tile, *plane)[0]]
    unnamed x9 -> x27, local copies, waits for them, and re-layouts: 3.26 us -> 7.72 us
    ppermute x2 -> x4, starting transfers between devices: 3.83 us -> 7.71 us  [swap(): return lax.ppermute(value, 'c', [(0, 1), (1, 0)])]
    ppermute x12 -> x21, waiting for transfers between devices: 24.2 us -> 24.3 us  [rotate(): return lax.ppermute(value, axis, [(i, (i + k) % 4) for i in range(4)])]
  transfers between devices with their start and end apart: 14 -> 28, of which waited for: 10 -> 15; matrix products, arithmetic and copies ran while one was open for 0% -> 0% of each run, Pallas kernels for 3% -> 6%
where the time goes in v3:
time: 234 us; the launch traced here: 230 us
  starting transfers between devices  111 us (47%)
  blocking collectives  60.4 us (26%)
  waiting for transfers between devices  26.5 us (11%)
  Pallas kernels  20.9 us (9%)
  local copies, waits for them, and re-layouts  7.72 us (3%)
    ppermute x21, starting transfers between devices, rotate(): return lax.ppermute(value, axis, [(i, (i + k) % 4) for i in range(4)])  73.8 us
    all_to_all x2, blocking collectives, exchange(): return lax.all_to_all(value, axes, 0, 0, tiled=True)  60.4 us
    all_to_all x3, starting transfers between devices, exchange(): return lax.all_to_all(value, axes, 0, 0, tiled=True)  29.5 us
    ppermute x21, waiting for transfers between devices, rotate(): return lax.ppermute(value, axis, [(i, (i + k) % 4) for i in range(4)])  24.3 us
    unnamed x27, local copies, waits for them, and re-layouts  7.72 us
    ppermute x4, starting transfers between devices, swap(): return lax.ppermute(value, 'c', [(0, 1), (1, 0)])  7.71 us
  transfers between devices with their start and end apart: 28, of which 15 were waited for; matrix products, arithmetic and copies ran while one was open for 0% of the time, Pallas kernels for 6%

profile of v3, /device:TPU:6, one launch (start us, length us, event | category | flops | bytes accessed | tf_op | source)
XLA Modules:
  0.0 230.2 jit_solution(3065674663849659979)
XLA Ops:
  0.6 6.1 %collective-permute-start.1 = (bf16[128,256]{1,0:T(8,128)(2,1)}, bf16[128,256]{1,0:T(8,128)(2,1)S(1)}, u32[]{:S(2)}, u32[]{:S(2)}) collective-permute-start(bf16[128,256]{1,0:T(8,128)(2,1)} %f0.1), channel_id=1, source_target_pairs={{0,256},{128,384},{256,0},{384,128},{1,257},{129,385},{257,1},{385... | collective-permute-start | bytes 196616 | tf_op jit(solution)/shard_map/ppermute | solution.py:216
  6.7 4.3 %collective-permute-start = (bf16[128,256]{1,0:T(8,128)(2,1)}, bf16[128,256]{1,0:T(8,128)(2,1)S(1)}, u32[]{:S(2)}, u32[]{:S(2)}) collective-permute-start(bf16[128,256]{1,0:T(8,128)(2,1)} %f0.1), channel_id=1, source_target_pairs={{0,128},{128,256},{256,384},{384,0},{1,129},{129,257},{257,385},{3... | collective-permute-start | bytes 196616 | tf_op jit(solution)/shard_map/ppermute | solution.py:216
  11.0 3.4 %collective-permute-start.2 = (bf16[128,256]{1,0:T(8,128)(2,1)}, bf16[128,256]{1,0:T(8,128)(2,1)S(1)}, u32[]{:S(2)}, u32[]{:S(2)}) collective-permute-start(bf16[128,256]{1,0:T(8,128)(2,1)} %f0.1), channel_id=1, source_target_pairs={{0,384},{128,0},{256,128},{384,256},{1,385},{129,1},{257,129},{385... | collective-permute-start | bytes 196616 | tf_op jit(solution)/shard_map/ppermute | solution.py:216
  15.1 2.2 collective-permute-done.2.f3
  18.9 2.7 %collective-permute-start.5 = (bf16[4,128,128]{2,1,0:T(8,128)(2,1)S(1)}, bf16[4,128,128]{2,1,0:T(8,128)(2,1)S(1)}, u32[]{:S(2)}, u32[]{:S(2)}) collective-permute-start(bf16[4,128,128]{2,1,0:T(8,128)(2,1)S(1)} %get-tuple-element.31.g0), channel_id=1, source_target_pairs={{0,96},{32,0},{64,32},{96,64},{1,97},{33,1},{65,33},{97,65},{2,98}... | collective-permute-start | bytes 393224 | tf_op jit(solution)/shard_map/ppermute | solution.py:216
  21.7 3.4 %collective-permute-start.4 = (bf16[4,128,128]{2,1,0:T(8,128)(2,1)S(1)}, bf16[4,128,128]{2,1,0:T(8,128)(2,1)S(1)}, u32[]{:S(2)}, u32[]{:S(2)}) collective-permute-start(bf16[4,128,128]{2,1,0:T(8,128)(2,1)S(1)} %get-tuple-element.31.g0), channel_id=1, source_target_pairs={{0,64},{32,96},{64,0},{96,32},{1,65},{33,97},{65,1},{97,33},{2,66}... | collective-permute-start | bytes 393224 | tf_op jit(solution)/shard_map/ppermute | solution.py:216
  25.1 3.6 %collective-permute-start.3 = (bf16[4,128,128]{2,1,0:T(8,128)(2,1)S(1)}, bf16[4,128,128]{2,1,0:T(8,128)(2,1)}, u32[]{:S(2)}, u32[]{:S(2)}) collective-permute-start(bf16[4,128,128]{2,1,0:T(8,128)(2,1)S(1)} %get-tuple-element.31.g0), channel_id=1, source_target_pairs={{0,32},{32,64},{64,96},{96,0},{1,33},{33,65},{65,97},{97,1},{2,34}... | collective-permute-start | bytes 393224 | tf_op jit(solution)/shard_map/ppermute | solution.py:216
  29.4 1.9 copy-done
  32.0 1.9 shard_map.85
  36.2 1.9 collective-permute-start.6
  38.2 1.7 shard_map.87
  41.0 13.1 %all-to-all-start = ((bf16[16,128,128]{2,1,0:T(8,128)(2,1)}), bf16[16,128,128]{2,1,0:T(8,128)(2,1)}, u32[]{:S(2)}, u32[]{:S(2)}) async-start(bf16[16,128,128]{2,1,0:T(8,128)(2,1)} %add_convert_fusion.1), calls=%async_computation | async-start | bytes 1048576 | tf_op jit(solution)/shard_map/all_to_all | solution.py:208
  54.1 2.4 %collective-permute-start.9 = (bf16[4,128,128]{2,1,0:T(8,128)(2,1)S(1)}, bf16[4,128,128]{2,1,0:T(8,128)(2,1)S(1)}, u32[]{:S(2)}, u32[]{:S(2)}) collective-permute-start(bf16[4,128,128]{2,1,0:T(8,128)(2,1)S(1)} %copy-done.5), channel_id=1, source_target_pairs={{0,96},{32,0},{64,32},{96,64},{1,97},{33,1},{65,33},{97,65},{2,98}... | collective-permute-start | bytes 393224 | tf_op jit(solution)/shard_map/ppermute | solution.py:216
  56.5 5.4 %collective-permute-start.8 = (bf16[4,128,128]{2,1,0:T(8,128)(2,1)S(1)}, bf16[4,128,128]{2,1,0:T(8,128)(2,1)S(1)}, u32[]{:S(2)}, u32[]{:S(2)}) collective-permute-start(bf16[4,128,128]{2,1,0:T(8,128)(2,1)S(1)} %copy-done.5), channel_id=1, source_target_pairs={{0,64},{32,96},{64,0},{96,32},{1,65},{33,97},{65,1},{97,33},{2,66}... | collective-permute-start | bytes 393224 | tf_op jit(solution)/shard_map/ppermute | solution.py:216
  61.9 4.5 %collective-permute-start.7 = (bf16[4,128,128]{2,1,0:T(8,128)(2,1)S(1)}, bf16[4,128,128]{2,1,0:T(8,128)(2,1)S(1)}, u32[]{:S(2)}, u32[]{:S(2)}) collective-permute-start(bf16[4,128,128]{2,1,0:T(8,128)(2,1)S(1)} %copy-done.5), channel_id=1, source_target_pairs={{0,32},{32,64},{64,96},{96,0},{1,33},{33,65},{65,97},{97,1},{2,34}... | collective-permute-start | bytes 393224 | tf_op jit(solution)/shard_map/ppermute | solution.py:216
  66.5 2.5 %collective-permute-done.7.g1 = bf16[4,128,128]{2,1,0:T(8,128)(2,1)S(1)} collective-permute-done((bf16[4,128,128]{2,1,0:T(8,128)(2,1)S(1)}, bf16[4,128,128]{2,1,0:T(8,128)(2,1)S(1)}, u32[]{:S(2)}, u32[]{:S(2)}) %collective-permute-start.7) | collective-permute-done | bytes 131104 | tf_op jit(solution)/shard_map/ppermute | solution.py:216
  70.1 1.9 collective-permute-start.10
  74.8 31.8 %all_to_all.25.parts1 = bf16[16,128,128]{2,1,0:T(8,128)(2,1)S(1)} all-to-all(bf16[16,128,128]{2,1,0:T(8,128)(2,1)} %add_convert_fusion), channel_id=1, replica_groups=mesh['zl'=4,'x'=4,'zh'=2,'y'=8,'c'=2] {'zh','y'}, dimensions={0} | all-to-all | bytes 1048576 | tf_op jit(solution)/shard_map/all_to_all | solution.py:208
  106.7 1.9 shard_map.91
  108.6 28.6 %all_to_all.26.own = bf16[16,160,128]{2,1,0:T(8,128)(2,1)} all-to-all(bf16[16,160,128]{2,1,0:T(8,128)(2,1)S(1)} %get-tuple-element.36), channel_id=1, replica_groups=mesh['zl'=4,'x'=4,'zh'=2,'y'=8,'c'=2] {'zh','y'}, dimensions={0} | all-to-all | bytes 1310720 | tf_op jit(solution)/shard_map/all_to_all | solution.py:208
  137.2 4.2 %all-to-all-start.3 = ((bf16[16,128,128]{2,1,0:T(8,128)(2,1)}), bf16[16,128,128]{2,1,0:T(8,128)(2,1)}, u32[]{:S(2)}, u32[]{:S(2)}) async-start(bf16[16,128,128]{2,1,0:T(8,128)(2,1)} %copy-done.6), calls=%async_computation.3 | async-start | bytes 1048576 | tf_op jit(solution)/shard_map/all_to_all | solution.py:208
  141.4 1.9 collective-permute-start.11
  145.8 1.8 shard_map.93
  147.6 5.5 %collective-permute-start.12 = (bf16[576,128]{1,0:T(8,128)(2,1)}, bf16[576,128]{1,0:T(8,128)(2,1)}, u32[]{:S(2)}, u32[]{:S(2)}) collective-permute-start(bf16[576,128]{1,0:T(8,128)(2,1)} %get-tuple-element.38), channel_id=1, source_target_pairs={{0,32},{32,64},{64,96},{96,0},{1,33},{33,65},{65,97},{97,1},{2,34}... | collective-permute-start | bytes 442376 | tf_op jit(solution)/shard_map/ppermute | solution.py:216
  153.1 2.3 %collective-permute-start.13 = (bf16[576,128]{1,0:T(8,128)(2,1)}, bf16[576,128]{1,0:T(8,128)(2,1)}, u32[]{:S(2)}, u32[]{:S(2)}) collective-permute-start(bf16[576,128]{1,0:T(8,128)(2,1)} %get-tuple-element.39), channel_id=1, source_target_pairs={{0,64},{32,96},{64,0},{96,32},{1,65},{33,97},{65,1},{97,33},{2,66}... | collective-permute-start | bytes 442376 | tf_op jit(solution)/shard_map/ppermute | solution.py:216
  155.4 2.4 %collective-permute-start.14 = (bf16[576,128]{1,0:T(8,128)(2,1)}, bf16[576,128]{1,0:T(8,128)(2,1)}, u32[]{:S(2)}, u32[]{:S(2)}) collective-permute-start(bf16[576,128]{1,0:T(8,128)(2,1)} %get-tuple-element.40), channel_id=1, source_target_pairs={{0,96},{32,0},{64,32},{96,64},{1,97},{33,1},{65,33},{97,65},{2,98}... | collective-permute-start | bytes 442376 | tf_op jit(solution)/shard_map/ppermute | solution.py:216
  157.8 1.6 all-to-all-done.3.later
  160.8 2.7 %collective-permute-done.13.b2 = bf16[576,128]{1,0:T(8,128)(2,1)} collective-permute-done((bf16[576,128]{1,0:T(8,128)(2,1)}, bf16[576,128]{1,0:T(8,128)(2,1)}, u32[]{:S(2)}, u32[]{:S(2)}) %collective-permute-start.13) | collective-permute-done | bytes 147488 | tf_op jit(solution)/shard_map/ppermute | solution.py:216
  163.5 2.9 %collective-permute-done.14.b3 = bf16[576,128]{1,0:T(8,128)(2,1)} collective-permute-done((bf16[576,128]{1,0:T(8,128)(2,1)}, bf16[576,128]{1,0:T(8,128)(2,1)}, u32[]{:S(2)}, u32[]{:S(2)}) %collective-permute-start.14) | collective-permute-done | bytes 147488 | tf_op jit(solution)/shard_map/ppermute | solution.py:216
  166.4 2.1 shard_map.94
  168.5 1.9 collective-permute-start.18
  170.5 2.0 collective-permute-start.15
  172.5 5.8 %collective-permute-start.16 = (bf16[192,128]{1,0:T(8,128)(2,1)S(1)}, bf16[192,128]{1,0:T(8,128)(2,1)S(1)}, u32[]{:S(2)}, u32[]{:S(2)}) collective-permute-start(bf16[192,128]{1,0:T(8,128)(2,1)S(1)} %get-tuple-element.44), channel_id=1, source_target_pairs={{0,256},{128,384},{256,0},{384,128},{1,257},{129,385},{257,1},{385... | collective-permute-start | bytes 147464 | tf_op jit(solution)/shard_map/ppermute | solution.py:216
  178.3 1.9 collective-permute-start.17
  181.2 3.1 %collective-permute-done.17.f3 = bf16[192,128]{1,0:T(8,128)(2,1)S(1)} collective-permute-done((bf16[192,128]{1,0:T(8,128)(2,1)S(1)}, bf16[192,128]{1,0:T(8,128)(2,1)S(1)}, u32[]{:S(2)}, u32[]{:S(2)}) %collective-permute-start.17) | collective-permute-done | bytes 49184 | tf_op jit(solution)/shard_map/ppermute | solution.py:216
  185.6 12.2 %all-to-all-start.4 = ((f32[16,16,256]{2,1,0:T(8,128)}), f32[16,16,256]{2,1,0:T(8,128)}, u32[]{:S(2)}, u32[]{:S(2)}) async-start(f32[16,16,256]{2,1,0:T(8,128)} %shard_map.99), calls=%async_computation.4 | async-start | bytes 524288 | tf_op jit(solution)/shard_map/all_to_all | solution.py:208
  197.8 1.8 shard_map.95.begun
  199.6 1.7 shard_map.96
  201.2 2.2 collective-permute-start.19
  203.4 3.2 %collective-permute-start.20 = (bf16[512,128]{1,0:T(8,128)(2,1)S(1)}, bf16[512,128]{1,0:T(8,128)(2,1)S(1)}, u32[]{:S(2)}, u32[]{:S(2)}) collective-permute-start(bf16[512,128]{1,0:T(8,128)(2,1)S(1)} %get-tuple-element.49), channel_id=1, source_target_pairs={{0,64},{32,96},{64,0},{96,32},{1,65},{33,97},{65,1},{97,33},{2,66}... | collective-permute-start | bytes 393224 | tf_op jit(solution)/shard_map/ppermute | solution.py:216
  206.6 2.8 %collective-permute-start.21 = (bf16[512,128]{1,0:T(8,128)(2,1)S(1)}, bf16[512,128]{1,0:T(8,128)(2,1)S(1)}, u32[]{:S(2)}, u32[]{:S(2)}) collective-permute-start(bf16[512,128]{1,0:T(8,128)(2,1)S(1)} %get-tuple-element.50), channel_id=1, source_target_pairs={{0,96},{32,0},{64,32},{96,64},{1,97},{33,1},{65,33},{97,65},{2,98}... | collective-permute-start | bytes 393224 | tf_op jit(solution)/shard_map/ppermute | solution.py:216
  209.3 2.4 %collective-permute-done.20.b2 = bf16[512,128]{1,0:T(8,128)(2,1)S(1)} collective-permute-done((bf16[512,128]{1,0:T(8,128)(2,1)S(1)}, bf16[512,128]{1,0:T(8,128)(2,1)S(1)}, u32[]{:S(2)}, u32[]{:S(2)}) %collective-permute-start.20) | collective-permute-done | bytes 131104 | tf_op jit(solution)/shard_map/ppermute | solution.py:216
  211.7 2.9 %collective-permute-done.21.b3 = bf16[512,128]{1,0:T(8,128)(2,1)S(1)} collective-permute-done((bf16[512,128]{1,0:T(8,128)(2,1)S(1)}, bf16[512,128]{1,0:T(8,128)(2,1)S(1)}, u32[]{:S(2)}, u32[]{:S(2)}) %collective-permute-start.21) | collective-permute-done | bytes 131104 | tf_op jit(solution)/shard_map/ppermute | solution.py:216
  215.2 3.5 %collective-permute-start.22 = (bf16[128,128]{1,0:T(8,128)(2,1)S(1)}, bf16[128,128]{1,0:T(8,128)(2,1)S(1)}, u32[]{:S(2)}, u32[]{:S(2)}) collective-permute-start(bf16[128,128]{1,0:T(8,128)(2,1)S(1)} %get-tuple-element.52), channel_id=1, source_target_pairs={{0,128},{128,256},{256,384},{384,0},{1,129},{129,257},{257,385},{3... | collective-permute-start | bytes 98312 | tf_op jit(solution)/shard_map/ppermute | solution.py:216
  218.7 3.1 %collective-permute-start.23 = (bf16[128,128]{1,0:T(8,128)(2,1)S(1)}, bf16[128,128]{1,0:T(8,128)(2,1)S(1)}, u32[]{:S(2)}, u32[]{:S(2)}) collective-permute-start(bf16[128,128]{1,0:T(8,128)(2,1)S(1)} %get-tuple-element.53), channel_id=1, source_target_pairs={{0,256},{128,384},{256,0},{384,128},{1,257},{129,385},{257,1},{385... | collective-permute-start | bytes 98312 | tf_op jit(solution)/shard_map/ppermute | solution.py:216
  221.8 3.3 %collective-permute-start.24 = (bf16[128,128]{1,0:T(8,128)(2,1)S(1)}, bf16[128,128]{1,0:T(8,128)(2,1)S(1)}, u32[]{:S(2)}, u32[]{:S(2)}) collective-permute-start(bf16[128,128]{1,0:T(8,128)(2,1)S(1)} %get-tuple-element.54), channel_id=1, source_target_pairs={{0,384},{128,0},{256,128},{384,256},{1,385},{129,1},{257,129},{385... | collective-permute-start | bytes 98312 | tf_op jit(solution)/shard_map/ppermute | solution.py:216
  225.9 1.7 collective-permute-done.24.h3
  228.5 1.7 copy.11
  (55 shorter events, 18.7 us)
Async XLA Ops:
  0.6 13.8 %collective-permute-start.1 = (bf16[128,256]{1,0:T(8,128)(2,1)}, bf16[128,256]{1,0:T(8,128)(2,1)S(1)}, u32[]{:S(2)}, u32[]{:S(2)}) collective-permute-start(bf16[128,256]{1,0:T(8,128)(2,1)} %f0.1), channel_id=1, source_target_pairs={{0,256},{128,384},{256,0},{384,128},{1,257},{129,385},{257,1},{385... | collective-permute-start | bytes 196616 | tf_op jit(solution)/shard_map/ppermute | solution.py:216
  6.7 8.4 %collective-permute-start = (bf16[128,256]{1,0:T(8,128)(2,1)}, bf16[128,256]{1,0:T(8,128)(2,1)S(1)}, u32[]{:S(2)}, u32[]{:S(2)}) collective-permute-start(bf16[128,256]{1,0:T(8,128)(2,1)} %f0.1), channel_id=1, source_target_pairs={{0,128},{128,256},{256,384},{384,0},{1,129},{129,257},{257,385},{3... | collective-permute-start | bytes 196616 | tf_op jit(solution)/shard_map/ppermute | solution.py:216
  11.0 6.4 %collective-permute-start.2 = (bf16[128,256]{1,0:T(8,128)(2,1)}, bf16[128,256]{1,0:T(8,128)(2,1)S(1)}, u32[]{:S(2)}, u32[]{:S(2)}) collective-permute-start(bf16[128,256]{1,0:T(8,128)(2,1)} %f0.1), channel_id=1, source_target_pairs={{0,384},{128,0},{256,128},{384,256},{1,385},{129,1},{257,129},{385... | collective-permute-start | bytes 196616 | tf_op jit(solution)/shard_map/ppermute | solution.py:216
  17.4 0.8 copy-start.11
  18.3 0.7 copy-start.8
  18.9 14.9 %collective-permute-start.5 = (bf16[4,128,128]{2,1,0:T(8,128)(2,1)S(1)}, bf16[4,128,128]{2,1,0:T(8,128)(2,1)S(1)}, u32[]{:S(2)}, u32[]{:S(2)}) collective-permute-start(bf16[4,128,128]{2,1,0:T(8,128)(2,1)S(1)} %get-tuple-element.31.g0), channel_id=1, source_target_pairs={{0,96},{32,0},{64,32},{96,64},{1,97},{33,1},{65,33},{97,65},{2,98}... | collective-permute-start | bytes 393224 | tf_op jit(solution)/shard_map/ppermute | solution.py:216
  21.7 12.2 %collective-permute-start.4 = (bf16[4,128,128]{2,1,0:T(8,128)(2,1)S(1)}, bf16[4,128,128]{2,1,0:T(8,128)(2,1)S(1)}, u32[]{:S(2)}, u32[]{:S(2)}) collective-permute-start(bf16[4,128,128]{2,1,0:T(8,128)(2,1)S(1)} %get-tuple-element.31.g0), channel_id=1, source_target_pairs={{0,64},{32,96},{64,0},{96,32},{1,65},{33,97},{65,1},{97,33},{2,66}... | collective-permute-start | bytes 393224 | tf_op jit(solution)/shard_map/ppermute | solution.py:216
  25.1 8.8 %collective-permute-start.3 = (bf16[4,128,128]{2,1,0:T(8,128)(2,1)S(1)}, bf16[4,128,128]{2,1,0:T(8,128)(2,1)}, u32[]{:S(2)}, u32[]{:S(2)}) collective-permute-start(bf16[4,128,128]{2,1,0:T(8,128)(2,1)S(1)} %get-tuple-element.31.g0), channel_id=1, source_target_pairs={{0,32},{32,64},{64,96},{96,0},{1,33},{33,65},{65,97},{97,1},{2,34}... | collective-permute-start | bytes 393224 | tf_op jit(solution)/shard_map/ppermute | solution.py:216
  29.4 1.9 copy-start
  31.3 0.7 copy-start.12
  32.0 1.9 copy-start.1
  33.9 0.9 copy-start.9
  36.2 3.7 %copy-start.4 = (bf16[4,128,128]{2,1,0:T(8,128)(2,1)}, bf16[4,128,128]{2,1,0:T(8,128)(2,1)S(1)}, u32[]{:S(2)}) copy-start(bf16[4,128,128]{2,1,0:T(8,128)(2,1)S(1)} %get-tuple-element.34.g0) | copy-start | bytes 393220
  36.2 3.8 %collective-permute-start.6 = (bf16[16,128,128]{2,1,0:T(8,128)(2,1)S(1)}, bf16[16,128,128]{2,1,0:T(8,128)(2,1)S(1)}, u32[]{:S(2)}, u32[]{:S(2)}) collective-permute-start(bf16[16,128,128]{2,1,0:T(8,128)(2,1)S(1)} %get-tuple-element.33), channel_id=1, source_target_pairs={{0,1},{1,0},{2,3},{3,2},{4,5},{5,4},{6,7},{7,6},{8,9},{9,8},{10,11... | collective-permute-start | bytes 1572872 | tf_op jit(solution)/shard_map/ppermute | solution.py:212
  40.0 14.0 %copy-start.5 = (bf16[4,128,128]{2,1,0:T(8,128)(2,1)S(1)}, bf16[4,128,128]{2,1,0:T(8,128)(2,1)}, u32[]{:S(2)}) copy-start(bf16[4,128,128]{2,1,0:T(8,128)(2,1)} %copy-done.4) | copy-start | bytes 393220
  41.0 33.8 %all-to-all-start = ((bf16[16,128,128]{2,1,0:T(8,128)(2,1)}), bf16[16,128,128]{2,1,0:T(8,128)(2,1)}, u32[]{:S(2)}, u32[]{:S(2)}) async-start(bf16[16,128,128]{2,1,0:T(8,128)(2,1)} %add_convert_fusion.1), calls=%async_computation | async-start | bytes 1048576 | tf_op jit(solution)/shard_map/all_to_all | solution.py:208
  54.1 12.4 %collective-permute-start.9 = (bf16[4,128,128]{2,1,0:T(8,128)(2,1)S(1)}, bf16[4,128,128]{2,1,0:T(8,128)(2,1)S(1)}, u32[]{:S(2)}, u32[]{:S(2)}) collective-permute-start(bf16[4,128,128]{2,1,0:T(8,128)(2,1)S(1)} %copy-done.5), channel_id=1, source_target_pairs={{0,96},{32,0},{64,32},{96,64},{1,97},{33,1},{65,33},{97,65},{2,98}... | collective-permute-start | bytes 393224 | tf_op jit(solution)/shard_map/ppermute | solution.py:216
  56.5 10.0 %collective-permute-start.8 = (bf16[4,128,128]{2,1,0:T(8,128)(2,1)S(1)}, bf16[4,128,128]{2,1,0:T(8,128)(2,1)S(1)}, u32[]{:S(2)}, u32[]{:S(2)}) collective-permute-start(bf16[4,128,128]{2,1,0:T(8,128)(2,1)S(1)} %copy-done.5), channel_id=1, source_target_pairs={{0,64},{32,96},{64,0},{96,32},{1,65},{33,97},{65,1},{97,33},{2,66}... | collective-permute-start | bytes 393224 | tf_op jit(solution)/shard_map/ppermute | solution.py:216
  61.9 7.0 %collective-permute-start.7 = (bf16[4,128,128]{2,1,0:T(8,128)(2,1)S(1)}, bf16[4,128,128]{2,1,0:T(8,128)(2,1)S(1)}, u32[]{:S(2)}, u32[]{:S(2)}) collective-permute-start(bf16[4,128,128]{2,1,0:T(8,128)(2,1)S(1)} %copy-done.5), channel_id=1, source_target_pairs={{0,32},{32,64},{64,96},{96,0},{1,33},{33,65},{65,97},{97,1},{2,34}... | collective-permute-start | bytes 393224 | tf_op jit(solution)/shard_map/ppermute | solution.py:216
  70.1 3.8 %collective-permute-start.10 = (bf16[16,128,128]{2,1,0:T(8,128)(2,1)S(1)}, bf16[16,128,128]{2,1,0:T(8,128)(2,1)S(1)}, u32[]{:S(2)}, u32[]{:S(2)}) collective-permute-start(bf16[16,128,128]{2,1,0:T(8,128)(2,1)S(1)} %shard_map.90), channel_id=1, source_target_pairs={{0,1},{1,0},{2,3},{3,2},{4,5},{5,4},{6,7},{7,6},{8,9},{9,8},{10,11... | collective-permute-start | bytes 1572872 | tf_op jit(solution)/shard_map/ppermute | solution.py:212
  73.4 33.3 %copy-start.7 = (bf16[256,256]{1,0:T(8,128)(2,1)S(1)}, bf16[256,256]{1,0:T(8,128)(2,1)}, u32[]{:S(2)}) copy-start(bf16[256,256]{1,0:T(8,128)(2,1)} %weight.3) | copy-start | bytes 393220
  73.4 33.3 %copy-start.10 = (bf16[128,256]{1,0:T(8,128)(2,1)S(1)}, bf16[128,256]{1,0:T(8,128)(2,1)}, u32[]{:S(2)}) copy-start(bf16[128,256]{1,0:T(8,128)(2,1)} %cotangent.1) | copy-start | bytes 196612
  108.6 28.6 %copy-start.6 = (bf16[16,128,128]{2,1,0:T(8,128)(2,1)}, bf16[16,128,128]{2,1,0:T(8,128)(2,1)S(1)}, u32[]{:S(2)}) copy-start(bf16[16,128,128]{2,1,0:T(8,128)(2,1)S(1)} %get-tuple-element.41) | copy-start | bytes 1572868
  137.2 22.2 %all-to-all-start.3 = ((bf16[16,128,128]{2,1,0:T(8,128)(2,1)}), bf16[16,128,128]{2,1,0:T(8,128)(2,1)}, u32[]{:S(2)}, u32[]{:S(2)}) async-start(bf16[16,128,128]{2,1,0:T(8,128)(2,1)} %copy-done.6), calls=%async_computation.3 | async-start | bytes 1048576 | tf_op jit(solution)/shard_map/all_to_all | solution.py:208
  141.4 4.3 %collective-permute-start.11 = (bf16[16,160,128]{2,1,0:T(8,128)(2,1)}, bf16[16,160,128]{2,1,0:T(8,128)(2,1)S(1)}, u32[]{:S(2)}, u32[]{:S(2)}) collective-permute-start(bf16[16,160,128]{2,1,0:T(8,128)(2,1)} %all_to_all.26.own), channel_id=1, source_target_pairs={{0,1},{1,0},{2,3},{3,2},{4,5},{5,4},{6,7},{7,6},{8,9},{9,8},{10,11... | collective-permute-start | bytes 1966088 | tf_op jit(solution)/shard_map/ppermute | solution.py:212
  143.4 1.1 copy-start.2
  144.4 1.3 copy-start.3
  147.6 13.2 %collective-permute-start.12 = (bf16[576,128]{1,0:T(8,128)(2,1)}, bf16[576,128]{1,0:T(8,128)(2,1)}, u32[]{:S(2)}, u32[]{:S(2)}) collective-permute-start(bf16[576,128]{1,0:T(8,128)(2,1)} %get-tuple-element.38), channel_id=1, source_target_pairs={{0,32},{32,64},{64,96},{96,0},{1,33},{33,65},{65,97},{97,1},{2,34}... | collective-permute-start | bytes 442376 | tf_op jit(solution)/shard_map/ppermute | solution.py:216
  153.1 10.4 %collective-permute-start.13 = (bf16[576,128]{1,0:T(8,128)(2,1)}, bf16[576,128]{1,0:T(8,128)(2,1)}, u32[]{:S(2)}, u32[]{:S(2)}) collective-permute-start(bf16[576,128]{1,0:T(8,128)(2,1)} %get-tuple-element.39), channel_id=1, source_target_pairs={{0,64},{32,96},{64,0},{96,32},{1,65},{33,97},{65,1},{97,33},{2,66}... | collective-permute-start | bytes 442376 | tf_op jit(solution)/shard_map/ppermute | solution.py:216
  155.4 11.0 %collective-permute-start.14 = (bf16[576,128]{1,0:T(8,128)(2,1)}, bf16[576,128]{1,0:T(8,128)(2,1)}, u32[]{:S(2)}, u32[]{:S(2)}) collective-permute-start(bf16[576,128]{1,0:T(8,128)(2,1)} %get-tuple-element.40), channel_id=1, source_target_pairs={{0,96},{32,0},{64,32},{96,64},{1,97},{33,1},{65,33},{97,65},{2,98}... | collective-permute-start | bytes 442376 | tf_op jit(solution)/shard_map/ppermute | solution.py:216
  168.5 31.0 %collective-permute-start.18 = (bf16[16,128,128]{2,1,0:T(8,128)(2,1)}, bf16[16,128,128]{2,1,0:T(8,128)(2,1)}, u32[]{:S(2)}, u32[]{:S(2)}) collective-permute-start(bf16[16,128,128]{2,1,0:T(8,128)(2,1)} %get-tuple-element.46.own), channel_id=1, source_target_pairs={{0,1},{1,0},{2,3},{3,2},{4,5},{5,4},{6,7},{7,6},{8,9},{9,8},{10,11... | collective-permute-start | bytes 1572872 | tf_op jit(solution)/shard_map/ppermute | solution.py:212
  170.5 9.8 %collective-permute-start.15 = (bf16[192,128]{1,0:T(8,128)(2,1)S(1)}, bf16[192,128]{1,0:T(8,128)(2,1)S(1)}, u32[]{:S(2)}, u32[]{:S(2)}) collective-permute-start(bf16[192,128]{1,0:T(8,128)(2,1)S(1)} %get-tuple-element.43), channel_id=1, source_target_pairs={{0,128},{128,256},{256,384},{384,0},{1,129},{129,257},{257,385},{3... | collective-permute-start | bytes 147464 | tf_op jit(solution)/shard_map/ppermute | solution.py:216
  172.5 8.7 %collective-permute-start.16 = (bf16[192,128]{1,0:T(8,128)(2,1)S(1)}, bf16[192,128]{1,0:T(8,128)(2,1)S(1)}, u32[]{:S(2)}, u32[]{:S(2)}) collective-permute-start(bf16[192,128]{1,0:T(8,128)(2,1)S(1)} %get-tuple-element.44), channel_id=1, source_target_pairs={{0,256},{128,384},{256,0},{384,128},{1,257},{129,385},{257,1},{385... | collective-permute-start | bytes 147464 | tf_op jit(solution)/shard_map/ppermute | solution.py:216
  178.3 6.0 %collective-permute-start.17 = (bf16[192,128]{1,0:T(8,128)(2,1)S(1)}, bf16[192,128]{1,0:T(8,128)(2,1)S(1)}, u32[]{:S(2)}, u32[]{:S(2)}) collective-permute-start(bf16[192,128]{1,0:T(8,128)(2,1)S(1)} %get-tuple-element.45), channel_id=1, source_target_pairs={{0,384},{128,0},{256,128},{384,256},{1,385},{129,1},{257,129},{385... | collective-permute-start | bytes 147464 | tf_op jit(solution)/shard_map/ppermute | solution.py:216
  185.6 39.5 %all-to-all-start.4 = ((f32[16,16,256]{2,1,0:T(8,128)}), f32[16,16,256]{2,1,0:T(8,128)}, u32[]{:S(2)}, u32[]{:S(2)}) async-start(f32[16,16,256]{2,1,0:T(8,128)} %shard_map.99), calls=%async_computation.4 | async-start | bytes 524288 | tf_op jit(solution)/shard_map/all_to_all | solution.py:208
  201.2 8.1 %collective-permute-start.19 = (bf16[512,128]{1,0:T(8,128)(2,1)S(1)}, bf16[512,128]{1,0:T(8,128)(2,1)S(1)}, u32[]{:S(2)}, u32[]{:S(2)}) collective-permute-start(bf16[512,128]{1,0:T(8,128)(2,1)S(1)} %get-tuple-element.48), channel_id=1, source_target_pairs={{0,32},{32,64},{64,96},{96,0},{1,33},{33,65},{65,97},{97,1},{2,34}... | collective-permute-start | bytes 393224 | tf_op jit(solution)/shard_map/ppermute | solution.py:216
  203.4 8.4 %collective-permute-start.20 = (bf16[512,128]{1,0:T(8,128)(2,1)S(1)}, bf16[512,128]{1,0:T(8,128)(2,1)S(1)}, u32[]{:S(2)}, u32[]{:S(2)}) collective-permute-start(bf16[512,128]{1,0:T(8,128)(2,1)S(1)} %get-tuple-element.49), channel_id=1, source_target_pairs={{0,64},{32,96},{64,0},{96,32},{1,65},{33,97},{65,1},{97,33},{2,66}... | collective-permute-start | bytes 393224 | tf_op jit(solution)/shard_map/ppermute | solution.py:216
  206.6 8.1 %collective-permute-start.21 = (bf16[512,128]{1,0:T(8,128)(2,1)S(1)}, bf16[512,128]{1,0:T(8,128)(2,1)S(1)}, u32[]{:S(2)}, u32[]{:S(2)}) collective-permute-start(bf16[512,128]{1,0:T(8,128)(2,1)S(1)} %get-tuple-element.50), channel_id=1, source_target_pairs={{0,96},{32,0},{64,32},{96,64},{1,97},{33,1},{65,33},{97,65},{2,98}... | collective-permute-start | bytes 393224 | tf_op jit(solution)/shard_map/ppermute | solution.py:216
  215.2 9.9 %collective-permute-start.22 = (bf16[128,128]{1,0:T(8,128)(2,1)S(1)}, bf16[128,128]{1,0:T(8,128)(2,1)S(1)}, u32[]{:S(2)}, u32[]{:S(2)}) collective-permute-start(bf16[128,128]{1,0:T(8,128)(2,1)S(1)} %get-tuple-element.52), channel_id=1, source_target_pairs={{0,128},{128,256},{256,384},{384,0},{1,129},{129,257},{257,385},{3... | collective-permute-start | bytes 98312 | tf_op jit(solution)/shard_map/ppermute | solution.py:216
  218.7 7.2 %collective-permute-start.23 = (bf16[128,128]{1,0:T(8,128)(2,1)S(1)}, bf16[128,128]{1,0:T(8,128)(2,1)S(1)}, u32[]{:S(2)}, u32[]{:S(2)}) collective-permute-start(bf16[128,128]{1,0:T(8,128)(2,1)S(1)} %get-tuple-element.53), channel_id=1, source_target_pairs={{0,256},{128,384},{256,0},{384,128},{1,257},{129,385},{257,1},{385... | collective-permute-start | bytes 98312 | tf_op jit(solution)/shard_map/ppermute | solution.py:216
  221.8 5.8 %collective-permute-start.24 = (bf16[128,128]{1,0:T(8,128)(2,1)S(1)}, bf16[128,128]{1,0:T(8,128)(2,1)S(1)}, u32[]{:S(2)}, u32[]{:S(2)}) collective-permute-start(bf16[128,128]{1,0:T(8,128)(2,1)S(1)} %get-tuple-element.54), channel_id=1, source_target_pairs={{0,384},{128,0},{256,128},{384,256},{1,385},{129,1},{257,129},{385... | collective-permute-start | bytes 98312 | tf_op jit(solution)/shard_map/ppermute | solution.py:216

commit v4 on v2

--- a/solution.py
+++ b/solution.py
@@ -22,7 +22,7 @@
     return lax.dot_general(a, b, dims, preferred_element_type=F32)
 
 
-def plan_kernel(place, info, lists, groups):
+def plan_kernel(place, info, blocks, lists, groups):
     count, core, xi, zi = info[0], info[1], info[2], info[3]
 
     def write(at, k, t, source, half, target):
@@ -34,7 +34,7 @@
         t, a = p >> 4, p & 15
         z, x = a >> 2, a & 3
         half = t >> 1
-        source = (((xi - x) & 3) << 2) + ((zi - z) & 3)
+        source = (x << 2) + z
         target = (((x - xi) & 3) << 2) + ((z - zi) & 3)
         mine, theirs = held
         away = (t & 1) ^ core
@@ -52,9 +52,7 @@
     return lists[field * 2 * SLOTS + which * SLOTS + j]
 
 
-def forward_kernel(which, lists, groups, blocks, g0, g1, g2, g3, out, nodes, acc):
-    for i, part in enumerate((g0, g1, g2, g3)):
-        nodes[4 * i : 4 * i + 4] = part[...]
+def forward_kernel(which, lists, groups, blocks, nodes, out, acc):
     acc[...] = jnp.zeros_like(acc)
 
     def step(i, _):
@@ -86,8 +84,9 @@
     grad = dot(share.astype(F32).T.astype(BF), slopes).astype(BF)
     for s in range(16):
         spread[s, 0:256, :] = turned
-        spread[s, 256:272, :] = grad[16 * s : 16 * s + 16, 0:128]
-        spread[s, 272:288, :] = grad[16 * s : 16 * s + 16, 128:256]
+        rows = slice(32 * (s % 8), 32 * (s % 8) + 32)
+        spread[s, 256:288, :] = grad[rows, 0:128]
+        spread[s, 288:320, :] = grad[rows, 128:256]
 
 
 def split(value):
@@ -115,22 +114,21 @@
 
 
 def backward_other_kernel(lists, groups, blocks, own, other, begun, b0, b1, b2, b3, acc):
-    acc[...] = begun[...]
     back_products(1, lists, groups, blocks, other, acc)
-    grad = jnp.zeros((32, 128), F32)
+    grad = jnp.zeros((64, 128), F32)
     for s in range(16):
-        grad += own[s, 256:288, :].astype(F32) + other[s, 256:288, :].astype(F32)
+        grad += own[s, 256:320, :].astype(F32) + other[s, 256:320, :].astype(F32)
     high, low = split(grad)
     for x, out in enumerate((b0, b1, b2, b3)):
         for z in range(4):
             out[256 * z : 256 * z + 256, :] = acc[4 * x + z].astype(BF)
-        out[1024:1056, :] = high
-        out[1056:1088, :] = low
+        out[1024:1088, :] = high
+        out[1088:1152, :] = low
 
 
 def ordered_sum(me, parts, row, scratch):
     for k, part in enumerate(parts):
-        high, low = part[row : row + 32, :], part[row + 32 : row + 64, :]
+        high, low = part[row : row + 64, :], part[row + 64 : row + 128, :]
         scratch[(me - k) & 3] = high.astype(F32) + low.astype(F32)
     return scratch[0] + scratch[1] + scratch[2] + scratch[3]
 
@@ -144,30 +142,33 @@
         for part in parts[1:]:
             total += part[rows, :].astype(F32)
         out[0:256, :] = total.astype(BF)
-        out[256:288, :] = high
-        out[288:320, :] = low
-
-
-def last_kernel(scale, info, f0, f1, f2, f3, weight, input_grad, grad_out, scratch):
-    parts = (f0, f1, f2, f3)
-    grad = ordered_sum(info[3], parts, 256, scratch) * scale
-    for s in range(16):
-        grad_out[s, :, 0:128] = grad[0:16]
-        grad_out[s, :, 128:256] = grad[16:32]
-    total = parts[0][0:256, :].astype(F32)
-    for part in parts[1:]:
+        out[256:320, :] = high
+        out[320:384, :] = low
+
+
+def grad_kernel(scale, info, f0, f1, f2, f3, grad_out, scratch):
+    grad = (ordered_sum(info[3], (f0, f1, f2, f3), 256, scratch) * scale).astype(BF)
+    for s in range(8):
+        grad_out[s, :, 0:128] = grad[0:32]
+        grad_out[s, :, 128:256] = grad[32:64]
+
+
+def last_kernel(f0, f1, f2, f3, weight, input_grad):
+    total = f0[0:256, :].astype(F32)
+    for part in (f1, f2, f3):
         total += part[0:256, :].astype(F32)
     back = total.astype(BF).astype(F32).T.astype(BF)
     input_grad[...] = dot(back, weight[...], (((1,), (1,)), ((), ()))).astype(BF)
 
 
-def call(kernel, outs, kinds, scratch=(), flops=0, size=0):
+def call(kernel, outs, kinds, scratch=(), flops=0, size=0, alias=None):
     return pl.pallas_call(
         kernel,
         out_shape=[jax.ShapeDtypeStruct(s, d) for s, d, _ in outs],
         in_specs=kinds,
         out_specs=[k for _, _, k in outs],
         scratch_shapes=list(scratch),
+        input_output_aliases=alias or {},
         compiler_params=LIMIT,
         cost_estimate=pl.CostEstimate(flops=flops, bytes_accessed=size, transcendentals=0),
     )
@@ -196,27 +197,27 @@
     lists, groups = call(
         plan_kernel,
         [((10 * SLOTS,), i32, SMEM), ((2,), i32, SMEM)],
-        [SMEM, SMEM],
+        [SMEM, SMEM, VMEM],
         size=2**20,
-    )(block_pos[0, 0], info)
-
-    line = jnp.stack([features] + [rotate(features, "zl", k) for k in (1, 2, 3)])
-    plane = [line] + [rotate(line, "x", k) for k in (1, 2, 3)]
+    )(block_pos[0, 0], info, tile)
+
+    line = exchange(jnp.broadcast_to(features[None], (4, 128, 256)), "zl")
+    nodes = exchange(jnp.broadcast_to(line[None], (4, 4, 128, 256)), "x").reshape(16, 128, 256)
     send, keep = [
         call(
             functools.partial(forward_kernel, which),
             [((16, 128, 256), BF, VMEM)],
-            [SMEM, SMEM] + [VMEM] * 5,
-            [pltpu.VMEM((16, 128, 256), BF), pltpu.VMEM((17, 128, 256), F32)],
+            [SMEM, SMEM, VMEM, VMEM],
+            [pltpu.VMEM((17, 128, 256), F32)],
             **heavy,
-        )(lists, groups, tile, *plane)[0]
+        )(lists, groups, tile, nodes)[0]
         for which in (1, 0)
     ]
     pair = (keep.astype(F32) + swap(send).astype(F32)).astype(BF)
     parts = exchange(pair, ("zh", "y"))
     output, spread = call(
         middle_kernel,
-        [((128, 256), BF, VMEM), ((16, 288, 128), BF, VMEM)],
+        [((128, 256), BF, VMEM), ((16, 320, 128), BF, VMEM)],
         [VMEM, VMEM, VMEM],
     )(parts, weight, cotangent)
     own = exchange(spread, ("zh", "y"))
@@ -229,26 +230,27 @@
     )(lists, groups, tile, own)
     back = call(
         backward_other_kernel,
-        [((1088, 128), BF, VMEM)] * 4,
+        [((1152, 128), BF, VMEM)] * 4 + [((17, 256, 128), F32, VMEM)],
         [SMEM, SMEM] + [VMEM] * 4,
-        [pltpu.VMEM((17, 256, 128), F32)],
+        alias={5: 4},
         **heavy,
     )(lists, groups, tile, own, other, begun)
     back = [back[0]] + [rotate(back[k], "x", k) for k in (1, 2, 3)]
     folded = call(
         fold_kernel,
-        [((320, 128), BF, VMEM)] * 4,
+        [((384, 128), BF, VMEM)] * 4,
         [SMEM] + [VMEM] * 4,
-        [pltpu.VMEM((4, 32, 128), F32)],
+        [pltpu.VMEM((4, 64, 128), F32)],
     )(info, *back)
     folded = [folded[0]] + [rotate(folded[k], "zl", k) for k in (1, 2, 3)]
-    input_grad, grad = call(
-        functools.partial(last_kernel, 1.0 / math.sqrt(nodes_total)),
-        [((128, 256), BF, VMEM), ((16, 16, 256), F32, VMEM)],
-        [SMEM] + [VMEM] * 5,
-        [pltpu.VMEM((4, 32, 128), F32)],
-    )(info, *folded, weight)
-    weight_grad = exchange(grad, ("zh", "y")).reshape(256, 256)
+    (grad,) = call(
+        functools.partial(grad_kernel, 1.0 / math.sqrt(nodes_total)),
+        [((8, 32, 256), BF, VMEM)],
+        [SMEM] + [VMEM] * 4,
+        [pltpu.VMEM((4, 64, 128), F32)],
+    )(info, *folded)
+    weight_grad = exchange(grad, "y").reshape(256, 256).astype(F32)
+    (input_grad,) = call(last_kernel, [((128, 256), BF, VMEM)], [VMEM] * 5, flops=2**24, size=2**20)(*folded, weight)
     return (output, input_grad, weight_grad)
 
 

time: 194 us -> 190 us (0.979)
  starting transfers between devices: 47.2 us -> 33.4 us
  Pallas kernels: 13.8 us -> 19.8 us
  waiting for transfers between devices: 25.7 us -> 31.4 us
    ppermute x12 -> x6, starting transfers between devices: 43.4 us -> 19.4 us  [rotate(): return lax.ppermute(value, axis, [(i, (i + k) % 4) for i in range(4)])]
    all_to_all x0 -> x2, waiting for transfers between devices: none -> 15.5 us  [exchange(): return lax.all_to_all(value, axes, 0, 0, tiled=True)]
    all_to_all x0 -> x2, starting transfers between devices: none -> 10.1 us  [exchange(): return lax.all_to_all(value, axes, 0, 0, tiled=True)]
    ppermute x12 -> x6, waiting for transfers between devices: 24.2 us -> 15.8 us  [rotate(): return lax.ppermute(value, axis, [(i, (i + k) % 4) for i in range(4)])]
    unnamed x9 -> x8, local copies, waits for them, and re-layouts: 3.26 us -> 0.02 us
    pallas_call x2, Pallas kernels: 3.19 us -> 6.01 us  [shards(): call(functools.partial(forward_kernel, which), [((16, 128, 256), BF, VMEM...]
    broadcast_in_dim x0 -> x2, local copies, waits for them, and re-layouts: none -> 2.1 us  [the longest x1 1.09 us: shards(): jnp.broadcast_to(line[None], (4, 4, 128, 256))]
    pallas_call x4 -> x5, Pallas kernels: 6.14 us -> 7.11 us  [the longest x1 3.39 us: shards(): call(backward_other_kernel, [((1152, 128), BF, VMEM)] * 4 + [((17, 256, 1...]
  transfers between devices with their start and end apart: 14 -> 10, of which waited for: 10 -> 7; matrix products, arithmetic and copies ran while one was open for 0% -> 0% of each run, Pallas kernels for 3% -> 6%
where the time goes in v4:
time: 190 us; the launch traced here: 189 us
  blocking collectives  99.5 us (52%)
  starting transfers between devices  33.4 us (18%)
  waiting for transfers between devices  31.4 us (17%)
  Pallas kernels  19.8 us (10%)
  local copies, waits for them, and re-layouts  2.12 us (1%)
    all_to_all x3, blocking collectives, exchange(): return lax.all_to_all(value, axes, 0, 0, tiled=True)  99.5 us
    ppermute x6, starting transfers between devices, rotate(): return lax.ppermute(value, axis, [(i, (i + k) % 4) for i in range(4)])  19.4 us
    ppermute x6, waiting for transfers between devices, rotate(): return lax.ppermute(value, axis, [(i, (i + k) % 4) for i in range(4)])  15.8 us
    all_to_all x2, waiting for transfers between devices, exchange(): return lax.all_to_all(value, axes, 0, 0, tiled=True)  15.5 us
    all_to_all x2, starting transfers between devices, exchange(): return lax.all_to_all(value, axes, 0, 0, tiled=True)  10.1 us
    pallas_call x2, Pallas kernels, shards(): call(functools.partial(forward_kernel, which), [((16, 128, 256), BF, VMEM...  6.01 us
    ppermute x2, starting transfers between devices, swap(): return lax.ppermute(value, 'c', [(0, 1), (1, 0)])  3.83 us
  transfers between devices with their start and end apart: 10, of which 7 were waited for; matrix products, arithmetic and copies ran while one was open for 0% of the time, Pallas kernels for 6%

profile of v4, /device:TPU:6, one launch (start us, length us, event | category | flops | bytes accessed | tf_op | source)
XLA Modules:
  0.0 188.8 jit_solution(3890826029353513301)
XLA Ops:
  0.6 0.0 copy-start.3
  0.6 0.0 copy-start
  0.7 1.0 broadcast_in_dim.4
  1.7 15.9 %all_to_all.25 = bf16[4,128,256]{2,1,0:T(8,128)(2,1)S(1)} all-to-all(bf16[4,128,256]{2,1,0:T(8,128)(2,1)S(1)} %broadcast_in_dim.4), channel_id=1, replica_groups=mesh['zl'=4,'x'=4,'zh'=2,'y'=8,'c'=2] {'zl'}, dimensions={0} | all-to-all | bytes 524288 | tf_op jit(solution)/shard_map/all_to_all | solution.py:178
  17.6 1.1 broadcast_in_dim.5
  18.7 4.8 %all-to-all-start.1 = ((bf16[4,4,128,256]{3,2,1,0:T(8,128)(2,1)}), bf16[4,4,128,256]{3,2,1,0:T(8,128)(2,1)}, u32[]{:S(2)}, u32[]{:S(2)}) async-start(bf16[4,4,128,256]{3,2,1,0:T(8,128)(2,1)} %broadcast_in_dim.5), calls=%async_computation.1 | async-start | bytes 2097152 | tf_op jit(solution)/shard_map/all_to_all | solution.py:178
  24.1 0.1 pad_add_fusion.info
  24.2 0.0 copy-done.3
  24.2 0.0 copy-done
  24.2 2.9 %shard_map.85 = (s32[1120]{0:T(1024)S(1)}, s32[2]{0:T(128)S(1)}) custom-call(s32[96]{0:T(128)S(1)} %bitcast.16, s32[4]{0:T(128)S(1)} %pad_add_fusion.info, bf16[96,128,128]{2,1,0:T(8,128)(2,1)S(1)} %bitcast.13), custom_call_target="tpu_custom_call" | custom-call | bytes 1048576 | tf_op jit(solution)/shard_map/pallas_call | solution.py:197
  27.1 7.3 %all-to-all-done.1 = bf16[4,4,128,256]{3,2,1,0:T(8,128)(2,1)} async-done(((bf16[4,4,128,256]{3,2,1,0:T(8,128)(2,1)}), bf16[4,4,128,256]{3,2,1,0:T(8,128)(2,1)}, u32[]{:S(2)}, u32[]{:S(2)}) %all-to-all-start.1) | async-done | bytes 1048608 | tf_op jit(solution)/shard_map/all_to_all | solution.py:178
  34.3 2.8 %shard_map.87 = bf16[16,128,256]{2,1,0:T(8,128)(2,1)S(1)} custom-call(s32[1120]{0:T(1024)S(1)} %get-tuple-element.15.lists, s32[2]{0:T(128)S(1)} %get-tuple-element.16.groups, bf16[96,128,128]{2,1,0:T(8,128)(2,1)S(1)} %bitcast.14, bf16[16,128,256]{2,1,0:T(8,128)(2,1)} %bitcast.6.nodes), custom_call_target="tpu_custom_call" | custom-call | flops 800000000 | bytes 6291456 | tf_op jit(solution)/shard_map/pallas_call | solution.py:207
  37.1 1.9 %collective-permute-start = (bf16[16,128,256]{2,1,0:T(8,128)(2,1)S(1)}, bf16[16,128,256]{2,1,0:T(8,128)(2,1)S(1)}, u32[]{:S(2)}, u32[]{:S(2)}) collective-permute-start(bf16[16,128,256]{2,1,0:T(8,128)(2,1)S(1)} %shard_map.87), channel_id=1, source_target_pairs={{0,1},{1,0},{2,3},{3,2},{4,5},{5,4},{6,7},{7,6},{8,9},{9,8},{10,11... | collective-permute-start | bytes 3145736 | tf_op jit(solution)/shard_map/ppermute | solution.py:182
  39.1 3.2 %shard_map.86 = bf16[16,128,256]{2,1,0:T(8,128)(2,1)S(1)} custom-call(s32[1120]{0:T(1024)S(1)} %get-tuple-element.15.lists, s32[2]{0:T(128)S(1)} %get-tuple-element.16.groups, bf16[96,128,128]{2,1,0:T(8,128)(2,1)S(1)} %bitcast.15, bf16[16,128,256]{2,1,0:T(8,128)(2,1)} %bitcast.6.nodes), custom_call_target="tpu_custom_call" | custom-call | flops 800000000 | bytes 6291456 | tf_op jit(solution)/shard_map/pallas_call | solution.py:207
  42.3 0.0 copy-start.1
  42.3 0.0 copy-start.2
  42.3 0.0 collective-permute-done
  42.3 0.3 add_convert_fusion
  42.7 42.4 %all_to_all.26.parts = bf16[16,128,256]{2,1,0:T(8,128)(2,1)S(1)} all-to-all(bf16[16,128,256]{2,1,0:T(8,128)(2,1)S(1)} %add_convert_fusion), channel_id=1, replica_groups=mesh['zl'=4,'x'=4,'zh'=2,'y'=8,'c'=2] {'zh','y'}, dimensions={0} | all-to-all | bytes 2097152 | tf_op jit(solution)/shard_map/all_to_all | solution.py:178
  85.1 0.0 copy-done.1
  85.1 0.0 copy-done.2
  85.1 0.9 shard_map.88
  86.0 41.1 %all_to_all.27.own = bf16[16,320,128]{2,1,0:T(8,128)(2,1)S(1)} all-to-all(bf16[16,320,128]{2,1,0:T(8,128)(2,1)S(1)} %get-tuple-element.18), channel_id=1, replica_groups=mesh['zl'=4,'x'=4,'zh'=2,'y'=8,'c'=2] {'zh','y'}, dimensions={0} | all-to-all | bytes 2621440 | tf_op jit(solution)/shard_map/all_to_all | solution.py:178
  127.2 1.9 %collective-permute-start.1 = (bf16[16,320,128]{2,1,0:T(8,128)(2,1)S(1)}, bf16[16,320,128]{2,1,0:T(8,128)(2,1)S(1)}, u32[]{:S(2)}, u32[]{:S(2)}) collective-permute-start(bf16[16,320,128]{2,1,0:T(8,128)(2,1)S(1)} %all_to_all.27.own), channel_id=1, source_target_pairs={{0,1},{1,0},{2,3},{3,2},{4,5},{5,4},{6,7},{7,6},{8,9},{9,8},{10,11... | collective-permute-start | bytes 3932168 | tf_op jit(solution)/shard_map/ppermute | solution.py:182
  129.1 3.8 %shard_map.89.begun = f32[17,256,128]{2,1,0:T(8,128)S(1)} custom-call(s32[1120]{0:T(1024)S(1)} %get-tuple-element.15.lists, s32[2]{0:T(128)S(1)} %get-tuple-element.16.groups, bf16[96,128,128]{2,1,0:T(8,128)(2,1)} %bitcast.11, bf16[16,320,128]{2,1,0:T(8,128)(2,1)S(1)} %all_to_all.27.own), custom_call_target="tpu_custom_call" | custom-call | flops 800000000 | bytes 6291456 | tf_op jit(solution)/shard_map/pallas_call | solution.py:225
  132.9 0.0 collective-permute-done.1.other
  132.9 3.4 %shard_map.90 = (bf16[1152,128]{1,0:T(8,128)(2,1)S(1)}, bf16[1152,128]{1,0:T(8,128)(2,1)S(1)}, bf16[1152,128]{1,0:T(8,128)(2,1)S(1)}, bf16[1152,128]{1,0:T(8,128)(2,1)S(1)}, f32[17,256,128]{2,1,0:T(8,128)S(1)}) custom-call(s32[1120]{0:T(1024)S(1)} %get-tuple-element.15.lists, s32[2]{0:T(128)S(1)} %get-tuple-element.16.groups, ...), custom_call_target="tpu_custom_call", output_to_operand_aliasing={{4}: (5, {})} | custom-call | flops 800000000 | bytes 6291456 | tf_op jit(solution)/shard_map/pallas_call | solution.py:231
  136.3 3.0 %collective-permute-start.2 = (bf16[1152,128]{1,0:T(8,128)(2,1)S(1)}, bf16[1152,128]{1,0:T(8,128)(2,1)S(1)}, u32[]{:S(2)}, u32[]{:S(2)}) collective-permute-start(bf16[1152,128]{1,0:T(8,128)(2,1)S(1)} %get-tuple-element.20), channel_id=1, source_target_pairs={{0,32},{32,64},{64,96},{96,0},{1,33},{33,65},{65,97},{97,1},{2,34}... | collective-permute-start | bytes 884744 | tf_op jit(solution)/shard_map/ppermute | solution.py:186
  139.3 2.4 %collective-permute-start.3 = (bf16[1152,128]{1,0:T(8,128)(2,1)S(1)}, bf16[1152,128]{1,0:T(8,128)(2,1)S(1)}, u32[]{:S(2)}, u32[]{:S(2)}) collective-permute-start(bf16[1152,128]{1,0:T(8,128)(2,1)S(1)} %get-tuple-element.21), channel_id=1, source_target_pairs={{0,64},{32,96},{64,0},{96,32},{1,65},{33,97},{65,1},{97,33},{2,66}... | collective-permute-start | bytes 884744 | tf_op jit(solution)/shard_map/ppermute | solution.py:186
  141.7 3.3 %collective-permute-start.4 = (bf16[1152,128]{1,0:T(8,128)(2,1)S(1)}, bf16[1152,128]{1,0:T(8,128)(2,1)S(1)}, u32[]{:S(2)}, u32[]{:S(2)}) collective-permute-start(bf16[1152,128]{1,0:T(8,128)(2,1)S(1)} %get-tuple-element.22), channel_id=1, source_target_pairs={{0,96},{32,0},{64,32},{96,64},{1,97},{33,1},{65,33},{97,65},{2,98}... | collective-permute-start | bytes 884744 | tf_op jit(solution)/shard_map/ppermute | solution.py:186
  145.1 7.0 %collective-permute-done.2.b1 = bf16[1152,128]{1,0:T(8,128)(2,1)S(1)} collective-permute-done((bf16[1152,128]{1,0:T(8,128)(2,1)S(1)}, bf16[1152,128]{1,0:T(8,128)(2,1)S(1)}, u32[]{:S(2)}, u32[]{:S(2)}) %collective-permute-start.2) | collective-permute-done | bytes 294944 | tf_op jit(solution)/shard_map/ppermute | solution.py:186
  152.1 0.6 collective-permute-done.3.b2
  152.7 5.0 %collective-permute-done.4.b3 = bf16[1152,128]{1,0:T(8,128)(2,1)S(1)} collective-permute-done((bf16[1152,128]{1,0:T(8,128)(2,1)S(1)}, bf16[1152,128]{1,0:T(8,128)(2,1)S(1)}, u32[]{:S(2)}, u32[]{:S(2)}) %collective-permute-start.4) | collective-permute-done | bytes 294944 | tf_op jit(solution)/shard_map/ppermute | solution.py:186
  157.7 0.7 shard_map.91
  158.4 3.4 %collective-permute-start.5 = (bf16[384,128]{1,0:T(8,128)(2,1)S(1)}, bf16[384,128]{1,0:T(8,128)(2,1)S(1)}, u32[]{:S(2)}, u32[]{:S(2)}) collective-permute-start(bf16[384,128]{1,0:T(8,128)(2,1)S(1)} %get-tuple-element.24), channel_id=1, source_target_pairs={{0,128},{128,256},{256,384},{384,0},{1,129},{129,257},{257,385},{3... | collective-permute-start | bytes 294920 | tf_op jit(solution)/shard_map/ppermute | solution.py:186
  161.8 3.5 %collective-permute-start.6 = (bf16[384,128]{1,0:T(8,128)(2,1)S(1)}, bf16[384,128]{1,0:T(8,128)(2,1)S(1)}, u32[]{:S(2)}, u32[]{:S(2)}) collective-permute-start(bf16[384,128]{1,0:T(8,128)(2,1)S(1)} %get-tuple-element.25), channel_id=1, source_target_pairs={{0,256},{128,384},{256,0},{384,128},{1,257},{129,385},{257,1},{385... | collective-permute-start | bytes 294920 | tf_op jit(solution)/shard_map/ppermute | solution.py:186
  165.2 3.9 %collective-permute-start.7 = (bf16[384,128]{1,0:T(8,128)(2,1)S(1)}, bf16[384,128]{1,0:T(8,128)(2,1)S(1)}, u32[]{:S(2)}, u32[]{:S(2)}) collective-permute-start(bf16[384,128]{1,0:T(8,128)(2,1)S(1)} %get-tuple-element.26), channel_id=1, source_target_pairs={{0,384},{128,0},{256,128},{384,256},{1,385},{129,1},{257,129},{385... | collective-permute-start | bytes 294920 | tf_op jit(solution)/shard_map/ppermute | solution.py:186
  169.1 0.0 collective-permute-done.5.f1
  169.1 2.7 %collective-permute-done.6.f2 = bf16[384,128]{1,0:T(8,128)(2,1)S(1)} collective-permute-done((bf16[384,128]{1,0:T(8,128)(2,1)S(1)}, bf16[384,128]{1,0:T(8,128)(2,1)S(1)}, u32[]{:S(2)}, u32[]{:S(2)}) %collective-permute-start.6) | collective-permute-done | bytes 98336 | tf_op jit(solution)/shard_map/ppermute | solution.py:186
  171.8 0.5 collective-permute-done.7.f3
  172.3 1.2 shard_map.93
  173.6 5.4 %all-to-all-start.4 = ((bf16[8,32,256]{2,1,0:T(8,128)(2,1)}), bf16[8,32,256]{2,1,0:T(8,128)(2,1)S(1)}, u32[]{:S(2)}, u32[]{:S(2)}) async-start(bf16[8,32,256]{2,1,0:T(8,128)(2,1)} %shard_map.93), calls=%async_computation.4 | async-start | bytes 262144 | tf_op jit(solution)/shard_map/all_to_all | solution.py:178
  178.9 0.9 shard_map.92
  179.8 8.3 %all-to-all-done.4 = bf16[8,32,256]{2,1,0:T(8,128)(2,1)S(1)} async-done(((bf16[8,32,256]{2,1,0:T(8,128)(2,1)}), bf16[8,32,256]{2,1,0:T(8,128)(2,1)S(1)}, u32[]{:S(2)}, u32[]{:S(2)}) %all-to-all-start.4) | async-done | bytes 131104 | tf_op jit(solution)/shard_map/all_to_all | solution.py:178
  188.0 0.7 bitcast_convert_fusion
Async XLA Ops:
  0.6 23.6 %copy-start.3 = (s32[1,1,96]{2,1,0:T(1,128)S(1)}, s32[1,1,96]{2,1,0:T(1,128)}, u32[]{:S(2)}) copy-start(s32[1,1,96]{2,1,0:T(1,128)} %param.10) | copy-start | bytes 1156
  0.6 23.5 %copy-start = (bf16[1,1,96,128,128]{4,3,2,1,0:T(8,128)(2,1)S(1)}, bf16[1,1,96,128,128]{4,3,2,1,0:T(8,128)(2,1)}, u32[]{:S(2)}) copy-start(bf16[1,1,96,128,128]{4,3,2,1,0:T(8,128)(2,1)} %param.9) | copy-start | bytes 9437188
  18.7 15.7 %all-to-all-start.1 = ((bf16[4,4,128,256]{3,2,1,0:T(8,128)(2,1)}), bf16[4,4,128,256]{3,2,1,0:T(8,128)(2,1)}, u32[]{:S(2)}, u32[]{:S(2)}) async-start(bf16[4,4,128,256]{3,2,1,0:T(8,128)(2,1)} %broadcast_in_dim.5), calls=%async_computation.1 | async-start | bytes 2097152 | tf_op jit(solution)/shard_map/all_to_all | solution.py:178
  37.1 5.2 %collective-permute-start = (bf16[16,128,256]{2,1,0:T(8,128)(2,1)S(1)}, bf16[16,128,256]{2,1,0:T(8,128)(2,1)S(1)}, u32[]{:S(2)}, u32[]{:S(2)}) collective-permute-start(bf16[16,128,256]{2,1,0:T(8,128)(2,1)S(1)} %shard_map.87), channel_id=1, source_target_pairs={{0,1},{1,0},{2,3},{3,2},{4,5},{5,4},{6,7},{7,6},{8,9},{9,8},{10,11... | collective-permute-start | bytes 3145736 | tf_op jit(solution)/shard_map/ppermute | solution.py:182
  42.3 42.8 %copy-start.1 = (bf16[256,256]{1,0:T(8,128)(2,1)S(1)}, bf16[256,256]{1,0:T(8,128)(2,1)}, u32[]{:S(2)}) copy-start(bf16[256,256]{1,0:T(8,128)(2,1)} %weight.3) | copy-start | bytes 393220
  42.3 42.8 %copy-start.2 = (bf16[128,256]{1,0:T(8,128)(2,1)S(1)}, bf16[128,256]{1,0:T(8,128)(2,1)}, u32[]{:S(2)}) copy-start(bf16[128,256]{1,0:T(8,128)(2,1)} %cotangent.1) | copy-start | bytes 196612
  127.2 5.7 %collective-permute-start.1 = (bf16[16,320,128]{2,1,0:T(8,128)(2,1)S(1)}, bf16[16,320,128]{2,1,0:T(8,128)(2,1)S(1)}, u32[]{:S(2)}, u32[]{:S(2)}) collective-permute-start(bf16[16,320,128]{2,1,0:T(8,128)(2,1)S(1)} %all_to_all.27.own), channel_id=1, source_target_pairs={{0,1},{1,0},{2,3},{3,2},{4,5},{5,4},{6,7},{7,6},{8,9},{9,8},{10,11... | collective-permute-start | bytes 3932168 | tf_op jit(solution)/shard_map/ppermute | solution.py:182
  136.3 15.8 %collective-permute-start.2 = (bf16[1152,128]{1,0:T(8,128)(2,1)S(1)}, bf16[1152,128]{1,0:T(8,128)(2,1)S(1)}, u32[]{:S(2)}, u32[]{:S(2)}) collective-permute-start(bf16[1152,128]{1,0:T(8,128)(2,1)S(1)} %get-tuple-element.20), channel_id=1, source_target_pairs={{0,32},{32,64},{64,96},{96,0},{1,33},{33,65},{65,97},{97,1},{2,34}... | collective-permute-start | bytes 884744 | tf_op jit(solution)/shard_map/ppermute | solution.py:186
  139.3 13.4 %collective-permute-start.3 = (bf16[1152,128]{1,0:T(8,128)(2,1)S(1)}, bf16[1152,128]{1,0:T(8,128)(2,1)S(1)}, u32[]{:S(2)}, u32[]{:S(2)}) collective-permute-start(bf16[1152,128]{1,0:T(8,128)(2,1)S(1)} %get-tuple-element.21), channel_id=1, source_target_pairs={{0,64},{32,96},{64,0},{96,32},{1,65},{33,97},{65,1},{97,33},{2,66}... | collective-permute-start | bytes 884744 | tf_op jit(solution)/shard_map/ppermute | solution.py:186
  141.7 15.9 %collective-permute-start.4 = (bf16[1152,128]{1,0:T(8,128)(2,1)S(1)}, bf16[1152,128]{1,0:T(8,128)(2,1)S(1)}, u32[]{:S(2)}, u32[]{:S(2)}) collective-permute-start(bf16[1152,128]{1,0:T(8,128)(2,1)S(1)} %get-tuple-element.22), channel_id=1, source_target_pairs={{0,96},{32,0},{64,32},{96,64},{1,97},{33,1},{65,33},{97,65},{2,98}... | collective-permute-start | bytes 884744 | tf_op jit(solution)/shard_map/ppermute | solution.py:186
  158.4 10.7 %collective-permute-start.5 = (bf16[384,128]{1,0:T(8,128)(2,1)S(1)}, bf16[384,128]{1,0:T(8,128)(2,1)S(1)}, u32[]{:S(2)}, u32[]{:S(2)}) collective-permute-start(bf16[384,128]{1,0:T(8,128)(2,1)S(1)} %get-tuple-element.24), channel_id=1, source_target_pairs={{0,128},{128,256},{256,384},{384,0},{1,129},{129,257},{257,385},{3... | collective-permute-start | bytes 294920 | tf_op jit(solution)/shard_map/ppermute | solution.py:186
  161.8 10.1 %collective-permute-start.6 = (bf16[384,128]{1,0:T(8,128)(2,1)S(1)}, bf16[384,128]{1,0:T(8,128)(2,1)S(1)}, u32[]{:S(2)}, u32[]{:S(2)}) collective-permute-start(bf16[384,128]{1,0:T(8,128)(2,1)S(1)} %get-tuple-element.25), channel_id=1, source_target_pairs={{0,256},{128,384},{256,0},{384,128},{1,257},{129,385},{257,1},{385... | collective-permute-start | bytes 294920 | tf_op jit(solution)/shard_map/ppermute | solution.py:186
  165.2 7.1 %collective-permute-start.7 = (bf16[384,128]{1,0:T(8,128)(2,1)S(1)}, bf16[384,128]{1,0:T(8,128)(2,1)S(1)}, u32[]{:S(2)}, u32[]{:S(2)}) collective-permute-start(bf16[384,128]{1,0:T(8,128)(2,1)S(1)} %get-tuple-element.26), channel_id=1, source_target_pairs={{0,384},{128,0},{256,128},{384,256},{1,385},{129,1},{257,129},{385... | collective-permute-start | bytes 294920 | tf_op jit(solution)/shard_map/ppermute | solution.py:186
  173.6 14.5 %all-to-all-start.4 = ((bf16[8,32,256]{2,1,0:T(8,128)(2,1)}), bf16[8,32,256]{2,1,0:T(8,128)(2,1)S(1)}, u32[]{:S(2)}, u32[]{:S(2)}) async-start(bf16[8,32,256]{2,1,0:T(8,128)(2,1)} %shard_map.93), calls=%async_computation.4 | async-start | bytes 262144 | tf_op jit(solution)/shard_map/all_to_all | solution.py:178

commit v5 on v4

--- a/solution.py
+++ b/solution.py
@@ -23,7 +23,7 @@
 
 
 def plan_kernel(place, info, blocks, lists, groups):
-    count, core, xi, zi = info[0], info[1], info[2], info[3]
+    count, core, xi, zi, odd = info[0], info[1], info[2], info[3], info[4]
 
     def write(at, k, t, source, half, target):
         for f, value in enumerate((k, t, source, half, target)):
@@ -33,7 +33,7 @@
         p = place[k]
         t, a = p >> 4, p & 15
         z, x = a >> 2, a & 3
-        half = t >> 1
+        half = (((t >> 1 & 1) ^ odd) << 3) + (t >> 2)
         source = (x << 2) + z
         target = (((x - xi) & 3) << 2) + ((z - zi) & 3)
         mine, theirs = held
@@ -71,7 +71,7 @@
 
 def middle_kernel(parts, weight, cotangent, output, spread):
     total = parts[0].astype(F32)
-    for s in range(1, 16):
+    for s in range(1, 8):
         total += parts[s].astype(F32)
     share = total.astype(BF)
     pre = dot(share, weight[...])
@@ -81,76 +81,77 @@
     slopes32 = cotangent[...].astype(F32) * slope
     slopes = slopes32.astype(BF)
     turned = slopes.astype(F32).T.astype(BF)
-    grad = dot(share.astype(F32).T.astype(BF), slopes).astype(BF)
-    for s in range(16):
-        spread[s, 0:256, :] = turned
-        rows = slice(32 * (s % 8), 32 * (s % 8) + 32)
-        spread[s, 256:288, :] = grad[rows, 0:128]
-        spread[s, 288:320, :] = grad[rows, 128:256]
-
-
-def split(value):
-    high = value.astype(BF)
-    return high, (value - high.astype(F32)).astype(BF)
-
-
-def back_products(which, lists, groups, blocks, source, acc):
+    columns = share.astype(F32).T.astype(BF)
+    for s in range(8):
+        spread[s, 0:128, :] = turned[0:128]
+        spread[s, 128:192, :] = columns[64 * (s % 4) : 64 * (s % 4) + 64]
+        spread[s, 192:320, :] = turned[128:256]
+
+
+def back_products(which, lists, groups, blocks, same, near, far, source, acc):
+    source[0:8, 0:128, :] = same[:, 0:128, :]
+    source[0:8, 128:256, :] = same[:, 192:320, :]
+    source[8:16, 0:128, :] = near[:, 0:128, :]
+    source[8:16, 128:256, :] = far[...]
+
     def step(i, _):
         products = []
         for g in range(GROUP):
             j = i * GROUP + g
-            product = dot(source[entry(lists, which, 3, j), 0:256, :], blocks[entry(lists, which, 0, j)])
+            product = dot(source[entry(lists, which, 3, j)], blocks[entry(lists, which, 0, j)])
             products.append((entry(lists, which, 4, j), product))
         for slot, product in products:
             acc[slot] += product
         return 0
 
     lax.fori_loop(0, groups[which], step, 0)
-
-
-def backward_own_kernel(lists, groups, blocks, own, acc):
+    sums = []
+    for first, part in ((0, same), (8, near)):
+        total = jnp.zeros((64, 256), F32)
+        for s in range(8):
+            total += dot(part[s, 128:192, :], source[first + s], (((1,), (1,)), ((), ())))
+        sums.append(total)
+    return sums[0] + sums[1]
+
+
+def backward_own_kernel(lists, groups, blocks, same, near, far, acc, grad, source):
     acc[...] = jnp.zeros_like(acc)
-    back_products(0, lists, groups, blocks, own, acc)
-
-
-def backward_other_kernel(lists, groups, blocks, own, other, begun, b0, b1, b2, b3, acc):
-    back_products(1, lists, groups, blocks, other, acc)
-    grad = jnp.zeros((64, 128), F32)
-    for s in range(16):
-        grad += own[s, 256:320, :].astype(F32) + other[s, 256:320, :].astype(F32)
-    high, low = split(grad)
+    grad[...] = back_products(0, lists, groups, blocks, same, near, far, source, acc)
+
+
+def backward_other_kernel(lists, groups, blocks, same, near, far, half, begun, b0, b1, b2, b3, acc, source):
+    grad = back_products(1, lists, groups, blocks, same, near, far, source, acc)
+    grad = (half[...] + grad).astype(BF)
     for x, out in enumerate((b0, b1, b2, b3)):
         for z in range(4):
             out[256 * z : 256 * z + 256, :] = acc[4 * x + z].astype(BF)
-        out[1024:1088, :] = high
-        out[1088:1152, :] = low
+        out[1024:1088, :] = grad[:, 0:128]
+        out[1088:1152, :] = grad[:, 128:256]
 
 
 def ordered_sum(me, parts, row, scratch):
     for k, part in enumerate(parts):
-        high, low = part[row : row + 64, :], part[row + 64 : row + 128, :]
-        scratch[(me - k) & 3] = high.astype(F32) + low.astype(F32)
+        scratch[(me - k) & 3] = part[row : row + 128, :].astype(F32)
     return scratch[0] + scratch[1] + scratch[2] + scratch[3]
 
 
 def fold_kernel(info, b0, b1, b2, b3, f0, f1, f2, f3, scratch):
     parts = (b0, b1, b2, b3)
-    high, low = split(ordered_sum(info[2], parts, 1024, scratch))
+    grad = ordered_sum(info[2], parts, 1024, scratch).astype(BF)
     for z, out in enumerate((f0, f1, f2, f3)):
         rows = slice(256 * z, 256 * z + 256)
         total = parts[0][rows, :].astype(F32)
         for part in parts[1:]:
             total += part[rows, :].astype(F32)
         out[0:256, :] = total.astype(BF)
-        out[256:320, :] = high
-        out[320:384, :] = low
+        out[256:384, :] = grad
 
 
 def grad_kernel(scale, info, f0, f1, f2, f3, grad_out, scratch):
     grad = (ordered_sum(info[3], (f0, f1, f2, f3), 256, scratch) * scale).astype(BF)
-    for s in range(8):
-        grad_out[s, :, 0:128] = grad[0:32]
-        grad_out[s, :, 128:256] = grad[32:64]
+    for s in range(4):
+        grad_out[s, :, 0:128] = grad[0:64]
+        grad_out[s, :, 128:256] = grad[64:128]
 
 
 def last_kernel(f0, f1, f2, f3, weight, input_grad):
@@ -182,13 +183,21 @@
     return lax.ppermute(value, "c", [(0, 1), (1, 0)])
 
 
+def near(value):
+    return lax.ppermute(value, "yl", [(0, 1), (1, 0)])
+
+
+def far(value):
+    return lax.ppermute(value, ("yh", "yl"), [(y, (y + 2 * (y % 2) - 1) % 8) for y in range(8)])
+
+
 def rotate(value, axis, k):
     return lax.ppermute(value, axis, [(i, (i + k) % 4) for i in range(4)])
 
 
 def shards(features, weight, cotangent, blocks, block_pos, counts):
     tile = blocks[0, 0]
-    index = [lax.axis_index(a).astype(jnp.int32) for a in ("c", "x", "zl")]
+    index = [lax.axis_index(a).astype(jnp.int32) for a in ("c", "x", "zl", "yl")]
     info = jnp.stack([counts[0, 0]] + index)
     nodes_total = 65536
     heavy = dict(flops=8 * 10**8, size=6 * 2**20)
@@ -213,51 +222,57 @@
         )(lists, groups, tile, nodes)[0]
         for which in (1, 0)
     ]
-    pair = (keep.astype(F32) + swap(send).astype(F32)).astype(BF)
-    parts = exchange(pair, ("zh", "y"))
+    pair = keep.astype(F32) + swap(send).astype(F32)
+    go = pair[8:].astype(BF)
+    came = jnp.concatenate([near(go[:, :, :128]), far(go[:, :, 128:])], axis=2)
+    parts = exchange((pair[:8] + came.astype(F32)).astype(BF), ("zh", "yh"))
     output, spread = call(
         middle_kernel,
-        [((128, 256), BF, VMEM), ((16, 320, 128), BF, VMEM)],
+        [((128, 256), BF, VMEM), ((8, 320, 128), BF, VMEM)],
         [VMEM, VMEM, VMEM],
     )(parts, weight, cotangent)
-    own = exchange(spread, ("zh", "y"))
-    other = swap(own)
-    (begun,) = call(
+    same = exchange(spread, ("zh", "yh"))
+    own = [same, near(same[:, :192]), far(same[:, 192:])]
+    other = [swap(part) for part in own]
+    source = pltpu.VMEM((16, 256, 128), BF)
+    begun, half = call(
         backward_own_kernel,
-        [((17, 256, 128), F32, VMEM)],
-        [SMEM, SMEM, VMEM, VMEM],
+        [((17, 256, 128), F32, VMEM), ((64, 256), F32, VMEM)],
+        [SMEM, SMEM] + [VMEM] * 4,
+        [source],
         **heavy,
-    )(lists, groups, tile, own)
+    )(lists, groups, tile, *own)
     back = call(
         backward_other_kernel,
         [((1152, 128), BF, VMEM)] * 4 + [((17, 256, 128), F32, VMEM)],
-        [SMEM, SMEM] + [VMEM] * 4,
-        alias={5: 4},
+        [SMEM, SMEM] + [VMEM] * 6,
+        [source],
+        alias={7: 4},
         **heavy,
-    )(lists, groups, tile, own, other, begun)
+    )(lists, groups, tile, *other, half, begun)
     back = [back[0]] + [rotate(back[k], "x", k) for k in (1, 2, 3)]
     folded = call(
         fold_kernel,
         [((384, 128), BF, VMEM)] * 4,
         [SMEM] + [VMEM] * 4,
-        [pltpu.VMEM((4, 64, 128), F32)],
+        [pltpu.VMEM((4, 128, 128), F32)],
     )(info, *back)
     folded = [folded[0]] + [rotate(folded[k], "zl", k) for k in (1, 2, 3)]
     (grad,) = call(
         functools.partial(grad_kernel, 1.0 / math.sqrt(nodes_total)),
-        [((8, 32, 256), BF, VMEM)],
+        [((4, 64, 256), BF, VMEM)],
         [SMEM] + [VMEM] * 4,
-        [pltpu.VMEM((4, 64, 128), F32)],
+        [pltpu.VMEM((4, 128, 128), F32)],
     )(info, *folded)
-    weight_grad = exchange(grad, "y").reshape(256, 256).astype(F32)
+    weight_grad = exchange(grad, "yh").reshape(256, 256).astype(F32)
     (input_grad,) = call(last_kernel, [((128, 256), BF, VMEM)], [VMEM] * 5, flops=2**24, size=2**20)(*folded, weight)
     return (output, input_grad, weight_grad)
 
 
 def solution(mesh):
-    names = ("zl", "x", "zh", "y", "c")
+    names = ("zl", "x", "zh", "yh", "yl", "c")
     row, col = names[:2], names[2:]
-    fine = Mesh(mesh.devices.reshape(4, 4, 2, 8, 2), names)
+    fine = Mesh(mesh.devices.reshape(4, 4, 2, 4, 2, 2), names)
     return jax.shard_map(
         shards,
         mesh=fine,

time: 190 us -> 196 us (1.032)
  blocking collectives: 99.5 us -> 76.5 us
  waiting for transfers between devices: 31.4 us -> 49.1 us
  starting transfers between devices: 33.4 us -> 48.9 us
  Pallas kernels: 19.8 us -> 15.2 us
    all_to_all x3, blocking collectives: 99.5 us -> 76.5 us  [exchange(): return lax.all_to_all(value, axes, 0, 0, tiled=True)]
    ppermute x0 -> x4, waiting for transfers between devices: none -> 14.2 us  [the longest x2 7.63 us: near(): return lax.ppermute(value, 'yl', [(0, 1), (1, 0)])]
    ppermute x0 -> x4, starting transfers between devices: none -> 13.2 us  [the longest x2 7.58 us: far(): lax.ppermute(value, ('yh', 'yl'), [(y, (y + 2 * (y % 2) - 1) % 8) for y i...]
    ppermute x2 -> x4, starting transfers between devices: 3.83 us -> 7.66 us  [swap(): return lax.ppermute(value, 'c', [(0, 1), (1, 0)])]
    pallas_call x2, Pallas kernels: 6.01 us -> 3.86 us  [shards(): call(functools.partial(forward_kernel, which), [((16, 128, 256), BF, VMEM...]
    ppermute x6, waiting for transfers between devices: 15.8 us -> 17.9 us  [rotate(): return lax.ppermute(value, axis, [(i, (i + k) % 4) for i in range(4)])]
  transfers between devices with their start and end apart: 10 -> 16, of which waited for: 7 -> 12; matrix products, arithmetic and copies ran while one was open for 0% -> 0% of each run, Pallas kernels for 6% -> 4%
where the time goes in v5:
time: 196 us; the launch traced here: 195 us
  blocking collectives  76.5 us (39%)
  waiting for transfers between devices  49.1 us (25%)
  starting transfers between devices  48.9 us (25%)
  Pallas kernels  15.2 us (8%)
  local copies, waits for them, and re-layouts  2.35 us (1%)
    all_to_all x3, blocking collectives, exchange(): return lax.all_to_all(value, axes, 0, 0, tiled=True)  76.5 us
    ppermute x6, starting transfers between devices, rotate(): return lax.ppermute(value, axis, [(i, (i + k) % 4) for i in range(4)])  19.3 us
    ppermute x6, waiting for transfers between devices, rotate(): return lax.ppermute(value, axis, [(i, (i + k) % 4) for i in range(4)])  17.9 us
    all_to_all x2, waiting for transfers between devices, exchange(): return lax.all_to_all(value, axes, 0, 0, tiled=True)  16.3 us
    all_to_all x2, starting transfers between devices, exchange(): return lax.all_to_all(value, axes, 0, 0, tiled=True)  8.79 us
    ppermute x4, starting transfers between devices, swap(): return lax.ppermute(value, 'c', [(0, 1), (1, 0)])  7.66 us
    ppermute x2, waiting for transfers between devices, near(): return lax.ppermute(value, 'yl', [(0, 1), (1, 0)])  7.63 us
    ppermute x2, starting transfers between devices, far(): lax.ppermute(value, ('yh', 'yl'), [(y, (y + 2 * (y % 2) - 1) % 8) for y i...  7.58 us
  transfers between devices with their start and end apart: 16, of which 12 were waited for; matrix products, arithmetic and copies ran while one was open for 0% of the time, Pallas kernels for 4%

profile of v5, /device:TPU:6, one launch (start us, length us, event | category | flops | bytes accessed | tf_op | source)
XLA Modules:
  0.0 194.8 jit_solution(18051913171088842256)
XLA Ops:
  0.6 0.0 copy-start
  0.7 1.0 broadcast_in_dim.4
  1.7 15.9 %all_to_all.25 = bf16[4,128,256]{2,1,0:T(8,128)(2,1)S(1)} all-to-all(bf16[4,128,256]{2,1,0:T(8,128)(2,1)S(1)} %broadcast_in_dim.4), channel_id=1, replica_groups=mesh['zl'=4,'x'=4,'zh'=2,'yh'=4,'yl'=2,'c'=2] {'zl'}, dimensions={0} | all-to-all | bytes 524288 | tf_op jit(solution)/shard_map/all_to_all | solution.py:179
  17.6 1.1 broadcast_in_dim.5
  18.7 4.8 %all-to-all-start.1 = ((bf16[4,4,128,256]{3,2,1,0:T(8,128)(2,1)}), bf16[4,4,128,256]{3,2,1,0:T(8,128)(2,1)}, u32[]{:S(2)}, u32[]{:S(2)}) async-start(bf16[4,4,128,256]{3,2,1,0:T(8,128)(2,1)} %broadcast_in_dim.5), calls=%async_computation.1 | async-start | bytes 2097152 | tf_op jit(solution)/shard_map/all_to_all | solution.py:179
  24.1 0.1 stack.19.info
  24.2 1.7 shard_map.85
  25.9 8.5 %all-to-all-done.1 = bf16[4,4,128,256]{3,2,1,0:T(8,128)(2,1)} async-done(((bf16[4,4,128,256]{3,2,1,0:T(8,128)(2,1)}), bf16[4,4,128,256]{3,2,1,0:T(8,128)(2,1)}, u32[]{:S(2)}, u32[]{:S(2)}) %all-to-all-start.1) | async-done | bytes 1048608 | tf_op jit(solution)/shard_map/all_to_all | solution.py:179
  34.3 1.9 shard_map.87
  36.2 1.9 collective-permute-start
  38.2 1.9 shard_map.86
  40.1 0.7 collective-permute-done
  40.8 0.4 fusion.1
  41.2 0.1 fusion.2
  41.4 3.7 %collective-permute-start.1 = (bf16[8,128,128]{2,1,0:T(8,128)(2,1)S(1)}, bf16[8,128,128]{2,1,0:T(8,128)(2,1)S(1)}, u32[]{:S(2)}, u32[]{:S(2)}) collective-permute-start(bf16[8,128,128]{2,1,0:T(8,128)(2,1)S(1)} %get-tuple-element.33), channel_id=1, source_target_pairs={{0,2},{2,0},{1,3},{3,1},{4,6},{6,4},{5,7},{7,5},{8,10},{10,8},{9,1... | collective-permute-start | bytes 786440 | tf_op jit(solution)/shard_map/ppermute | solution.py:187
  45.0 5.6 %collective-permute-start.2 = (bf16[8,128,128]{2,1,0:T(8,128)(2,1)S(1)}, bf16[8,128,128]{2,1,0:T(8,128)(2,1)S(1)}, u32[]{:S(2)}, u32[]{:S(2)}) collective-permute-start(bf16[8,128,128]{2,1,0:T(8,128)(2,1)S(1)} %get-tuple-element.34), channel_id=1, source_target_pairs={{0,14},{2,4},{4,2},{6,8},{8,6},{10,12},{12,10},{14,0},{1,15},{3,5}... | collective-permute-start | bytes 786440 | tf_op jit(solution)/shard_map/ppermute | solution.py:191
  50.6 1.1 collective-permute-done.1
  51.8 5.2 %collective-permute-done.2 = bf16[8,128,128]{2,1,0:T(8,128)(2,1)S(1)} collective-permute-done((bf16[8,128,128]{2,1,0:T(8,128)(2,1)S(1)}, bf16[8,128,128]{2,1,0:T(8,128)(2,1)S(1)}, u32[]{:S(2)}, u32[]{:S(2)}) %collective-permute-start.2) | collective-permute-done | bytes 262176 | tf_op jit(solution)/shard_map/ppermute | solution.py:191
  57.0 0.2 fusion
  57.1 33.3 %all_to_all.26.parts = bf16[8,128,256]{2,1,0:T(8,128)(2,1)S(1)} all-to-all(bf16[8,128,256]{2,1,0:T(8,128)(2,1)S(1)} %fusion), channel_id=1, replica_groups=mesh['zl'=4,'x'=4,'zh'=2,'yh'=4,'yl'=2,'c'=2] {'zh','yh'}, dimensions={0} | all-to-all | bytes 1048576 | tf_op jit(solution)/shard_map/all_to_all | solution.py:179
  90.5 0.9 shard_map.88
  91.3 27.2 %all_to_all.27.same = bf16[8,320,128]{2,1,0:T(8,128)(2,1)S(1)} all-to-all(bf16[8,320,128]{2,1,0:T(8,128)(2,1)S(1)} %get-tuple-element.20), channel_id=1, replica_groups=mesh['zl'=4,'x'=4,'zh'=2,'yh'=4,'yl'=2,'c'=2] {'zh','yh'}, dimensions={0} | all-to-all | bytes 1310720 | tf_op jit(solution)/shard_map/all_to_all | solution.py:179
  118.5 1.9 collective-permute-start.4
  120.5 1.9 collective-permute-start.3
  122.4 2.0 %collective-permute-start.6 = (bf16[8,128,128]{2,1,0:T(8,128)(2,1)S(1)}, bf16[8,128,128]{2,1,0:T(8,128)(2,1)S(1)}, u32[]{:S(2)}, u32[]{:S(2)}) collective-permute-start(bf16[8,128,128]{2,1,0:T(8,128)(2,1)S(1)} %slice.28), channel_id=1, source_target_pairs={{0,14},{2,4},{4,2},{6,8},{8,6},{10,12},{12,10},{14,0},{1,15},{3,5}... | collective-permute-start | bytes 786440 | tf_op jit(solution)/shard_map/ppermute | solution.py:191
  124.4 6.5 %collective-permute-done.4.near = bf16[8,192,128]{2,1,0:T(8,128)(2,1)S(1)} collective-permute-done((bf16[8,192,128]{2,1,0:T(8,128)(2,1)S(1)}, bf16[8,192,128]{2,1,0:T(8,128)(2,1)S(1)}, u32[]{:S(2)}, u32[]{:S(2)}) %collective-permute-start.4) | collective-permute-done | bytes 393248 | tf_op jit(solution)/shard_map/ppermute | solution.py:187
  130.9 1.9 collective-permute-start.5
  132.8 1.4 collective-permute-done.6.far
  134.2 1.9 collective-permute-start.7
  136.1 3.0 %shard_map.89 = (f32[17,256,128]{2,1,0:T(8,128)S(1)}, f32[64,256]{1,0:T(8,128)S(1)}) custom-call(s32[1120]{0:T(1024)S(1)} %get-tuple-element.17.lists, s32[2]{0:T(128)S(1)} %get-tuple-element.18.groups, bf16[96,128,128]{2,1,0:T(8,128)(2,1)} %bitcast.12, bf16[8,320,128]{2,1,0:T(8,128)(2,1)S(1)} %all_to_all.27.same, ...), custom_call_target="tpu_custom_call" | custom-call | flops 800000000 | bytes 6291456 | tf_op jit(solution)/shard_map/pallas_call | solution.py:238
  139.2 2.9 %shard_map.90 = (bf16[1152,128]{1,0:T(8,128)(2,1)S(1)}, bf16[1152,128]{1,0:T(8,128)(2,1)S(1)}, bf16[1152,128]{1,0:T(8,128)(2,1)S(1)}, bf16[1152,128]{1,0:T(8,128)(2,1)S(1)}, f32[17,256,128]{2,1,0:T(8,128)S(1)}) custom-call(s32[1120]{0:T(1024)S(1)} %get-tuple-element.17.lists, s32[2]{0:T(128)S(1)} %get-tuple-element.18.groups, ...), custom_call_target="tpu_custom_call", output_to_operand_aliasing={{4}: (7, {})} | custom-call | flops 800000000 | bytes 6291456 | tf_op jit(solution)/shard_map/pallas_call | solution.py:245
  142.1 1.9 collective-permute-start.8
  144.1 3.4 %collective-permute-start.9 = (bf16[1152,128]{1,0:T(8,128)(2,1)S(1)}, bf16[1152,128]{1,0:T(8,128)(2,1)S(1)}, u32[]{:S(2)}, u32[]{:S(2)}) collective-permute-start(bf16[1152,128]{1,0:T(8,128)(2,1)S(1)} %get-tuple-element.25), channel_id=1, source_target_pairs={{0,64},{32,96},{64,0},{96,32},{1,65},{33,97},{65,1},{97,33},{2,66}... | collective-permute-start | bytes 884744 | tf_op jit(solution)/shard_map/ppermute | solution.py:195
  147.5 3.3 %collective-permute-start.10 = (bf16[1152,128]{1,0:T(8,128)(2,1)S(1)}, bf16[1152,128]{1,0:T(8,128)(2,1)S(1)}, u32[]{:S(2)}, u32[]{:S(2)}) collective-permute-start(bf16[1152,128]{1,0:T(8,128)(2,1)S(1)} %get-tuple-element.26), channel_id=1, source_target_pairs={{0,96},{32,0},{64,32},{96,64},{1,97},{33,1},{65,33},{97,65},{2,98}... | collective-permute-start | bytes 884744 | tf_op jit(solution)/shard_map/ppermute | solution.py:195
  150.8 2.8 %collective-permute-done.8.b1 = bf16[1152,128]{1,0:T(8,128)(2,1)S(1)} collective-permute-done((bf16[1152,128]{1,0:T(8,128)(2,1)S(1)}, bf16[1152,128]{1,0:T(8,128)(2,1)S(1)}, u32[]{:S(2)}, u32[]{:S(2)}) %collective-permute-start.8) | collective-permute-done | bytes 294944 | tf_op jit(solution)/shard_map/ppermute | solution.py:195
  153.6 3.5 %collective-permute-done.9.b2 = bf16[1152,128]{1,0:T(8,128)(2,1)S(1)} collective-permute-done((bf16[1152,128]{1,0:T(8,128)(2,1)S(1)}, bf16[1152,128]{1,0:T(8,128)(2,1)S(1)}, u32[]{:S(2)}, u32[]{:S(2)}) %collective-permute-start.9) | collective-permute-done | bytes 294944 | tf_op jit(solution)/shard_map/ppermute | solution.py:195
  157.1 6.5 %collective-permute-done.10.b3 = bf16[1152,128]{1,0:T(8,128)(2,1)S(1)} collective-permute-done((bf16[1152,128]{1,0:T(8,128)(2,1)S(1)}, bf16[1152,128]{1,0:T(8,128)(2,1)S(1)}, u32[]{:S(2)}, u32[]{:S(2)}) %collective-permute-start.10) | collective-permute-done | bytes 294944 | tf_op jit(solution)/shard_map/ppermute | solution.py:195
  163.7 0.7 shard_map.91
  164.4 4.5 %collective-permute-start.11 = (bf16[384,128]{1,0:T(8,128)(2,1)S(1)}, bf16[384,128]{1,0:T(8,128)(2,1)S(1)}, u32[]{:S(2)}, u32[]{:S(2)}) collective-permute-start(bf16[384,128]{1,0:T(8,128)(2,1)S(1)} %get-tuple-element.28), channel_id=1, source_target_pairs={{0,128},{128,256},{256,384},{384,0},{1,129},{129,257},{257,385},{3... | collective-permute-start | bytes 294920 | tf_op jit(solution)/shard_map/ppermute | solution.py:195
  168.9 3.2 %collective-permute-start.12 = (bf16[384,128]{1,0:T(8,128)(2,1)S(1)}, bf16[384,128]{1,0:T(8,128)(2,1)S(1)}, u32[]{:S(2)}, u32[]{:S(2)}) collective-permute-start(bf16[384,128]{1,0:T(8,128)(2,1)S(1)} %get-tuple-element.29), channel_id=1, source_target_pairs={{0,256},{128,384},{256,0},{384,128},{1,257},{129,385},{257,1},{385... | collective-permute-start | bytes 294920 | tf_op jit(solution)/shard_map/ppermute | solution.py:195
  172.1 3.0 %collective-permute-start.13 = (bf16[384,128]{1,0:T(8,128)(2,1)S(1)}, bf16[384,128]{1,0:T(8,128)(2,1)S(1)}, u32[]{:S(2)}, u32[]{:S(2)}) collective-permute-start(bf16[384,128]{1,0:T(8,128)(2,1)S(1)} %get-tuple-element.30), channel_id=1, source_target_pairs={{0,384},{128,0},{256,128},{384,256},{1,385},{129,1},{257,129},{385... | collective-permute-start | bytes 294920 | tf_op jit(solution)/shard_map/ppermute | solution.py:195
  175.1 3.0 %collective-permute-done.12.f2 = bf16[384,128]{1,0:T(8,128)(2,1)S(1)} collective-permute-done((bf16[384,128]{1,0:T(8,128)(2,1)S(1)}, bf16[384,128]{1,0:T(8,128)(2,1)S(1)}, u32[]{:S(2)}, u32[]{:S(2)}) %collective-permute-start.12) | collective-permute-done | bytes 98336 | tf_op jit(solution)/shard_map/ppermute | solution.py:195
  178.1 2.0 %collective-permute-done.13.f3 = bf16[384,128]{1,0:T(8,128)(2,1)S(1)} collective-permute-done((bf16[384,128]{1,0:T(8,128)(2,1)S(1)}, bf16[384,128]{1,0:T(8,128)(2,1)S(1)}, u32[]{:S(2)}, u32[]{:S(2)}) %collective-permute-start.13) | collective-permute-done | bytes 98336 | tf_op jit(solution)/shard_map/ppermute | solution.py:195
  180.1 1.2 shard_map.93
  181.3 4.0 %all-to-all-start.4 = ((bf16[4,64,256]{2,1,0:T(8,128)(2,1)}), bf16[4,64,256]{2,1,0:T(8,128)(2,1)S(1)}, u32[]{:S(2)}, u32[]{:S(2)}) async-start(bf16[4,64,256]{2,1,0:T(8,128)(2,1)} %shard_map.93), calls=%async_computation.4 | async-start | bytes 262144 | tf_op jit(solution)/shard_map/all_to_all | solution.py:179
  185.4 0.9 shard_map.92
  186.2 7.9 %all-to-all-done.4 = bf16[4,64,256]{2,1,0:T(8,128)(2,1)S(1)} async-done(((bf16[4,64,256]{2,1,0:T(8,128)(2,1)}), bf16[4,64,256]{2,1,0:T(8,128)(2,1)S(1)}, u32[]{:S(2)}, u32[]{:S(2)}) %all-to-all-start.4) | async-done | bytes 131104 | tf_op jit(solution)/shard_map/all_to_all | solution.py:179
  194.1 0.7 bitcast_convert_fusion
  (13 shorter events, 0.1 us)
Async XLA Ops:
  0.6 23.5 %copy-start.3 = (s32[1,1,96]{2,1,0:T(1,128)S(1)}, s32[1,1,96]{2,1,0:T(1,128)}, u32[]{:S(2)}) copy-start(s32[1,1,96]{2,1,0:T(1,128)} %param.10) | copy-start | bytes 1156
  0.6 23.5 %copy-start = (bf16[1,1,96,128,128]{4,3,2,1,0:T(8,128)(2,1)S(1)}, bf16[1,1,96,128,128]{4,3,2,1,0:T(8,128)(2,1)}, u32[]{:S(2)}) copy-start(bf16[1,1,96,128,128]{4,3,2,1,0:T(8,128)(2,1)} %param.9) | copy-start | bytes 9437188
  18.7 15.7 %all-to-all-start.1 = ((bf16[4,4,128,256]{3,2,1,0:T(8,128)(2,1)}), bf16[4,4,128,256]{3,2,1,0:T(8,128)(2,1)}, u32[]{:S(2)}, u32[]{:S(2)}) async-start(bf16[4,4,128,256]{3,2,1,0:T(8,128)(2,1)} %broadcast_in_dim.5), calls=%async_computation.1 | async-start | bytes 2097152 | tf_op jit(solution)/shard_map/all_to_all | solution.py:179
  36.2 4.6 %collective-permute-start = (bf16[16,128,256]{2,1,0:T(8,128)(2,1)S(1)}, bf16[16,128,256]{2,1,0:T(8,128)(2,1)S(1)}, u32[]{:S(2)}, u32[]{:S(2)}) collective-permute-start(bf16[16,128,256]{2,1,0:T(8,128)(2,1)S(1)} %shard_map.87), channel_id=1, source_target_pairs={{0,1},{1,0},{2,3},{3,2},{4,5},{5,4},{6,7},{7,6},{8,9},{9,8},{10,11... | collective-permute-start | bytes 3145736 | tf_op jit(solution)/shard_map/ppermute | solution.py:183
  41.2 49.3 %copy-start.1 = (bf16[256,256]{1,0:T(8,128)(2,1)S(1)}, bf16[256,256]{1,0:T(8,128)(2,1)}, u32[]{:S(2)}) copy-start(bf16[256,256]{1,0:T(8,128)(2,1)} %weight.3) | copy-start | bytes 393220
  41.2 49.2 %copy-start.2 = (bf16[128,256]{1,0:T(8,128)(2,1)S(1)}, bf16[128,256]{1,0:T(8,128)(2,1)}, u32[]{:S(2)}) copy-start(bf16[128,256]{1,0:T(8,128)(2,1)} %cotangent.1) | copy-start | bytes 196612
  41.4 10.4 %collective-permute-start.1 = (bf16[8,128,128]{2,1,0:T(8,128)(2,1)S(1)}, bf16[8,128,128]{2,1,0:T(8,128)(2,1)S(1)}, u32[]{:S(2)}, u32[]{:S(2)}) collective-permute-start(bf16[8,128,128]{2,1,0:T(8,128)(2,1)S(1)} %get-tuple-element.33), channel_id=1, source_target_pairs={{0,2},{2,0},{1,3},{3,1},{4,6},{6,4},{5,7},{7,5},{8,10},{10,8},{9,1... | collective-permute-start | bytes 786440 | tf_op jit(solution)/shard_map/ppermute | solution.py:187
  45.0 11.9 %collective-permute-start.2 = (bf16[8,128,128]{2,1,0:T(8,128)(2,1)S(1)}, bf16[8,128,128]{2,1,0:T(8,128)(2,1)S(1)}, u32[]{:S(2)}, u32[]{:S(2)}) collective-permute-start(bf16[8,128,128]{2,1,0:T(8,128)(2,1)S(1)} %get-tuple-element.34), channel_id=1, source_target_pairs={{0,14},{2,4},{4,2},{6,8},{8,6},{10,12},{12,10},{14,0},{1,15},{3,5}... | collective-permute-start | bytes 786440 | tf_op jit(solution)/shard_map/ppermute | solution.py:191
  118.5 12.4 %collective-permute-start.4 = (bf16[8,192,128]{2,1,0:T(8,128)(2,1)S(1)}, bf16[8,192,128]{2,1,0:T(8,128)(2,1)S(1)}, u32[]{:S(2)}, u32[]{:S(2)}) collective-permute-start(bf16[8,192,128]{2,1,0:T(8,128)(2,1)S(1)} %slice.27), channel_id=1, source_target_pairs={{0,2},{2,0},{1,3},{3,1},{4,6},{6,4},{5,7},{7,5},{8,10},{10,8},{9,1... | collective-permute-start | bytes 1179656 | tf_op jit(solution)/shard_map/ppermute | solution.py:187
  120.5 18.7 %collective-permute-start.3 = (bf16[8,320,128]{2,1,0:T(8,128)(2,1)S(1)}, bf16[8,320,128]{2,1,0:T(8,128)(2,1)S(1)}, u32[]{:S(2)}, u32[]{:S(2)}) collective-permute-start(bf16[8,320,128]{2,1,0:T(8,128)(2,1)S(1)} %all_to_all.27.same), channel_id=1, source_target_pairs={{0,1},{1,0},{2,3},{3,2},{4,5},{5,4},{6,7},{7,6},{8,9},{9,8},{10,11... | collective-permute-start | bytes 1966088 | tf_op jit(solution)/shard_map/ppermute | solution.py:183
  122.4 11.8 %collective-permute-start.6 = (bf16[8,128,128]{2,1,0:T(8,128)(2,1)S(1)}, bf16[8,128,128]{2,1,0:T(8,128)(2,1)S(1)}, u32[]{:S(2)}, u32[]{:S(2)}) collective-permute-start(bf16[8,128,128]{2,1,0:T(8,128)(2,1)S(1)} %slice.28), channel_id=1, source_target_pairs={{0,14},{2,4},{4,2},{6,8},{8,6},{10,12},{12,10},{14,0},{1,15},{3,5}... | collective-permute-start | bytes 786440 | tf_op jit(solution)/shard_map/ppermute | solution.py:191
  130.9 8.3 %collective-permute-start.5 = (bf16[8,192,128]{2,1,0:T(8,128)(2,1)S(1)}, bf16[8,192,128]{2,1,0:T(8,128)(2,1)S(1)}, u32[]{:S(2)}, u32[]{:S(2)}) collective-permute-start(bf16[8,192,128]{2,1,0:T(8,128)(2,1)S(1)} %collective-permute-done.4.near), channel_id=1, source_target_pairs={{0,1},{1,0},{2,3},{3,2},{4,5},{5,4},{6,7},{7,6},{8,9},{9,8},{10,11... | collective-permute-start | bytes 1179656 | tf_op jit(solution)/shard_map/ppermute | solution.py:183
  134.2 5.0 %collective-permute-start.7 = (bf16[8,128,128]{2,1,0:T(8,128)(2,1)S(1)}, bf16[8,128,128]{2,1,0:T(8,128)(2,1)S(1)}, u32[]{:S(2)}, u32[]{:S(2)}) collective-permute-start(bf16[8,128,128]{2,1,0:T(8,128)(2,1)S(1)} %collective-permute-done.6.far), channel_id=1, source_target_pairs={{0,1},{1,0},{2,3},{3,2},{4,5},{5,4},{6,7},{7,6},{8,9},{9,8},{10,11... | collective-permute-start | bytes 786440 | tf_op jit(solution)/shard_map/ppermute | solution.py:183
  142.1 11.5 %collective-permute-start.8 = (bf16[1152,128]{1,0:T(8,128)(2,1)S(1)}, bf16[1152,128]{1,0:T(8,128)(2,1)S(1)}, u32[]{:S(2)}, u32[]{:S(2)}) collective-permute-start(bf16[1152,128]{1,0:T(8,128)(2,1)S(1)} %get-tuple-element.24), channel_id=1, source_target_pairs={{0,32},{32,64},{64,96},{96,0},{1,33},{33,65},{65,97},{97,1},{2,34}... | collective-permute-start | bytes 884744 | tf_op jit(solution)/shard_map/ppermute | solution.py:195
  144.1 13.1 %collective-permute-start.9 = (bf16[1152,128]{1,0:T(8,128)(2,1)S(1)}, bf16[1152,128]{1,0:T(8,128)(2,1)S(1)}, u32[]{:S(2)}, u32[]{:S(2)}) collective-permute-start(bf16[1152,128]{1,0:T(8,128)(2,1)S(1)} %get-tuple-element.25), channel_id=1, source_target_pairs={{0,64},{32,96},{64,0},{96,32},{1,65},{33,97},{65,1},{97,33},{2,66}... | collective-permute-start | bytes 884744 | tf_op jit(solution)/shard_map/ppermute | solution.py:195
  147.5 16.2 %collective-permute-start.10 = (bf16[1152,128]{1,0:T(8,128)(2,1)S(1)}, bf16[1152,128]{1,0:T(8,128)(2,1)S(1)}, u32[]{:S(2)}, u32[]{:S(2)}) collective-permute-start(bf16[1152,128]{1,0:T(8,128)(2,1)S(1)} %get-tuple-element.26), channel_id=1, source_target_pairs={{0,96},{32,0},{64,32},{96,64},{1,97},{33,1},{65,33},{97,65},{2,98}... | collective-permute-start | bytes 884744 | tf_op jit(solution)/shard_map/ppermute | solution.py:195
  164.4 10.7 %collective-permute-start.11 = (bf16[384,128]{1,0:T(8,128)(2,1)S(1)}, bf16[384,128]{1,0:T(8,128)(2,1)S(1)}, u32[]{:S(2)}, u32[]{:S(2)}) collective-permute-start(bf16[384,128]{1,0:T(8,128)(2,1)S(1)} %get-tuple-element.28), channel_id=1, source_target_pairs={{0,128},{128,256},{256,384},{384,0},{1,129},{129,257},{257,385},{3... | collective-permute-start | bytes 294920 | tf_op jit(solution)/shard_map/ppermute | solution.py:195
  168.9 9.2 %collective-permute-start.12 = (bf16[384,128]{1,0:T(8,128)(2,1)S(1)}, bf16[384,128]{1,0:T(8,128)(2,1)S(1)}, u32[]{:S(2)}, u32[]{:S(2)}) collective-permute-start(bf16[384,128]{1,0:T(8,128)(2,1)S(1)} %get-tuple-element.29), channel_id=1, source_target_pairs={{0,256},{128,384},{256,0},{384,128},{1,257},{129,385},{257,1},{385... | collective-permute-start | bytes 294920 | tf_op jit(solution)/shard_map/ppermute | solution.py:195
  172.1 8.0 %collective-permute-start.13 = (bf16[384,128]{1,0:T(8,128)(2,1)S(1)}, bf16[384,128]{1,0:T(8,128)(2,1)S(1)}, u32[]{:S(2)}, u32[]{:S(2)}) collective-permute-start(bf16[384,128]{1,0:T(8,128)(2,1)S(1)} %get-tuple-element.30), channel_id=1, source_target_pairs={{0,384},{128,0},{256,128},{384,256},{1,385},{129,1},{257,129},{385... | collective-permute-start | bytes 294920 | tf_op jit(solution)/shard_map/ppermute | solution.py:195
  181.3 12.8 %all-to-all-start.4 = ((bf16[4,64,256]{2,1,0:T(8,128)(2,1)}), bf16[4,64,256]{2,1,0:T(8,128)(2,1)S(1)}, u32[]{:S(2)}, u32[]{:S(2)}) async-start(bf16[4,64,256]{2,1,0:T(8,128)(2,1)} %shard_map.93), calls=%async_computation.4 | async-start | bytes 262144 | tf_op jit(solution)/shard_map/all_to_all | solution.py:179

commit v6 on v4

--- a/solution.py
+++ b/solution.py
@@ -23,7 +23,7 @@
 
 
 def plan_kernel(place, info, blocks, lists, groups):
-    count, core, xi, zi = info[0], info[1], info[2], info[3]
+    count, core = info[0], info[1]
 
     def write(at, k, t, source, half, target):
         for f, value in enumerate((k, t, source, half, target)):
@@ -35,7 +35,7 @@
         z, x = a >> 2, a & 3
         half = t >> 1
         source = (x << 2) + z
-        target = (((x - xi) & 3) << 2) + ((z - zi) & 3)
+        target = a
         mine, theirs = held
         away = (t & 1) ^ core
         write(jnp.where(away == 0, mine, SLOTS + theirs), k, half, source, half, target)
@@ -69,7 +69,7 @@
     out[...] = acc[0:16].astype(BF)
 
 
-def middle_kernel(parts, weight, cotangent, output, spread):
+def middle_kernel(info, parts, weight, cotangent, output, spread, stay, go, grad):
     total = parts[0].astype(F32)
     for s in range(1, 16):
         total += parts[s].astype(F32)
@@ -78,20 +78,31 @@
     sigma = 1.0 / (1.0 + jnp.exp(-pre))
     output[...] = (pre * sigma).astype(BF)
     slope = sigma * (1.0 + pre * (1.0 - sigma))
-    slopes32 = cotangent[...].astype(F32) * slope
-    slopes = slopes32.astype(BF)
+    slopes = (cotangent[...].astype(F32) * slope).astype(BF)
     turned = slopes.astype(F32).T.astype(BF)
-    grad = dot(share.astype(F32).T.astype(BF), slopes).astype(BF)
     for s in range(16):
-        spread[s, 0:256, :] = turned
-        rows = slice(32 * (s % 8), 32 * (s % 8) + 32)
-        spread[s, 256:288, :] = grad[rows, 0:128]
-        spread[s, 288:320, :] = grad[rows, 128:256]
-
-
-def split(value):
-    high = value.astype(BF)
-    return high, (value - high.astype(F32)).astype(BF)
+        spread[s] = turned
+    grad[...] = dot(share.astype(F32).T.astype(BF), slopes).reshape(2, 128, 256)
+    stay[...] = grad[info[1]]
+    go[...] = grad[1 - info[1]]
+
+
+def scatter_kernel(me, count, info, *refs):
+    parts, outs, scratch = refs[:count], refs[count:-1], refs[-1]
+    total = parts[0][...]
+    for part in parts[1:]:
+        total += part[...]
+    rows = total.shape[0] // 4
+    for k in range(4):
+        scratch[k] = total[rows * k : rows * k + rows]
+    for k, out in enumerate(outs):
+        out[...] = scratch[(info[me] + k) & 3]
+
+
+def offer_kernel(w0, w1, w2, w3, own, out, held):
+    total = w0[...] + w1[...] + w2[...] + w3[...]
+    for s in range(16):
+        out[s] = total
 
 
 def back_products(which, lists, groups, blocks, source, acc):
@@ -99,7 +110,7 @@
         products = []
         for g in range(GROUP):
             j = i * GROUP + g
-            product = dot(source[entry(lists, which, 3, j), 0:256, :], blocks[entry(lists, which, 0, j)])
+            product = dot(source[entry(lists, which, 3, j)], blocks[entry(lists, which, 0, j)])
             products.append((entry(lists, which, 4, j), product))
         for slot, product in products:
             acc[slot] += product
@@ -113,52 +124,38 @@
     back_products(0, lists, groups, blocks, own, acc)
 
 
-def backward_other_kernel(lists, groups, blocks, own, other, begun, b0, b1, b2, b3, acc):
+def backward_other_kernel(scale, lists, groups, blocks, other, grads, begun, out, acc):
     back_products(1, lists, groups, blocks, other, acc)
-    grad = jnp.zeros((64, 128), F32)
+    grad = grads[0]
+    for s in range(1, 16):
+        grad += grads[s]
+    grad = grad * scale
+    packed = jnp.concatenate([grad[:, 0:128], grad[:, 128:256]], axis=0).astype(BF)
     for s in range(16):
-        grad += own[s, 256:320, :].astype(F32) + other[s, 256:320, :].astype(F32)
-    high, low = split(grad)
-    for x, out in enumerate((b0, b1, b2, b3)):
-        for z in range(4):
-            out[256 * z : 256 * z + 256, :] = acc[4 * x + z].astype(BF)
-        out[1024:1088, :] = high
-        out[1088:1152, :] = low
-
-
-def ordered_sum(me, parts, row, scratch):
-    for k, part in enumerate(parts):
-        high, low = part[row : row + 64, :], part[row + 64 : row + 128, :]
-        scratch[(me - k) & 3] = high.astype(F32) + low.astype(F32)
-    return scratch[0] + scratch[1] + scratch[2] + scratch[3]
-
-
-def fold_kernel(info, b0, b1, b2, b3, f0, f1, f2, f3, scratch):
-    parts = (b0, b1, b2, b3)
-    high, low = split(ordered_sum(info[2], parts, 1024, scratch))
-    for z, out in enumerate((f0, f1, f2, f3)):
-        rows = slice(256 * z, 256 * z + 256)
-        total = parts[0][rows, :].astype(F32)
-        for part in parts[1:]:
-            total += part[rows, :].astype(F32)
-        out[0:256, :] = total.astype(BF)
-        out[256:320, :] = high
-        out[320:384, :] = low
-
-
-def grad_kernel(scale, info, f0, f1, f2, f3, grad_out, scratch):
-    grad = (ordered_sum(info[3], (f0, f1, f2, f3), 256, scratch) * scale).astype(BF)
-    for s in range(8):
-        grad_out[s, :, 0:128] = grad[0:32]
-        grad_out[s, :, 128:256] = grad[32:64]
-
-
-def last_kernel(f0, f1, f2, f3, weight, input_grad):
-    total = f0[0:256, :].astype(F32)
-    for part in (f1, f2, f3):
-        total += part[0:256, :].astype(F32)
+        out[s, 0:256, :] = acc[s].astype(BF)
+        out[s, 256:272, :] = packed
+
+
+def grad_kernel(parts, out):
+    for z in range(4):
+        for x in range(4):
+            packed = parts[4 * z + x, 256:272, :].astype(F32)
+            row = 32 * x + 8 * z
+            out[row : row + 8, 0:128] = packed[0:8]
+            out[row : row + 8, 128:256] = packed[8:16]
+
+
+def last_kernel(parts, weight, input_grad):
+    total = parts[0, 0:256, :].astype(F32)
+    for s in range(1, 16):
+        total += parts[s, 0:256, :].astype(F32)
     back = total.astype(BF).astype(F32).T.astype(BF)
     input_grad[...] = dot(back, weight[...], (((1,), (1,)), ((), ()))).astype(BF)
+
+
+def join_kernel(info, mine, theirs, out):
+    out[info[1]] = mine[...]
+    out[1 - info[1]] = theirs[...]
 
 
 def call(kernel, outs, kinds, scratch=(), flops=0, size=0, alias=None):
@@ -193,6 +190,7 @@
     nodes_total = 65536
     heavy = dict(flops=8 * 10**8, size=6 * 2**20)
     i32 = jnp.int32
+    rounds = (1, 2, 3)
 
     lists, groups = call(
         plan_kernel,
@@ -215,12 +213,32 @@
     ]
     pair = (keep.astype(F32) + swap(send).astype(F32)).astype(BF)
     parts = exchange(pair, ("zh", "y"))
-    output, spread = call(
+    output, spread, stay, go = call(
         middle_kernel,
-        [((128, 256), BF, VMEM), ((16, 320, 128), BF, VMEM)],
-        [VMEM, VMEM, VMEM],
-    )(parts, weight, cotangent)
+        [((128, 256), BF, VMEM), ((16, 256, 128), BF, VMEM)] + [((128, 256), F32, VMEM)] * 2,
+        [SMEM, VMEM, VMEM, VMEM],
+        [pltpu.VMEM((2, 128, 256), F32)],
+    )(info, parts, weight, cotangent)
     own = exchange(spread, ("zh", "y"))
+
+    def scatter(me, rows, held):
+        return call(
+            functools.partial(scatter_kernel, me, len(held)),
+            [((rows, 256), F32, VMEM)] * 4,
+            [SMEM] + [VMEM] * len(held),
+            [pltpu.VMEM((4, rows, 256), F32)],
+        )(info, *held)
+
+    held = scatter(2, 32, [stay, swap(go)])
+    held = scatter(3, 8, [held[0]] + [rotate(held[k], "x", k) for k in rounds])
+    held = [held[0]] + [rotate(held[k], "zl", k) for k in rounds]
+    offer, own = call(
+        offer_kernel,
+        [((16, 8, 256), F32, VMEM), ((16, 256, 128), BF, VMEM)],
+        [VMEM] * 5,
+        alias={4: 1},
+    )(*held, own)
+    grads = exchange(offer, ("zh", "y"))
     other = swap(own)
     (begun,) = call(
         backward_own_kernel,
@@ -228,29 +246,19 @@
         [SMEM, SMEM, VMEM, VMEM],
         **heavy,
     )(lists, groups, tile, own)
-    back = call(
-        backward_other_kernel,
-        [((1152, 128), BF, VMEM)] * 4 + [((17, 256, 128), F32, VMEM)],
+    back, _ = call(
+        functools.partial(backward_other_kernel, 1.0 / math.sqrt(nodes_total)),
+        [((16, 272, 128), BF, VMEM), ((17, 256, 128), F32, VMEM)],
         [SMEM, SMEM] + [VMEM] * 4,
-        alias={5: 4},
+        alias={5: 1},
         **heavy,
-    )(lists, groups, tile, own, other, begun)
-    back = [back[0]] + [rotate(back[k], "x", k) for k in (1, 2, 3)]
-    folded = call(
-        fold_kernel,
-        [((384, 128), BF, VMEM)] * 4,
-        [SMEM] + [VMEM] * 4,
-        [pltpu.VMEM((4, 64, 128), F32)],
-    )(info, *back)
-    folded = [folded[0]] + [rotate(folded[k], "zl", k) for k in (1, 2, 3)]
-    (grad,) = call(
-        functools.partial(grad_kernel, 1.0 / math.sqrt(nodes_total)),
-        [((8, 32, 256), BF, VMEM)],
-        [SMEM] + [VMEM] * 4,
-        [pltpu.VMEM((4, 64, 128), F32)],
-    )(info, *folded)
-    weight_grad = exchange(grad, "y").reshape(256, 256).astype(F32)
-    (input_grad,) = call(last_kernel, [((128, 256), BF, VMEM)], [VMEM] * 5, flops=2**24, size=2**20)(*folded, weight)
+    )(lists, groups, tile, other, grads, begun)
+    parts = exchange(back, ("zl", "x"))
+    (mine,) = call(grad_kernel, [((128, 256), F32, VMEM)], [VMEM])(parts)
+    theirs = swap(mine)
+    (input_grad,) = call(last_kernel, [((128, 256), BF, VMEM)], [VMEM] * 2, flops=2**24, size=2**20)(parts, weight)
+    (weight_grad,) = call(join_kernel, [((2, 128, 256), F32, VMEM)], [SMEM, VMEM, VMEM])(info, mine, theirs)
+    weight_grad = weight_grad.reshape(256, 256)
     return (output, input_grad, weight_grad)
 
 

time: 190 us -> 195 us (1.026); the launches traced: 189 us -> 191 us
  starting transfers between devices: 33.4 us -> 47.2 us
  blocking collectives: 99.5 us -> 94.8 us
  waiting for transfers between devices: 31.4 us -> 28.2 us
  Pallas kernels: 19.8 us -> 16.9 us
    ppermute x6, waiting for transfers between devices: 15.8 us -> 5.78 us  [rotate(): return lax.ppermute(value, axis, [(i, (i + k) % 4) for i in range(4)])]
    all_to_all x2 -> x3, starting transfers between devices: 10.1 us -> 20 us  [exchange(): return lax.all_to_all(value, axes, 0, 0, tiled=True)]
    all_to_all x3, blocking collectives: 99.5 us -> 94.8 us  [exchange(): return lax.all_to_all(value, axes, 0, 0, tiled=True)]
    all_to_all x2 -> x3, waiting for transfers between devices: 15.5 us -> 20 us  [exchange(): return lax.all_to_all(value, axes, 0, 0, tiled=True)]
    ppermute x2 -> x4, starting transfers between devices: 3.83 us -> 7.67 us  [swap(): return lax.ppermute(value, 'c', [(0, 1), (1, 0)])]
    ppermute x2 -> x4, waiting for transfers between devices: 0.01 us -> 2.34 us  [swap(): return lax.ppermute(value, 'c', [(0, 1), (1, 0)])]
    pallas_call x2, Pallas kernels: 6.01 us -> 3.84 us  [shards(): call(functools.partial(forward_kernel, which), [((16, 128, 256), BF, VMEM...]
    pallas_call x5 -> x8, Pallas kernels: 7.11 us -> 8.76 us  [the longest x1 2.74 us: shards(): call(functools.partial(backward_other_kernel, 1.0 / math.sqrt(nodes_total...]
  transfers between devices with their start and end apart: 10 -> 13, of which waited for: 7 -> 9; matrix products, arithmetic and copies ran while one was open for 0% -> 0% of each run, Pallas kernels for 6% -> 4%
where the time goes in v6:
time: 195 us; the launch traced here: 191 us
  blocking collectives  94.8 us (49%)
  starting transfers between devices  47.2 us (24%)
  waiting for transfers between devices  28.2 us (14%)
  Pallas kernels  16.9 us (9%)
  local copies, waits for them, and re-layouts  2.1 us (1%)
    all_to_all x3, blocking collectives, exchange(): return lax.all_to_all(value, axes, 0, 0, tiled=True)  94.8 us
    all_to_all x3, waiting for transfers between devices, exchange(): return lax.all_to_all(value, axes, 0, 0, tiled=True)  20 us
    all_to_all x3, starting transfers between devices, exchange(): return lax.all_to_all(value, axes, 0, 0, tiled=True)  20 us
    ppermute x6, starting transfers between devices, rotate(): return lax.ppermute(value, axis, [(i, (i + k) % 4) for i in range(4)])  19.4 us
    ppermute x4, starting transfers between devices, swap(): return lax.ppermute(value, 'c', [(0, 1), (1, 0)])  7.67 us
    ppermute x6, waiting for transfers between devices, rotate(): return lax.ppermute(value, axis, [(i, (i + k) % 4) for i in range(4)])  5.78 us
  transfers between devices with their start and end apart: 13, of which 9 were waited for; matrix products, arithmetic and copies ran while one was open for 0% of the time, Pallas kernels for 4%

profile of v6, /device:TPU:6, one launch (start us, length us, event | category | flops | bytes accessed | tf_op | source)
XLA Modules:
  0.0 191.0 jit_solution(6500490471770298068)
XLA Ops:
  0.6 0.0 copy-start.3
  0.6 0.0 copy-start
  0.7 1.0 broadcast_in_dim.4
  1.7 15.9 %all_to_all.30 = bf16[4,128,256]{2,1,0:T(8,128)(2,1)S(1)} all-to-all(bf16[4,128,256]{2,1,0:T(8,128)(2,1)S(1)} %broadcast_in_dim.4), channel_id=1, replica_groups=mesh['zl'=4,'x'=4,'zh'=2,'y'=8,'c'=2] {'zl'}, dimensions={0} | all-to-all | bytes 524288 | tf_op jit(solution)/shard_map/all_to_all | solution.py:175
  17.6 1.1 broadcast_in_dim.5
  18.7 4.8 %all-to-all-start.1 = ((bf16[4,4,128,256]{3,2,1,0:T(8,128)(2,1)}), bf16[4,4,128,256]{3,2,1,0:T(8,128)(2,1)}, u32[]{:S(2)}, u32[]{:S(2)}) async-start(bf16[4,4,128,256]{3,2,1,0:T(8,128)(2,1)} %broadcast_in_dim.5), calls=%async_computation.1 | async-start | bytes 2097152 | tf_op jit(solution)/shard_map/all_to_all | solution.py:175
  24.1 0.1 pad_add_fusion.info
  24.2 1.8 shard_map.85
  26.0 8.4 %all-to-all-done.1 = bf16[4,4,128,256]{3,2,1,0:T(8,128)(2,1)} async-done(((bf16[4,4,128,256]{3,2,1,0:T(8,128)(2,1)}), bf16[4,4,128,256]{3,2,1,0:T(8,128)(2,1)}, u32[]{:S(2)}, u32[]{:S(2)}) %all-to-all-start.1) | async-done | bytes 1048608 | tf_op jit(solution)/shard_map/all_to_all | solution.py:175
  34.3 1.9 %shard_map.87 = bf16[16,128,256]{2,1,0:T(8,128)(2,1)S(1)} custom-call(s32[1120]{0:T(1024)S(1)} %get-tuple-element.20.lists, s32[2]{0:T(128)S(1)} %get-tuple-element.21.groups, bf16[96,128,128]{2,1,0:T(8,128)(2,1)S(1)} %bitcast.12, bf16[16,128,256]{2,1,0:T(8,128)(2,1)} %bitcast.6.nodes), custom_call_target="tpu_custom_call" | custom-call | flops 800000000 | bytes 6291456 | tf_op jit(solution)/shard_map/pallas_call | solution.py:205
  36.2 1.9 %collective-permute-start = (bf16[16,128,256]{2,1,0:T(8,128)(2,1)S(1)}, bf16[16,128,256]{2,1,0:T(8,128)(2,1)S(1)}, u32[]{:S(2)}, u32[]{:S(2)}) collective-permute-start(bf16[16,128,256]{2,1,0:T(8,128)(2,1)S(1)} %shard_map.87), channel_id=1, source_target_pairs={{0,1},{1,0},{2,3},{3,2},{4,5},{5,4},{6,7},{7,6},{8,9},{9,8},{10,11... | collective-permute-start | bytes 3145736 | tf_op jit(solution)/shard_map/ppermute | solution.py:179
  38.2 1.9 %shard_map.86 = bf16[16,128,256]{2,1,0:T(8,128)(2,1)S(1)} custom-call(s32[1120]{0:T(1024)S(1)} %get-tuple-element.20.lists, s32[2]{0:T(128)S(1)} %get-tuple-element.21.groups, bf16[96,128,128]{2,1,0:T(8,128)(2,1)S(1)} %bitcast.13, bf16[16,128,256]{2,1,0:T(8,128)(2,1)} %bitcast.6.nodes), custom_call_target="tpu_custom_call" | custom-call | flops 800000000 | bytes 6291456 | tf_op jit(solution)/shard_map/pallas_call | solution.py:205
  40.1 0.0 copy-start.1
  40.1 0.0 copy-start.2
  40.1 0.7 collective-permute-done
  40.8 0.3 add_convert_fusion
  41.1 44.9 %all_to_all.31.parts = bf16[16,128,256]{2,1,0:T(8,128)(2,1)S(1)} all-to-all(bf16[16,128,256]{2,1,0:T(8,128)(2,1)S(1)} %add_convert_fusion), channel_id=1, replica_groups=mesh['zl'=4,'x'=4,'zh'=2,'y'=8,'c'=2] {'zh','y'}, dimensions={0} | all-to-all | bytes 2097152 | tf_op jit(solution)/shard_map/all_to_all | solution.py:175
  86.0 2.0 %shard_map.88 = (bf16[128,256]{1,0:T(8,128)(2,1)}, bf16[16,256,128]{2,1,0:T(8,128)(2,1)}, f32[128,256]{1,0:T(8,128)S(1)}, f32[128,256]{1,0:T(8,128)S(1)}) custom-call(s32[4]{0:T(128)S(1)} %pad_add_fusion.info, bf16[16,128,256]{2,1,0:T(8,128)(2,1)S(1)} %all_to_all.31.parts, bf16[256,256]{1,0:T(8,128)(2,1)S(1)} %copy-done.1, bf16[128,256]{1,0:T(8,128)(2,1)S(1)} %copy-done.2), custom_call_target="tpu_custom_call" | custom-call | tf_op jit(solution)/shard_map/pallas_call | solution.py:216
  88.0 4.8 %all-to-all-start.3 = ((bf16[16,256,128]{2,1,0:T(8,128)(2,1)}), bf16[16,256,128]{2,1,0:T(8,128)(2,1)S(1)}, u32[]{:S(2)}, u32[]{:S(2)}) async-start(bf16[16,256,128]{2,1,0:T(8,128)(2,1)} %get-tuple-element.33), calls=%async_computation.3 | async-start | bytes 2097152 | tf_op jit(solution)/shard_map/all_to_all | solution.py:175
  92.8 1.9 %collective-permute-start.1 = (f32[128,256]{1,0:T(8,128)S(1)}, f32[128,256]{1,0:T(8,128)S(1)}, u32[]{:S(2)}, u32[]{:S(2)}) collective-permute-start(f32[128,256]{1,0:T(8,128)S(1)} %get-tuple-element.24), channel_id=1, source_target_pairs={{0,1},{1,0},{2,3},{3,2},{4,5},{5,4},{6,7},{7,6},{8,9},{9,8},{10,11... | collective-permute-start | bytes 393224 | tf_op jit(solution)/shard_map/ppermute | solution.py:179
  94.8 1.3 collective-permute-done.1.refs_1_
  96.1 0.6 shard_map.89
  96.6 3.3 %collective-permute-start.2 = (f32[32,256]{1,0:T(8,128)S(1)}, f32[32,256]{1,0:T(8,128)S(1)}, u32[]{:S(2)}, u32[]{:S(2)}) collective-permute-start(f32[32,256]{1,0:T(8,128)S(1)} %get-tuple-element.26), channel_id=1, source_target_pairs={{0,32},{32,64},{64,96},{96,0},{1,33},{33,65},{65,97},{97,1},{2,34}... | collective-permute-start | bytes 98312 | tf_op jit(solution)/shard_map/ppermute | solution.py:183
  100.0 1.9 %collective-permute-start.3 = (f32[32,256]{1,0:T(8,128)S(1)}, f32[32,256]{1,0:T(8,128)S(1)}, u32[]{:S(2)}, u32[]{:S(2)}) collective-permute-start(f32[32,256]{1,0:T(8,128)S(1)} %get-tuple-element.27), channel_id=1, source_target_pairs={{0,64},{32,96},{64,0},{96,32},{1,65},{33,97},{65,1},{97,33},{2,66}... | collective-permute-start | bytes 98312 | tf_op jit(solution)/shard_map/ppermute | solution.py:183
  101.9 3.3 %collective-permute-start.4 = (f32[32,256]{1,0:T(8,128)S(1)}, f32[32,256]{1,0:T(8,128)S(1)}, u32[]{:S(2)}, u32[]{:S(2)}) collective-permute-start(f32[32,256]{1,0:T(8,128)S(1)} %get-tuple-element.28), channel_id=1, source_target_pairs={{0,96},{32,0},{64,32},{96,64},{1,97},{33,1},{65,33},{97,65},{2,98}... | collective-permute-start | bytes 98312 | tf_op jit(solution)/shard_map/ppermute | solution.py:183
  105.2 0.0 collective-permute-done.2.refs_1_
  105.3 2.0 %collective-permute-done.3.refs_2_ = f32[32,256]{1,0:T(8,128)S(1)} collective-permute-done((f32[32,256]{1,0:T(8,128)S(1)}, f32[32,256]{1,0:T(8,128)S(1)}, u32[]{:S(2)}, u32[]{:S(2)}) %collective-permute-start.3) | collective-permute-done | bytes 32800 | tf_op jit(solution)/shard_map/ppermute | solution.py:183
  107.3 1.7 collective-permute-done.4.refs_3_
  109.0 0.6 shard_map.90
  109.5 2.9 %collective-permute-start.5 = (f32[8,256]{1,0:T(8,128)S(1)}, f32[8,256]{1,0:T(8,128)S(1)}, u32[]{:S(2)}, u32[]{:S(2)}) collective-permute-start(f32[8,256]{1,0:T(8,128)S(1)} %get-tuple-element.30), channel_id=1, source_target_pairs={{0,128},{128,256},{256,384},{384,0},{1,129},{129,257},{257,385},{3... | collective-permute-start | bytes 24584 | tf_op jit(solution)/shard_map/ppermute | solution.py:183
  112.4 4.5 %collective-permute-start.6 = (f32[8,256]{1,0:T(8,128)S(1)}, f32[8,256]{1,0:T(8,128)S(1)}, u32[]{:S(2)}, u32[]{:S(2)}) collective-permute-start(f32[8,256]{1,0:T(8,128)S(1)} %get-tuple-element.31), channel_id=1, source_target_pairs={{0,256},{128,384},{256,0},{384,128},{1,257},{129,385},{257,1},{385... | collective-permute-start | bytes 24584 | tf_op jit(solution)/shard_map/ppermute | solution.py:183
  117.0 3.5 %collective-permute-start.7 = (f32[8,256]{1,0:T(8,128)S(1)}, f32[8,256]{1,0:T(8,128)S(1)}, u32[]{:S(2)}, u32[]{:S(2)}) collective-permute-start(f32[8,256]{1,0:T(8,128)S(1)} %get-tuple-element.32), channel_id=1, source_target_pairs={{0,384},{128,0},{256,128},{384,256},{1,385},{129,1},{257,129},{385... | collective-permute-start | bytes 24584 | tf_op jit(solution)/shard_map/ppermute | solution.py:183
  120.4 0.0 collective-permute-done.5.w1
  120.4 0.0 collective-permute-done.6.w2
  120.4 2.1 %collective-permute-done.7.w3 = f32[8,256]{1,0:T(8,128)S(1)} collective-permute-done((f32[8,256]{1,0:T(8,128)S(1)}, f32[8,256]{1,0:T(8,128)S(1)}, u32[]{:S(2)}, u32[]{:S(2)}) %collective-permute-start.7) | collective-permute-done | bytes 8224 | tf_op jit(solution)/shard_map/ppermute | solution.py:183
  122.5 1.6 all-to-all-done.3.own
  124.1 0.7 shard_map.91
  124.7 1.9 collective-permute-start.8
  126.7 10.5 %all-to-all-start.4 = ((f32[16,8,256]{2,1,0:T(8,128)}), f32[16,8,256]{2,1,0:T(8,128)S(1)}, u32[]{:S(2)}, u32[]{:S(2)}) async-start(f32[16,8,256]{2,1,0:T(8,128)} %get-tuple-element.35), calls=%async_computation.4 | async-start | bytes 262144 | tf_op jit(solution)/shard_map/all_to_all | solution.py:175
  137.1 2.5 %shard_map.92.begun = f32[17,256,128]{2,1,0:T(8,128)S(1)} custom-call(s32[1120]{0:T(1024)S(1)} %get-tuple-element.20.lists, s32[2]{0:T(128)S(1)} %get-tuple-element.21.groups, bf16[96,128,128]{2,1,0:T(8,128)(2,1)} %bitcast.9, bf16[16,256,128]{2,1,0:T(8,128)(2,1)S(1)} %get-tuple-element.34.own), custom_call_target="tpu_custom_call" | custom-call | flops 800000000 | bytes 6291456 | tf_op jit(solution)/shard_map/pallas_call | solution.py:243
  139.6 10.1 %all-to-all-done.4.grads = f32[16,8,256]{2,1,0:T(8,128)S(1)} async-done(((f32[16,8,256]{2,1,0:T(8,128)}), f32[16,8,256]{2,1,0:T(8,128)S(1)}, u32[]{:S(2)}, u32[]{:S(2)}) %all-to-all-start.4) | async-done | bytes 131104 | tf_op jit(solution)/shard_map/all_to_all | solution.py:175
  149.7 0.0 collective-permute-done.8.other
  149.7 2.7 %shard_map.93 = (bf16[16,272,128]{2,1,0:T(8,128)(2,1)S(1)}, f32[17,256,128]{2,1,0:T(8,128)S(1)}) custom-call(s32[1120]{0:T(1024)S(1)} %get-tuple-element.20.lists, s32[2]{0:T(128)S(1)} %get-tuple-element.21.groups, bf16[96,128,128]{2,1,0:T(8,128)(2,1)} %bitcast.10, ...), custom_call_target="tpu_custom_call", output_to_operand_aliasing={{1}: (5, {})} | custom-call | flops 800000000 | bytes 6291456 | tf_op jit(solution)/shard_map/pallas_call | solution.py:249
  152.5 34.0 %all_to_all.32.parts = bf16[16,272,128]{2,1,0:T(8,128)(2,1)S(1)} all-to-all(bf16[16,272,128]{2,1,0:T(8,128)(2,1)S(1)} %get-tuple-element.36), channel_id=1, replica_groups=mesh['zl'=4,'x'=4,'zh'=2,'y'=8,'c'=2] {'zl','x'}, dimensions={0} | all-to-all | bytes 2228224 | tf_op jit(solution)/shard_map/all_to_all | solution.py:175
  186.5 1.9 %collective-permute-start.9 = (f32[128,256]{1,0:T(8,128)S(1)}, f32[128,256]{1,0:T(8,128)S(1)}, u32[]{:S(2)}, u32[]{:S(2)}) collective-permute-start(f32[128,256]{1,0:T(8,128)S(1)} %shard_map.95.mine), channel_id=1, source_target_pairs={{0,1},{1,0},{2,3},{3,2},{4,5},{5,4},{6,7},{7,6},{8,9},{9,8},{10,11... | collective-permute-start | bytes 393224 | tf_op jit(solution)/shard_map/ppermute | solution.py:179
  188.4 1.0 shard_map.94
  189.4 0.4 collective-permute-done.9.theirs
  189.8 1.3 shard_map.96
  (5 shorter events, 0.0 us)
Async XLA Ops:
  0.6 23.5 %copy-start.3 = (s32[1,1,96]{2,1,0:T(1,128)S(1)}, s32[1,1,96]{2,1,0:T(1,128)}, u32[]{:S(2)}) copy-start(s32[1,1,96]{2,1,0:T(1,128)} %param.10) | copy-start | bytes 1156
  0.6 23.5 %copy-start = (bf16[1,1,96,128,128]{4,3,2,1,0:T(8,128)(2,1)S(1)}, bf16[1,1,96,128,128]{4,3,2,1,0:T(8,128)(2,1)}, u32[]{:S(2)}) copy-start(bf16[1,1,96,128,128]{4,3,2,1,0:T(8,128)(2,1)} %param.9) | copy-start | bytes 9437188
  18.7 15.7 %all-to-all-start.1 = ((bf16[4,4,128,256]{3,2,1,0:T(8,128)(2,1)}), bf16[4,4,128,256]{3,2,1,0:T(8,128)(2,1)}, u32[]{:S(2)}, u32[]{:S(2)}) async-start(bf16[4,4,128,256]{3,2,1,0:T(8,128)(2,1)} %broadcast_in_dim.5), calls=%async_computation.1 | async-start | bytes 2097152 | tf_op jit(solution)/shard_map/all_to_all | solution.py:175
  36.2 4.6 %collective-permute-start = (bf16[16,128,256]{2,1,0:T(8,128)(2,1)S(1)}, bf16[16,128,256]{2,1,0:T(8,128)(2,1)S(1)}, u32[]{:S(2)}, u32[]{:S(2)}) collective-permute-start(bf16[16,128,256]{2,1,0:T(8,128)(2,1)S(1)} %shard_map.87), channel_id=1, source_target_pairs={{0,1},{1,0},{2,3},{3,2},{4,5},{5,4},{6,7},{7,6},{8,9},{9,8},{10,11... | collective-permute-start | bytes 3145736 | tf_op jit(solution)/shard_map/ppermute | solution.py:179
  40.1 45.9 %copy-start.1 = (bf16[256,256]{1,0:T(8,128)(2,1)S(1)}, bf16[256,256]{1,0:T(8,128)(2,1)}, u32[]{:S(2)}) copy-start(bf16[256,256]{1,0:T(8,128)(2,1)} %weight.3) | copy-start | bytes 393220
  40.1 45.9 %copy-start.2 = (bf16[128,256]{1,0:T(8,128)(2,1)S(1)}, bf16[128,256]{1,0:T(8,128)(2,1)}, u32[]{:S(2)}) copy-start(bf16[128,256]{1,0:T(8,128)(2,1)} %cotangent.1) | copy-start | bytes 196612
  88.0 36.1 %all-to-all-start.3 = ((bf16[16,256,128]{2,1,0:T(8,128)(2,1)}), bf16[16,256,128]{2,1,0:T(8,128)(2,1)S(1)}, u32[]{:S(2)}, u32[]{:S(2)}) async-start(bf16[16,256,128]{2,1,0:T(8,128)(2,1)} %get-tuple-element.33), calls=%async_computation.3 | async-start | bytes 2097152 | tf_op jit(solution)/shard_map/all_to_all | solution.py:175
  92.8 3.2 %collective-permute-start.1 = (f32[128,256]{1,0:T(8,128)S(1)}, f32[128,256]{1,0:T(8,128)S(1)}, u32[]{:S(2)}, u32[]{:S(2)}) collective-permute-start(f32[128,256]{1,0:T(8,128)S(1)} %get-tuple-element.24), channel_id=1, source_target_pairs={{0,1},{1,0},{2,3},{3,2},{4,5},{5,4},{6,7},{7,6},{8,9},{9,8},{10,11... | collective-permute-start | bytes 393224 | tf_op jit(solution)/shard_map/ppermute | solution.py:179
  96.6 8.6 %collective-permute-start.2 = (f32[32,256]{1,0:T(8,128)S(1)}, f32[32,256]{1,0:T(8,128)S(1)}, u32[]{:S(2)}, u32[]{:S(2)}) collective-permute-start(f32[32,256]{1,0:T(8,128)S(1)} %get-tuple-element.26), channel_id=1, source_target_pairs={{0,32},{32,64},{64,96},{96,0},{1,33},{33,65},{65,97},{97,1},{2,34}... | collective-permute-start | bytes 98312 | tf_op jit(solution)/shard_map/ppermute | solution.py:183
  100.0 7.3 %collective-permute-start.3 = (f32[32,256]{1,0:T(8,128)S(1)}, f32[32,256]{1,0:T(8,128)S(1)}, u32[]{:S(2)}, u32[]{:S(2)}) collective-permute-start(f32[32,256]{1,0:T(8,128)S(1)} %get-tuple-element.27), channel_id=1, source_target_pairs={{0,64},{32,96},{64,0},{96,32},{1,65},{33,97},{65,1},{97,33},{2,66}... | collective-permute-start | bytes 98312 | tf_op jit(solution)/shard_map/ppermute | solution.py:183
  101.9 7.0 %collective-permute-start.4 = (f32[32,256]{1,0:T(8,128)S(1)}, f32[32,256]{1,0:T(8,128)S(1)}, u32[]{:S(2)}, u32[]{:S(2)}) collective-permute-start(f32[32,256]{1,0:T(8,128)S(1)} %get-tuple-element.28), channel_id=1, source_target_pairs={{0,96},{32,0},{64,32},{96,64},{1,97},{33,1},{65,33},{97,65},{2,98}... | collective-permute-start | bytes 98312 | tf_op jit(solution)/shard_map/ppermute | solution.py:183
  109.5 10.9 %collective-permute-start.5 = (f32[8,256]{1,0:T(8,128)S(1)}, f32[8,256]{1,0:T(8,128)S(1)}, u32[]{:S(2)}, u32[]{:S(2)}) collective-permute-start(f32[8,256]{1,0:T(8,128)S(1)} %get-tuple-element.30), channel_id=1, source_target_pairs={{0,128},{128,256},{256,384},{384,0},{1,129},{129,257},{257,385},{3... | collective-permute-start | bytes 24584 | tf_op jit(solution)/shard_map/ppermute | solution.py:183
  112.4 8.0 %collective-permute-start.6 = (f32[8,256]{1,0:T(8,128)S(1)}, f32[8,256]{1,0:T(8,128)S(1)}, u32[]{:S(2)}, u32[]{:S(2)}) collective-permute-start(f32[8,256]{1,0:T(8,128)S(1)} %get-tuple-element.31), channel_id=1, source_target_pairs={{0,256},{128,384},{256,0},{384,128},{1,257},{129,385},{257,1},{385... | collective-permute-start | bytes 24584 | tf_op jit(solution)/shard_map/ppermute | solution.py:183
  117.0 5.5 %collective-permute-start.7 = (f32[8,256]{1,0:T(8,128)S(1)}, f32[8,256]{1,0:T(8,128)S(1)}, u32[]{:S(2)}, u32[]{:S(2)}) collective-permute-start(f32[8,256]{1,0:T(8,128)S(1)} %get-tuple-element.32), channel_id=1, source_target_pairs={{0,384},{128,0},{256,128},{384,256},{1,385},{129,1},{257,129},{385... | collective-permute-start | bytes 24584 | tf_op jit(solution)/shard_map/ppermute | solution.py:183
  124.7 25.0 %collective-permute-start.8 = (bf16[16,256,128]{2,1,0:T(8,128)(2,1)S(1)}, bf16[16,256,128]{2,1,0:T(8,128)(2,1)}, u32[]{:S(2)}, u32[]{:S(2)}) collective-permute-start(bf16[16,256,128]{2,1,0:T(8,128)(2,1)S(1)} %get-tuple-element.34.own), channel_id=1, source_target_pairs={{0,1},{1,0},{2,3},{3,2},{4,5},{5,4},{6,7},{7,6},{8,9},{9,8},{10,11... | collective-permute-start | bytes 3145736 | tf_op jit(solution)/shard_map/ppermute | solution.py:179
  126.7 23.1 %all-to-all-start.4 = ((f32[16,8,256]{2,1,0:T(8,128)}), f32[16,8,256]{2,1,0:T(8,128)S(1)}, u32[]{:S(2)}, u32[]{:S(2)}) async-start(f32[16,8,256]{2,1,0:T(8,128)} %get-tuple-element.35), calls=%async_computation.4 | async-start | bytes 262144 | tf_op jit(solution)/shard_map/all_to_all | solution.py:175
  186.5 3.2 %collective-permute-start.9 = (f32[128,256]{1,0:T(8,128)S(1)}, f32[128,256]{1,0:T(8,128)S(1)}, u32[]{:S(2)}, u32[]{:S(2)}) collective-permute-start(f32[128,256]{1,0:T(8,128)S(1)} %shard_map.95.mine), channel_id=1, source_target_pairs={{0,1},{1,0},{2,3},{3,2},{4,5},{5,4},{6,7},{7,6},{8,9},{9,8},{10,11... | collective-permute-start | bytes 393224 | tf_op jit(solution)/shard_map/ppermute | solution.py:179

commit v7 on v6

--- a/solution.py
+++ b/solution.py
@@ -69,7 +69,7 @@
     out[...] = acc[0:16].astype(BF)
 
 
-def middle_kernel(info, parts, weight, cotangent, output, spread, stay, go, grad):
+def middle_kernel(parts, weight, cotangent, output, spread, turned_share, slopes_out):
     total = parts[0].astype(F32)
     for s in range(1, 16):
         total += parts[s].astype(F32)
@@ -82,7 +82,12 @@
     turned = slopes.astype(F32).T.astype(BF)
     for s in range(16):
         spread[s] = turned
-    grad[...] = dot(share.astype(F32).T.astype(BF), slopes).reshape(2, 128, 256)
+    turned_share[...] = share.astype(F32).T.astype(BF)
+    slopes_out[...] = slopes
+
+
+def product_kernel(info, turned_share, slopes, stay, go, grad):
+    grad[...] = dot(turned_share[...], slopes[...]).reshape(2, 128, 256)
     stay[...] = grad[info[1]]
     go[...] = grad[1 - info[1]]
 
@@ -99,10 +104,8 @@
         out[...] = scratch[(info[me] + k) & 3]
 
 
-def offer_kernel(w0, w1, w2, w3, own, out, held):
-    total = w0[...] + w1[...] + w2[...] + w3[...]
-    for s in range(16):
-        out[s] = total
+def gate_kernel(mine, theirs, own, out, held):
+    out[...] = mine[...] + theirs[...]
 
 
 def back_products(which, lists, groups, blocks, source, acc):
@@ -124,31 +127,21 @@
     back_products(0, lists, groups, blocks, own, acc)
 
 
-def backward_other_kernel(scale, lists, groups, blocks, other, grads, begun, out, acc):
+def backward_other_kernel(lists, groups, blocks, other, mine, theirs, begun, out, total, acc):
+    total[...] = mine[...] + theirs[...]
     back_products(1, lists, groups, blocks, other, acc)
-    grad = grads[0]
+    out[...] = acc[0:16].astype(BF)
+
+
+def gather_kernel(scale, info, w0, w1, w2, w3, parts, out, held):
+    for k, part in enumerate((w0, w1, w2, w3)):
+        out[(info[2] - k) & 3] = part[...] * scale
+
+
+def last_kernel(parts, weight, input_grad):
+    total = parts[0].astype(F32)
     for s in range(1, 16):
-        grad += grads[s]
-    grad = grad * scale
-    packed = jnp.concatenate([grad[:, 0:128], grad[:, 128:256]], axis=0).astype(BF)
-    for s in range(16):
-        out[s, 0:256, :] = acc[s].astype(BF)
-        out[s, 256:272, :] = packed
-
-
-def grad_kernel(parts, out):
-    for z in range(4):
-        for x in range(4):
-            packed = parts[4 * z + x, 256:272, :].astype(F32)
-            row = 32 * x + 8 * z
-            out[row : row + 8, 0:128] = packed[0:8]
-            out[row : row + 8, 128:256] = packed[8:16]
-
-
-def last_kernel(parts, weight, input_grad):
-    total = parts[0, 0:256, :].astype(F32)
-    for s in range(1, 16):
-        total += parts[s, 0:256, :].astype(F32)
+        total += parts[s].astype(F32)
     back = total.astype(BF).astype(F32).T.astype(BF)
     input_grad[...] = dot(back, weight[...], (((1,), (1,)), ((), ()))).astype(BF)
 
@@ -177,6 +170,10 @@
 
 def swap(value):
     return lax.ppermute(value, "c", [(0, 1), (1, 0)])
+
+
+def paired_sum(value, axis, size, k):
+    return value + lax.ppermute(value, axis, [(i, i ^ k) for i in range(size)])
 
 
 def rotate(value, axis, k):
@@ -213,32 +210,33 @@
     ]
     pair = (keep.astype(F32) + swap(send).astype(F32)).astype(BF)
     parts = exchange(pair, ("zh", "y"))
-    output, spread, stay, go = call(
+    output, spread, share, slopes = call(
         middle_kernel,
-        [((128, 256), BF, VMEM), ((16, 256, 128), BF, VMEM)] + [((128, 256), F32, VMEM)] * 2,
-        [SMEM, VMEM, VMEM, VMEM],
+        [((128, 256), BF, VMEM), ((16, 256, 128), BF, VMEM), ((256, 128), BF, VMEM), ((128, 256), BF, VMEM)],
+        [VMEM, VMEM, VMEM],
+    )(parts, weight, cotangent)
+    own = exchange(spread, ("zh", "y"))
+
+    stay, go = call(
+        product_kernel,
+        [((128, 256), F32, VMEM)] * 2,
+        [SMEM, VMEM, VMEM],
         [pltpu.VMEM((2, 128, 256), F32)],
-    )(info, parts, weight, cotangent)
-    own = exchange(spread, ("zh", "y"))
-
-    def scatter(me, rows, held):
-        return call(
-            functools.partial(scatter_kernel, me, len(held)),
-            [((rows, 256), F32, VMEM)] * 4,
-            [SMEM] + [VMEM] * len(held),
-            [pltpu.VMEM((4, rows, 256), F32)],
-        )(info, *held)
-
-    held = scatter(2, 32, [stay, swap(go)])
-    held = scatter(3, 8, [held[0]] + [rotate(held[k], "x", k) for k in rounds])
-    held = [held[0]] + [rotate(held[k], "zl", k) for k in rounds]
-    offer, own = call(
-        offer_kernel,
-        [((16, 8, 256), F32, VMEM), ((16, 256, 128), BF, VMEM)],
-        [VMEM] * 5,
-        alias={4: 1},
-    )(*held, own)
-    grads = exchange(offer, ("zh", "y"))
+    )(info, share, slopes)
+    held = call(
+        functools.partial(scatter_kernel, 2, 2),
+        [((32, 256), F32, VMEM)] * 4,
+        [SMEM, VMEM, VMEM],
+        [pltpu.VMEM((4, 32, 256), F32)],
+    )(info, stay, swap(go))
+    held = [held[0]] + [rotate(held[k], "x", k) for k in rounds]
+    total = paired_sum(held[0] + held[1] + held[2] + held[3], "zh", 2, 1)
+    total, own = call(
+        gate_kernel,
+        [((32, 256), F32, VMEM), ((16, 256, 128), BF, VMEM)],
+        [VMEM] * 3,
+        alias={2: 1},
+    )(total, lax.ppermute(total, "y", [(i, i ^ 1) for i in range(8)]), own)
     other = swap(own)
     (begun,) = call(
         backward_own_kernel,
@@ -246,18 +244,26 @@
         [SMEM, SMEM, VMEM, VMEM],
         **heavy,
     )(lists, groups, tile, own)
-    back, _ = call(
-        functools.partial(backward_other_kernel, 1.0 / math.sqrt(nodes_total)),
-        [((16, 272, 128), BF, VMEM), ((17, 256, 128), F32, VMEM)],
-        [SMEM, SMEM] + [VMEM] * 4,
+    theirs = lax.ppermute(total, "y", [(i, i ^ 2) for i in range(8)])
+    back, total, _ = call(
+        backward_other_kernel,
+        [((16, 256, 128), BF, VMEM), ((32, 256), F32, VMEM), ((17, 256, 128), F32, VMEM)],
+        [SMEM, SMEM] + [VMEM] * 5,
+        alias={6: 2},
+        **heavy,
+    )(lists, groups, tile, other, total, theirs, begun)
+    total = paired_sum(total, "y", 8, 4)
+    total = paired_sum(paired_sum(total, "zl", 4, 1), "zl", 4, 2)
+    parts = exchange(back, ("zl", "x"))
+    mine, parts = call(
+        functools.partial(gather_kernel, 1.0 / math.sqrt(nodes_total)),
+        [((4, 32, 256), F32, VMEM), ((16, 256, 128), BF, VMEM)],
+        [SMEM] + [VMEM] * 5,
         alias={5: 1},
-        **heavy,
-    )(lists, groups, tile, other, grads, begun)
-    parts = exchange(back, ("zl", "x"))
-    (mine,) = call(grad_kernel, [((128, 256), F32, VMEM)], [VMEM])(parts)
+    )(info, total, *[rotate(total, "x", k) for k in rounds], parts)
     theirs = swap(mine)
     (input_grad,) = call(last_kernel, [((128, 256), BF, VMEM)], [VMEM] * 2, flops=2**24, size=2**20)(parts, weight)
-    (weight_grad,) = call(join_kernel, [((2, 128, 256), F32, VMEM)], [SMEM, VMEM, VMEM])(info, mine, theirs)
+    (weight_grad,) = call(join_kernel, [((2, 4, 32, 256), F32, VMEM)], [SMEM, VMEM, VMEM])(info, mine, theirs)
     weight_grad = weight_grad.reshape(256, 256)
     return (output, input_grad, weight_grad)
 

time: 195 us -> 197 us (1.010)
  the two profiles are of different devices: /device:TPU:6 before, /device:TPU:57 now
where the time goes in v7:
time: 197 us; the launch traced here: 196 us
  starting transfers between devices  78.6 us (40%)
  blocking collectives  55.4 us (28%)
  waiting for transfers between devices  41.2 us (21%)
  Pallas kernels  17 us (9%)
  local copies, waits for them, and re-layouts  2.11 us (1%)
    all_to_all x2, blocking collectives, exchange(): return lax.all_to_all(value, axes, 0, 0, tiled=True)  55.4 us
    ppermute x4, waiting for transfers between devices, paired_sum(): return value + lax.ppermute(value, axis, [(i, i ^ k) for i in range(size)])  23.7 us
    ppermute x4, starting transfers between devices, paired_sum(): return value + lax.ppermute(value, axis, [(i, i ^ k) for i in range(size)])  20.1 us
    ppermute x6, starting transfers between devices, rotate(): return lax.ppermute(value, axis, [(i, (i + k) % 4) for i in range(4)])  17.8 us
    ppermute x4, starting transfers between devices, swap(): return lax.ppermute(value, 'c', [(0, 1), (1, 0)])  17.1 us
    all_to_all x3, starting transfers between devices, exchange(): return lax.all_to_all(value, axes, 0, 0, tiled=True)  16.6 us
    all_to_all x3, waiting for transfers between devices, exchange(): return lax.all_to_all(value, axes, 0, 0, tiled=True)  9.33 us
    ppermute x6, waiting for transfers between devices, rotate(): return lax.ppermute(value, axis, [(i, (i + k) % 4) for i in range(4)])  5.59 us
  transfers between devices with their start and end apart: 19, of which 11 were waited for; matrix products, arithmetic and copies ran while one was open for 0% of the time, Pallas kernels for 4%

profile of v7, /device:TPU:57, one launch (start us, length us, event | category | flops | bytes accessed | tf_op | source)
XLA Modules:
  0.0 196.5 jit_solution(14320112561286022510)
XLA Ops:
  0.7 1.0 broadcast_in_dim.4
  1.7 13.7 %all_to_all.25 = bf16[4,128,256]{2,1,0:T(8,128)(2,1)S(1)} all-to-all(bf16[4,128,256]{2,1,0:T(8,128)(2,1)S(1)} %broadcast_in_dim.4), channel_id=1, replica_groups=mesh['zl'=4,'x'=4,'zh'=2,'y'=8,'c'=2] {'zl'}, dimensions={0} | all-to-all | bytes 524288 | tf_op jit(solution)/shard_map/all_to_all | solution.py:168
  15.3 1.1 broadcast_in_dim.5
  16.4 4.2 %all-to-all-start.1 = ((bf16[4,4,128,256]{3,2,1,0:T(8,128)(2,1)}), bf16[4,4,128,256]{3,2,1,0:T(8,128)(2,1)}, u32[]{:S(2)}, u32[]{:S(2)}) async-start(bf16[4,4,128,256]{3,2,1,0:T(8,128)(2,1)} %broadcast_in_dim.5), calls=%async_computation.1 | async-start | bytes 2097152 | tf_op jit(solution)/shard_map/all_to_all | solution.py:168
  21.3 0.1 pad_add_fusion.info
  21.4 1.8 shard_map.85
  23.2 9.3 %all-to-all-done.1 = bf16[4,4,128,256]{3,2,1,0:T(8,128)(2,1)} async-done(((bf16[4,4,128,256]{3,2,1,0:T(8,128)(2,1)}), bf16[4,4,128,256]{3,2,1,0:T(8,128)(2,1)}, u32[]{:S(2)}, u32[]{:S(2)}) %all-to-all-start.1) | async-done | bytes 1048608 | tf_op jit(solution)/shard_map/all_to_all | solution.py:168
  32.5 1.9 shard_map.87
  34.4 6.2 %collective-permute-start = (bf16[16,128,256]{2,1,0:T(8,128)(2,1)S(1)}, bf16[16,128,256]{2,1,0:T(8,128)(2,1)S(1)}, u32[]{:S(2)}, u32[]{:S(2)}) collective-permute-start(bf16[16,128,256]{2,1,0:T(8,128)(2,1)S(1)} %shard_map.87), channel_id=1, source_target_pairs={{0,1},{1,0},{2,3},{3,2},{4,5},{5,4},{6,7},{7,6},{8,9},{9,8},{10,11... | collective-permute-start | bytes 3145736 | tf_op jit(solution)/shard_map/ppermute | solution.py:172
  40.6 1.9 shard_map.86
  42.5 0.0 copy-start.2
  42.6 0.3 collective-permute-done
  42.9 0.3 add_convert_fusion
  43.2 41.8 %all_to_all.26.parts = bf16[16,128,256]{2,1,0:T(8,128)(2,1)S(1)} all-to-all(bf16[16,128,256]{2,1,0:T(8,128)(2,1)S(1)} %add_convert_fusion), channel_id=1, replica_groups=mesh['zl'=4,'x'=4,'zh'=2,'y'=8,'c'=2] {'zh','y'}, dimensions={0} | all-to-all | bytes 2097152 | tf_op jit(solution)/shard_map/all_to_all | solution.py:168
  84.9 1.4 shard_map.88
  86.4 6.9 %all-to-all-start.3 = ((bf16[16,256,128]{2,1,0:T(8,128)(2,1)}), bf16[16,256,128]{2,1,0:T(8,128)(2,1)S(1)}, u32[]{:S(2)}, u32[]{:S(2)}) async-start(bf16[16,256,128]{2,1,0:T(8,128)(2,1)} %get-tuple-element.32), calls=%async_computation.3 | async-start | bytes 2097152 | tf_op jit(solution)/shard_map/all_to_all | solution.py:168
  93.3 0.7 shard_map.89
  94.1 3.2 %collective-permute-start.1 = (f32[128,256]{1,0:T(8,128)S(1)}, f32[128,256]{1,0:T(8,128)S(1)}, u32[]{:S(2)}, u32[]{:S(2)}) collective-permute-start(f32[128,256]{1,0:T(8,128)S(1)} %get-tuple-element.27), channel_id=1, source_target_pairs={{0,1},{1,0},{2,3},{3,2},{4,5},{5,4},{6,7},{7,6},{8,9},{9,8},{10,11... | collective-permute-start | bytes 393224 | tf_op jit(solution)/shard_map/ppermute | solution.py:172
  97.2 1.0 collective-permute-done.1.refs_1_
  98.2 0.6 shard_map.90
  98.8 1.9 collective-permute-start.2
  100.7 2.7 %collective-permute-start.3 = (f32[32,256]{1,0:T(8,128)S(1)}, f32[32,256]{1,0:T(8,128)S(1)}, u32[]{:S(2)}, u32[]{:S(2)}) collective-permute-start(f32[32,256]{1,0:T(8,128)S(1)} %get-tuple-element.30), channel_id=1, source_target_pairs={{0,64},{32,96},{64,0},{96,32},{1,65},{33,97},{65,1},{97,33},{2,66}... | collective-permute-start | bytes 98312 | tf_op jit(solution)/shard_map/ppermute | solution.py:180
  103.4 3.8 %collective-permute-start.4 = (f32[32,256]{1,0:T(8,128)S(1)}, f32[32,256]{1,0:T(8,128)S(1)}, u32[]{:S(2)}, u32[]{:S(2)}) collective-permute-start(f32[32,256]{1,0:T(8,128)S(1)} %get-tuple-element.31), channel_id=1, source_target_pairs={{0,96},{32,0},{64,32},{96,64},{1,97},{33,1},{65,33},{97,65},{2,98}... | collective-permute-start | bytes 98312 | tf_op jit(solution)/shard_map/ppermute | solution.py:180
  107.2 2.1 %collective-permute-done.4 = f32[32,256]{1,0:T(8,128)S(1)} collective-permute-done((f32[32,256]{1,0:T(8,128)S(1)}, f32[32,256]{1,0:T(8,128)S(1)}, u32[]{:S(2)}, u32[]{:S(2)}) %collective-permute-start.4) | collective-permute-done | bytes 32800 | tf_op jit(solution)/shard_map/ppermute | solution.py:180
  109.4 7.0 %collective-permute-start.5 = (f32[32,256]{1,0:T(8,128)S(1)}, f32[32,256]{1,0:T(8,128)S(1)}, u32[]{:S(2)}, u32[]{:S(2)}) collective-permute-start(f32[32,256]{1,0:T(8,128)S(1)} %add_add_fusion), channel_id=1, source_target_pairs={{0,16},{16,0},{1,17},{17,1},{2,18},{18,2},{3,19},{19,3},{4,20},{20... | collective-permute-start | bytes 98312 | tf_op jit(solution)/shard_map/ppermute | solution.py:176
  116.4 9.8 %collective-permute-done.5 = f32[32,256]{1,0:T(8,128)S(1)} collective-permute-done((f32[32,256]{1,0:T(8,128)S(1)}, f32[32,256]{1,0:T(8,128)S(1)}, u32[]{:S(2)}, u32[]{:S(2)}) %collective-permute-start.5) | collective-permute-done | bytes 32800 | tf_op jit(solution)/shard_map/ppermute | solution.py:176
  126.2 3.9 %collective-permute-start.6 = (f32[32,256]{1,0:T(8,128)S(1)}, f32[32,256]{1,0:T(8,128)S(1)}, u32[]{:S(2)}, u32[]{:S(2)}) collective-permute-start(f32[32,256]{1,0:T(8,128)S(1)} %add.28.mine), channel_id=1, source_target_pairs={{0,2},{2,0},{4,6},{6,4},{8,10},{10,8},{12,14},{14,12},{1,3},{3,1},... | collective-permute-start | bytes 98312 | tf_op jit(solution)/shard_map/ppermute | solution.py:239
  130.1 1.3 collective-permute-done.6.theirs
  131.4 3.3 %collective-permute-start.7 = (bf16[16,256,128]{2,1,0:T(8,128)(2,1)S(1)}, bf16[16,256,128]{2,1,0:T(8,128)(2,1)S(1)}, u32[]{:S(2)}, u32[]{:S(2)}) collective-permute-start(bf16[16,256,128]{2,1,0:T(8,128)(2,1)S(1)} %get-tuple-element.33.own), channel_id=1, source_target_pairs={{0,1},{1,0},{2,3},{3,2},{4,5},{5,4},{6,7},{7,6},{8,9},{9,8},{10,11... | collective-permute-start | bytes 3145736 | tf_op jit(solution)/shard_map/ppermute | solution.py:172
  134.8 3.2 %collective-permute-start.8 = (f32[32,256]{1,0:T(8,128)S(1)}, f32[32,256]{1,0:T(8,128)S(1)}, u32[]{:S(2)}, u32[]{:S(2)}) collective-permute-start(f32[32,256]{1,0:T(8,128)S(1)} %get-tuple-element.34.mine), channel_id=1, source_target_pairs={{0,4},{2,6},{4,0},{6,2},{8,12},{10,14},{12,8},{14,10},{1,5},{3,7},... | collective-permute-start | bytes 98312 | tf_op jit(solution)/shard_map/ppermute | solution.py:247
  137.9 2.5 %shard_map.92.begun = f32[17,256,128]{2,1,0:T(8,128)S(1)} custom-call(s32[1120]{0:T(1024)S(1)} %get-tuple-element.21.lists, s32[2]{0:T(128)S(1)} %get-tuple-element.22.groups, bf16[96,128,128]{2,1,0:T(8,128)(2,1)} %bitcast.9, bf16[16,256,128]{2,1,0:T(8,128)(2,1)S(1)} %get-tuple-element.33.own), custom_call_target="tpu_custom_call" | custom-call | flops 800000000 | bytes 6291456 | tf_op jit(solution)/shard_map/pallas_call | solution.py:241
  140.5 3.4 %shard_map.93 = (bf16[16,256,128]{2,1,0:T(8,128)(2,1)}, f32[32,256]{1,0:T(8,128)S(1)}, f32[17,256,128]{2,1,0:T(8,128)S(1)}) custom-call(s32[1120]{0:T(1024)S(1)} %get-tuple-element.21.lists, s32[2]{0:T(128)S(1)} %get-tuple-element.22.groups, bf16[96,128,128]{2,1,0:T(8,128)(2,1)} %bitcast.10, ...), custom_call_target="tpu_custom_call", output_to_operand_aliasing={{2}: (6, {})} | custom-call | flops 800000000 | bytes 6291456 | tf_op jit(solution)/shard_map/pallas_call | solution.py:248
  143.9 5.4 %all-to-all-start.4 = ((bf16[16,256,128]{2,1,0:T(8,128)(2,1)}), bf16[16,256,128]{2,1,0:T(8,128)(2,1)S(1)}, u32[]{:S(2)}, u32[]{:S(2)}) async-start(bf16[16,256,128]{2,1,0:T(8,128)(2,1)} %get-tuple-element.36), calls=%async_computation.4 | async-start | bytes 2097152 | tf_op jit(solution)/shard_map/all_to_all | solution.py:168
  149.3 3.9 %collective-permute-start.9 = (f32[32,256]{1,0:T(8,128)S(1)}, f32[32,256]{1,0:T(8,128)S(1)}, u32[]{:S(2)}, u32[]{:S(2)}) collective-permute-start(f32[32,256]{1,0:T(8,128)S(1)} %get-tuple-element.35), channel_id=1, source_target_pairs={{0,8},{2,10},{4,12},{6,14},{8,0},{10,2},{12,4},{14,6},{1,9},{3,11}... | collective-permute-start | bytes 98312 | tf_op jit(solution)/shard_map/ppermute | solution.py:176
  153.2 5.0 %collective-permute-done.9 = f32[32,256]{1,0:T(8,128)S(1)} collective-permute-done((f32[32,256]{1,0:T(8,128)S(1)}, f32[32,256]{1,0:T(8,128)S(1)}, u32[]{:S(2)}, u32[]{:S(2)}) %collective-permute-start.9) | collective-permute-done | bytes 32800 | tf_op jit(solution)/shard_map/ppermute | solution.py:176
  158.2 3.3 %collective-permute-start.10 = (f32[32,256]{1,0:T(8,128)S(1)}, f32[32,256]{1,0:T(8,128)S(1)}, u32[]{:S(2)}, u32[]{:S(2)}) collective-permute-start(f32[32,256]{1,0:T(8,128)S(1)} %add.29), channel_id=1, source_target_pairs={{0,128},{128,0},{256,384},{384,256},{1,129},{129,1},{257,385},{385... | collective-permute-start | bytes 98312 | tf_op jit(solution)/shard_map/ppermute | solution.py:176
  161.4 6.1 %collective-permute-done.10 = f32[32,256]{1,0:T(8,128)S(1)} collective-permute-done((f32[32,256]{1,0:T(8,128)S(1)}, f32[32,256]{1,0:T(8,128)S(1)}, u32[]{:S(2)}, u32[]{:S(2)}) %collective-permute-start.10) | collective-permute-done | bytes 32800 | tf_op jit(solution)/shard_map/ppermute | solution.py:176
  167.5 5.9 %collective-permute-start.11 = (f32[32,256]{1,0:T(8,128)S(1)}, f32[32,256]{1,0:T(8,128)S(1)}, u32[]{:S(2)}, u32[]{:S(2)}) collective-permute-start(f32[32,256]{1,0:T(8,128)S(1)} %add.30), channel_id=1, source_target_pairs={{0,256},{128,384},{256,0},{384,128},{1,257},{129,385},{257,1},{385... | collective-permute-start | bytes 98312 | tf_op jit(solution)/shard_map/ppermute | solution.py:176
  173.4 2.9 %collective-permute-done.11 = f32[32,256]{1,0:T(8,128)S(1)} collective-permute-done((f32[32,256]{1,0:T(8,128)S(1)}, f32[32,256]{1,0:T(8,128)S(1)}, u32[]{:S(2)}, u32[]{:S(2)}) %collective-permute-start.11) | collective-permute-done | bytes 32800 | tf_op jit(solution)/shard_map/ppermute | solution.py:176
  176.3 4.4 %collective-permute-start.14 = (f32[32,256]{1,0:T(8,128)S(1)}, f32[32,256]{1,0:T(8,128)S(1)}, u32[]{:S(2)}, u32[]{:S(2)}) collective-permute-start(f32[32,256]{1,0:T(8,128)S(1)} %add.31.w0), channel_id=1, source_target_pairs={{0,96},{32,0},{64,32},{96,64},{1,97},{33,1},{65,33},{97,65},{2,98}... | collective-permute-start | bytes 98312 | tf_op jit(solution)/shard_map/ppermute | solution.py:180
  180.7 2.4 %collective-permute-start.13 = (f32[32,256]{1,0:T(8,128)S(1)}, f32[32,256]{1,0:T(8,128)S(1)}, u32[]{:S(2)}, u32[]{:S(2)}) collective-permute-start(f32[32,256]{1,0:T(8,128)S(1)} %add.31.w0), channel_id=1, source_target_pairs={{0,64},{32,96},{64,0},{96,32},{1,65},{33,97},{65,1},{97,33},{2,66}... | collective-permute-start | bytes 98312 | tf_op jit(solution)/shard_map/ppermute | solution.py:180
  183.1 2.6 %collective-permute-start.12 = (f32[32,256]{1,0:T(8,128)S(1)}, f32[32,256]{1,0:T(8,128)S(1)}, u32[]{:S(2)}, u32[]{:S(2)}) collective-permute-start(f32[32,256]{1,0:T(8,128)S(1)} %add.31.w0), channel_id=1, source_target_pairs={{0,32},{32,64},{64,96},{96,0},{1,33},{33,65},{65,97},{97,1},{2,34}... | collective-permute-start | bytes 98312 | tf_op jit(solution)/shard_map/ppermute | solution.py:180
  185.7 1.2 collective-permute-done.13.w2
  186.9 2.3 %collective-permute-done.12.w1 = f32[32,256]{1,0:T(8,128)S(1)} collective-permute-done((f32[32,256]{1,0:T(8,128)S(1)}, f32[32,256]{1,0:T(8,128)S(1)}, u32[]{:S(2)}, u32[]{:S(2)}) %collective-permute-start.12) | collective-permute-done | bytes 32800 | tf_op jit(solution)/shard_map/ppermute | solution.py:180
  189.2 0.6 shard_map.94
  189.7 4.5 %collective-permute-start.15 = (f32[4,32,256]{2,1,0:T(8,128)S(1)}, f32[4,32,256]{2,1,0:T(8,128)S(1)}, u32[]{:S(2)}, u32[]{:S(2)}) collective-permute-start(f32[4,32,256]{2,1,0:T(8,128)S(1)} %get-tuple-element.38.mine), channel_id=1, source_target_pairs={{0,1},{1,0},{2,3},{3,2},{4,5},{5,4},{6,7},{7,6},{8,9},{9,8},{10,11... | collective-permute-start | bytes 393224 | tf_op jit(solution)/shard_map/ppermute | solution.py:172
  194.2 1.0 shard_map.95
  195.2 1.3 shard_map.96
  (21 shorter events, 0.1 us)
Async XLA Ops:
  0.6 20.8 %copy-start.3 = (s32[1,1,96]{2,1,0:T(1,128)S(1)}, s32[1,1,96]{2,1,0:T(1,128)}, u32[]{:S(2)}) copy-start(s32[1,1,96]{2,1,0:T(1,128)} %param.10) | copy-start | bytes 1156
  0.6 20.7 %copy-start = (bf16[1,1,96,128,128]{4,3,2,1,0:T(8,128)(2,1)S(1)}, bf16[1,1,96,128,128]{4,3,2,1,0:T(8,128)(2,1)}, u32[]{:S(2)}) copy-start(bf16[1,1,96,128,128]{4,3,2,1,0:T(8,128)(2,1)} %param.9) | copy-start | bytes 9437188
  16.4 16.1 %all-to-all-start.1 = ((bf16[4,4,128,256]{3,2,1,0:T(8,128)(2,1)}), bf16[4,4,128,256]{3,2,1,0:T(8,128)(2,1)}, u32[]{:S(2)}, u32[]{:S(2)}) async-start(bf16[4,4,128,256]{3,2,1,0:T(8,128)(2,1)} %broadcast_in_dim.5), calls=%async_computation.1 | async-start | bytes 2097152 | tf_op jit(solution)/shard_map/all_to_all | solution.py:168
  34.4 8.4 %collective-permute-start = (bf16[16,128,256]{2,1,0:T(8,128)(2,1)S(1)}, bf16[16,128,256]{2,1,0:T(8,128)(2,1)S(1)}, u32[]{:S(2)}, u32[]{:S(2)}) collective-permute-start(bf16[16,128,256]{2,1,0:T(8,128)(2,1)S(1)} %shard_map.87), channel_id=1, source_target_pairs={{0,1},{1,0},{2,3},{3,2},{4,5},{5,4},{6,7},{7,6},{8,9},{9,8},{10,11... | collective-permute-start | bytes 3145736 | tf_op jit(solution)/shard_map/ppermute | solution.py:172
  42.5 42.4 %copy-start.1 = (bf16[256,256]{1,0:T(8,128)(2,1)S(1)}, bf16[256,256]{1,0:T(8,128)(2,1)}, u32[]{:S(2)}) copy-start(bf16[256,256]{1,0:T(8,128)(2,1)} %weight.3) | copy-start | bytes 393220
  42.5 42.4 %copy-start.2 = (bf16[128,256]{1,0:T(8,128)(2,1)S(1)}, bf16[128,256]{1,0:T(8,128)(2,1)}, u32[]{:S(2)}) copy-start(bf16[128,256]{1,0:T(8,128)(2,1)} %cotangent.1) | copy-start | bytes 196612
  86.4 45.0 %all-to-all-start.3 = ((bf16[16,256,128]{2,1,0:T(8,128)(2,1)}), bf16[16,256,128]{2,1,0:T(8,128)(2,1)S(1)}, u32[]{:S(2)}, u32[]{:S(2)}) async-start(bf16[16,256,128]{2,1,0:T(8,128)(2,1)} %get-tuple-element.32), calls=%async_computation.3 | async-start | bytes 2097152 | tf_op jit(solution)/shard_map/all_to_all | solution.py:168
  94.1 4.1 %collective-permute-start.1 = (f32[128,256]{1,0:T(8,128)S(1)}, f32[128,256]{1,0:T(8,128)S(1)}, u32[]{:S(2)}, u32[]{:S(2)}) collective-permute-start(f32[128,256]{1,0:T(8,128)S(1)} %get-tuple-element.27), channel_id=1, source_target_pairs={{0,1},{1,0},{2,3},{3,2},{4,5},{5,4},{6,7},{7,6},{8,9},{9,8},{10,11... | collective-permute-start | bytes 393224 | tf_op jit(solution)/shard_map/ppermute | solution.py:172
  98.8 8.4 %collective-permute-start.2 = (f32[32,256]{1,0:T(8,128)S(1)}, f32[32,256]{1,0:T(8,128)S(1)}, u32[]{:S(2)}, u32[]{:S(2)}) collective-permute-start(f32[32,256]{1,0:T(8,128)S(1)} %get-tuple-element.29), channel_id=1, source_target_pairs={{0,32},{32,64},{64,96},{96,0},{1,33},{33,65},{65,97},{97,1},{2,34}... | collective-permute-start | bytes 98312 | tf_op jit(solution)/shard_map/ppermute | solution.py:180
  100.7 6.5 %collective-permute-start.3 = (f32[32,256]{1,0:T(8,128)S(1)}, f32[32,256]{1,0:T(8,128)S(1)}, u32[]{:S(2)}, u32[]{:S(2)}) collective-permute-start(f32[32,256]{1,0:T(8,128)S(1)} %get-tuple-element.30), channel_id=1, source_target_pairs={{0,64},{32,96},{64,0},{96,32},{1,65},{33,97},{65,1},{97,33},{2,66}... | collective-permute-start | bytes 98312 | tf_op jit(solution)/shard_map/ppermute | solution.py:180
  103.4 6.0 %collective-permute-start.4 = (f32[32,256]{1,0:T(8,128)S(1)}, f32[32,256]{1,0:T(8,128)S(1)}, u32[]{:S(2)}, u32[]{:S(2)}) collective-permute-start(f32[32,256]{1,0:T(8,128)S(1)} %get-tuple-element.31), channel_id=1, source_target_pairs={{0,96},{32,0},{64,32},{96,64},{1,97},{33,1},{65,33},{97,65},{2,98}... | collective-permute-start | bytes 98312 | tf_op jit(solution)/shard_map/ppermute | solution.py:180
  109.4 16.8 %collective-permute-start.5 = (f32[32,256]{1,0:T(8,128)S(1)}, f32[32,256]{1,0:T(8,128)S(1)}, u32[]{:S(2)}, u32[]{:S(2)}) collective-permute-start(f32[32,256]{1,0:T(8,128)S(1)} %add_add_fusion), channel_id=1, source_target_pairs={{0,16},{16,0},{1,17},{17,1},{2,18},{18,2},{3,19},{19,3},{4,20},{20... | collective-permute-start | bytes 98312 | tf_op jit(solution)/shard_map/ppermute | solution.py:176
  126.2 5.2 %collective-permute-start.6 = (f32[32,256]{1,0:T(8,128)S(1)}, f32[32,256]{1,0:T(8,128)S(1)}, u32[]{:S(2)}, u32[]{:S(2)}) collective-permute-start(f32[32,256]{1,0:T(8,128)S(1)} %add.28.mine), channel_id=1, source_target_pairs={{0,2},{2,0},{4,6},{6,4},{8,10},{10,8},{12,14},{14,12},{1,3},{3,1},... | collective-permute-start | bytes 98312 | tf_op jit(solution)/shard_map/ppermute | solution.py:239
  131.4 9.0 %collective-permute-start.7 = (bf16[16,256,128]{2,1,0:T(8,128)(2,1)S(1)}, bf16[16,256,128]{2,1,0:T(8,128)(2,1)S(1)}, u32[]{:S(2)}, u32[]{:S(2)}) collective-permute-start(bf16[16,256,128]{2,1,0:T(8,128)(2,1)S(1)} %get-tuple-element.33.own), channel_id=1, source_target_pairs={{0,1},{1,0},{2,3},{3,2},{4,5},{5,4},{6,7},{7,6},{8,9},{9,8},{10,11... | collective-permute-start | bytes 3145736 | tf_op jit(solution)/shard_map/ppermute | solution.py:172
  134.8 5.7 %collective-permute-start.8 = (f32[32,256]{1,0:T(8,128)S(1)}, f32[32,256]{1,0:T(8,128)S(1)}, u32[]{:S(2)}, u32[]{:S(2)}) collective-permute-start(f32[32,256]{1,0:T(8,128)S(1)} %get-tuple-element.34.mine), channel_id=1, source_target_pairs={{0,4},{2,6},{4,0},{6,2},{8,12},{10,14},{12,8},{14,10},{1,5},{3,7},... | collective-permute-start | bytes 98312 | tf_op jit(solution)/shard_map/ppermute | solution.py:247
  143.9 45.3 %all-to-all-start.4 = ((bf16[16,256,128]{2,1,0:T(8,128)(2,1)}), bf16[16,256,128]{2,1,0:T(8,128)(2,1)S(1)}, u32[]{:S(2)}, u32[]{:S(2)}) async-start(bf16[16,256,128]{2,1,0:T(8,128)(2,1)} %get-tuple-element.36), calls=%async_computation.4 | async-start | bytes 2097152 | tf_op jit(solution)/shard_map/all_to_all | solution.py:168
  149.3 8.9 %collective-permute-start.9 = (f32[32,256]{1,0:T(8,128)S(1)}, f32[32,256]{1,0:T(8,128)S(1)}, u32[]{:S(2)}, u32[]{:S(2)}) collective-permute-start(f32[32,256]{1,0:T(8,128)S(1)} %get-tuple-element.35), channel_id=1, source_target_pairs={{0,8},{2,10},{4,12},{6,14},{8,0},{10,2},{12,4},{14,6},{1,9},{3,11}... | collective-permute-start | bytes 98312 | tf_op jit(solution)/shard_map/ppermute | solution.py:176
  158.2 9.3 %collective-permute-start.10 = (f32[32,256]{1,0:T(8,128)S(1)}, f32[32,256]{1,0:T(8,128)S(1)}, u32[]{:S(2)}, u32[]{:S(2)}) collective-permute-start(f32[32,256]{1,0:T(8,128)S(1)} %add.29), channel_id=1, source_target_pairs={{0,128},{128,0},{256,384},{384,256},{1,129},{129,1},{257,385},{385... | collective-permute-start | bytes 98312 | tf_op jit(solution)/shard_map/ppermute | solution.py:176
  167.5 8.8 %collective-permute-start.11 = (f32[32,256]{1,0:T(8,128)S(1)}, f32[32,256]{1,0:T(8,128)S(1)}, u32[]{:S(2)}, u32[]{:S(2)}) collective-permute-start(f32[32,256]{1,0:T(8,128)S(1)} %add.30), channel_id=1, source_target_pairs={{0,256},{128,384},{256,0},{384,128},{1,257},{129,385},{257,1},{385... | collective-permute-start | bytes 98312 | tf_op jit(solution)/shard_map/ppermute | solution.py:176
  176.3 9.4 %collective-permute-start.14 = (f32[32,256]{1,0:T(8,128)S(1)}, f32[32,256]{1,0:T(8,128)S(1)}, u32[]{:S(2)}, u32[]{:S(2)}) collective-permute-start(f32[32,256]{1,0:T(8,128)S(1)} %add.31.w0), channel_id=1, source_target_pairs={{0,96},{32,0},{64,32},{96,64},{1,97},{33,1},{65,33},{97,65},{2,98}... | collective-permute-start | bytes 98312 | tf_op jit(solution)/shard_map/ppermute | solution.py:180
  180.7 6.2 %collective-permute-start.13 = (f32[32,256]{1,0:T(8,128)S(1)}, f32[32,256]{1,0:T(8,128)S(1)}, u32[]{:S(2)}, u32[]{:S(2)}) collective-permute-start(f32[32,256]{1,0:T(8,128)S(1)} %add.31.w0), channel_id=1, source_target_pairs={{0,64},{32,96},{64,0},{96,32},{1,65},{33,97},{65,1},{97,33},{2,66}... | collective-permute-start | bytes 98312 | tf_op jit(solution)/shard_map/ppermute | solution.py:180
  183.1 6.1 %collective-permute-start.12 = (f32[32,256]{1,0:T(8,128)S(1)}, f32[32,256]{1,0:T(8,128)S(1)}, u32[]{:S(2)}, u32[]{:S(2)}) collective-permute-start(f32[32,256]{1,0:T(8,128)S(1)} %add.31.w0), channel_id=1, source_target_pairs={{0,32},{32,64},{64,96},{96,0},{1,33},{33,65},{65,97},{97,1},{2,34}... | collective-permute-start | bytes 98312 | tf_op jit(solution)/shard_map/ppermute | solution.py:180
  189.7 5.5 %collective-permute-start.15 = (f32[4,32,256]{2,1,0:T(8,128)S(1)}, f32[4,32,256]{2,1,0:T(8,128)S(1)}, u32[]{:S(2)}, u32[]{:S(2)}) collective-permute-start(f32[4,32,256]{2,1,0:T(8,128)S(1)} %get-tuple-element.38.mine), channel_id=1, source_target_pairs={{0,1},{1,0},{2,3},{3,2},{4,5},{5,4},{6,7},{7,6},{8,9},{9,8},{10,11... | collective-permute-start | bytes 393224 | tf_op jit(solution)/shard_map/ppermute | solution.py:172

commit v8 on v4

--- a/solution.py
+++ b/solution.py
@@ -23,7 +23,7 @@
 
 
 def plan_kernel(place, info, blocks, lists, groups):
-    count, core, xi, zi = info[0], info[1], info[2], info[3]
+    count, core = info[0], info[1]
 
     def write(at, k, t, source, half, target):
         for f, value in enumerate((k, t, source, half, target)):
@@ -35,7 +35,7 @@
         z, x = a >> 2, a & 3
         half = t >> 1
         source = (x << 2) + z
-        target = (((x - xi) & 3) << 2) + ((z - zi) & 3)
+        target = a
         mine, theirs = held
         away = (t & 1) ^ core
         write(jnp.where(away == 0, mine, SLOTS + theirs), k, half, source, half, target)
@@ -89,11 +89,6 @@
         spread[s, 288:320, :] = grad[rows, 128:256]
 
 
-def split(value):
-    high = value.astype(BF)
-    return high, (value - high.astype(F32)).astype(BF)
-
-
 def back_products(which, lists, groups, blocks, source, acc):
     def step(i, _):
         products = []
@@ -113,50 +108,26 @@
     back_products(0, lists, groups, blocks, own, acc)
 
 
-def backward_other_kernel(lists, groups, blocks, own, other, begun, b0, b1, b2, b3, acc):
+def backward_other_kernel(lists, groups, blocks, own, other, begun, out, grad_out, acc):
     back_products(1, lists, groups, blocks, other, acc)
+    out[...] = acc[0:16].astype(BF)
     grad = jnp.zeros((64, 128), F32)
     for s in range(16):
         grad += own[s, 256:320, :].astype(F32) + other[s, 256:320, :].astype(F32)
-    high, low = split(grad)
-    for x, out in enumerate((b0, b1, b2, b3)):
-        for z in range(4):
-            out[256 * z : 256 * z + 256, :] = acc[4 * x + z].astype(BF)
-        out[1024:1088, :] = high
-        out[1088:1152, :] = low
-
-
-def ordered_sum(me, parts, row, scratch):
-    for k, part in enumerate(parts):
-        high, low = part[row : row + 64, :], part[row + 64 : row + 128, :]
-        scratch[(me - k) & 3] = high.astype(F32) + low.astype(F32)
-    return scratch[0] + scratch[1] + scratch[2] + scratch[3]
-
-
-def fold_kernel(info, b0, b1, b2, b3, f0, f1, f2, f3, scratch):
-    parts = (b0, b1, b2, b3)
-    high, low = split(ordered_sum(info[2], parts, 1024, scratch))
-    for z, out in enumerate((f0, f1, f2, f3)):
-        rows = slice(256 * z, 256 * z + 256)
-        total = parts[0][rows, :].astype(F32)
-        for part in parts[1:]:
-            total += part[rows, :].astype(F32)
-        out[0:256, :] = total.astype(BF)
-        out[256:320, :] = high
-        out[320:384, :] = low
-
-
-def grad_kernel(scale, info, f0, f1, f2, f3, grad_out, scratch):
-    grad = (ordered_sum(info[3], (f0, f1, f2, f3), 256, scratch) * scale).astype(BF)
+    grad_out[...] = grad
+
+
+def gate_kernel(scale, total, parts, out, held):
+    grad = (total[...] * scale).astype(BF)
     for s in range(8):
-        grad_out[s, :, 0:128] = grad[0:32]
-        grad_out[s, :, 128:256] = grad[32:64]
-
-
-def last_kernel(f0, f1, f2, f3, weight, input_grad):
-    total = f0[0:256, :].astype(F32)
-    for part in (f1, f2, f3):
-        total += part[0:256, :].astype(F32)
+        out[s, :, 0:128] = grad[0:32]
+        out[s, :, 128:256] = grad[32:64]
+
+
+def last_kernel(parts, weight, input_grad):
+    total = parts[0].astype(F32)
+    for s in range(1, 16):
+        total += parts[s].astype(F32)
     back = total.astype(BF).astype(F32).T.astype(BF)
     input_grad[...] = dot(back, weight[...], (((1,), (1,)), ((), ()))).astype(BF)
 
@@ -182,8 +153,8 @@
     return lax.ppermute(value, "c", [(0, 1), (1, 0)])
 
 
-def rotate(value, axis, k):
-    return lax.ppermute(value, axis, [(i, (i + k) % 4) for i in range(4)])
+def paired_sum(value, axis, k):
+    return value + lax.ppermute(value, axis, [(i, i ^ k) for i in range(4)])
 
 
 def shards(features, weight, cotangent, blocks, block_pos, counts):
@@ -228,29 +199,24 @@
         [SMEM, SMEM, VMEM, VMEM],
         **heavy,
     )(lists, groups, tile, own)
-    back = call(
+    back, total, _ = call(
         backward_other_kernel,
-        [((1152, 128), BF, VMEM)] * 4 + [((17, 256, 128), F32, VMEM)],
+        [((16, 256, 128), BF, VMEM), ((64, 128), F32, VMEM), ((17, 256, 128), F32, VMEM)],
         [SMEM, SMEM] + [VMEM] * 4,
-        alias={5: 4},
+        alias={5: 2},
         **heavy,
     )(lists, groups, tile, own, other, begun)
-    back = [back[0]] + [rotate(back[k], "x", k) for k in (1, 2, 3)]
-    folded = call(
-        fold_kernel,
-        [((384, 128), BF, VMEM)] * 4,
-        [SMEM] + [VMEM] * 4,
-        [pltpu.VMEM((4, 64, 128), F32)],
-    )(info, *back)
-    folded = [folded[0]] + [rotate(folded[k], "zl", k) for k in (1, 2, 3)]
-    (grad,) = call(
-        functools.partial(grad_kernel, 1.0 / math.sqrt(nodes_total)),
-        [((8, 32, 256), BF, VMEM)],
-        [SMEM] + [VMEM] * 4,
-        [pltpu.VMEM((4, 64, 128), F32)],
-    )(info, *folded)
+    parts = exchange(back, ("zl", "x"))
+    for axis in ("x", "zl"):
+        total = paired_sum(paired_sum(total, axis, 1), axis, 2)
+    grad, parts = call(
+        functools.partial(gate_kernel, 1.0 / math.sqrt(nodes_total)),
+        [((8, 32, 256), BF, VMEM), ((16, 256, 128), BF, VMEM)],
+        [VMEM, VMEM],
+        alias={1: 1},
+    )(total, parts)
     weight_grad = exchange(grad, "y").reshape(256, 256).astype(F32)
-    (input_grad,) = call(last_kernel, [((128, 256), BF, VMEM)], [VMEM] * 5, flops=2**24, size=2**20)(*folded, weight)
+    (input_grad,) = call(last_kernel, [((128, 256), BF, VMEM)], [VMEM] * 2, flops=2**24, size=2**20)(parts, weight)
     return (output, input_grad, weight_grad)
 
 

time: 190 us -> 190 us (level)
  waiting for transfers between devices: 31.4 us -> 39.2 us
  starting transfers between devices: 33.4 us -> 28.6 us
  Pallas kernels: 19.8 us -> 16 us
    ppermute x6 -> x4, starting transfers between devices: 19.4 us -> 8.81 us  [paired_sum(): return value + lax.ppermute(value, axis, [(i, i ^ k) for i in range(4)])]
    ppermute x6 -> x4, waiting for transfers between devices: 15.8 us -> 22.5 us  [paired_sum(): return value + lax.ppermute(value, axis, [(i, i ^ k) for i in range(4)])]
    all_to_all x2 -> x3, starting transfers between devices: 10.1 us -> 16 us  [exchange(): return lax.all_to_all(value, axes, 0, 0, tiled=True)]
    all_to_all x2 -> x3, waiting for transfers between devices: 15.5 us -> 16.3 us  [exchange(): return lax.all_to_all(value, axes, 0, 0, tiled=True)]
    pallas_call x4 -> x3, Pallas kernels: 6.2 us -> 5.51 us  [the longest x1 3.89 us: shards(): call(backward_other_kernel, [((16, 256, 128), BF, VMEM), ((64, 128), F32,...]
  transfers between devices with their start and end apart: 10 -> 9, of which waited for: 7 -> 8; matrix products, arithmetic and copies ran while one was open for 0% -> 0% of each run, Pallas kernels for 6% -> 4%
where the time goes in v8:
time: 190 us; the launch traced here: 189 us
  blocking collectives  101 us (53%)
  waiting for transfers between devices  39.2 us (21%)
  starting transfers between devices  28.6 us (15%)
  Pallas kernels  16 us (8%)
  local copies, waits for them, and re-layouts  2.12 us (1%)
    all_to_all x3, blocking collectives, exchange(): return lax.all_to_all(value, axes, 0, 0, tiled=True)  101 us
    ppermute x4, waiting for transfers between devices, paired_sum(): return value + lax.ppermute(value, axis, [(i, i ^ k) for i in range(4)])  22.5 us
    all_to_all x3, waiting for transfers between devices, exchange(): return lax.all_to_all(value, axes, 0, 0, tiled=True)  16.3 us
    all_to_all x3, starting transfers between devices, exchange(): return lax.all_to_all(value, axes, 0, 0, tiled=True)  16 us
    ppermute x4, starting transfers between devices, paired_sum(): return value + lax.ppermute(value, axis, [(i, i ^ k) for i in range(4)])  8.81 us
    pallas_call x2, Pallas kernels, shards(): call(functools.partial(forward_kernel, which), [((16, 128, 256), BF, VMEM...  4.7 us
    pallas_call x1, Pallas kernels, shards(): call(backward_other_kernel, [((16, 256, 128), BF, VMEM), ((64, 128), F32,...  3.89 us
    ppermute x2, starting transfers between devices, swap(): return lax.ppermute(value, 'c', [(0, 1), (1, 0)])  3.83 us
  transfers between devices with their start and end apart: 9, of which 8 were waited for; matrix products, arithmetic and copies ran while one was open for 0% of the time, Pallas kernels for 4%

profile of v8, /device:TPU:6, one launch (start us, length us, event | category | flops | bytes accessed | tf_op | source)
XLA Modules:
  0.0 189.3 jit_solution(3028144946411304671)
XLA Ops:
  0.6 0.0 copy-start.3
  0.6 0.0 copy-start
  0.7 1.0 broadcast_in_dim.4
  1.7 15.9 %all_to_all.30 = bf16[4,128,256]{2,1,0:T(8,128)(2,1)S(1)} all-to-all(bf16[4,128,256]{2,1,0:T(8,128)(2,1)S(1)} %broadcast_in_dim.4), channel_id=1, replica_groups=mesh['zl'=4,'x'=4,'zh'=2,'y'=8,'c'=2] {'zl'}, dimensions={0} | all-to-all | bytes 524288 | tf_op jit(solution)/shard_map/all_to_all | solution.py:149
  17.6 1.1 broadcast_in_dim.5
  18.7 4.8 %all-to-all-start.1 = ((bf16[4,4,128,256]{3,2,1,0:T(8,128)(2,1)}), bf16[4,4,128,256]{3,2,1,0:T(8,128)(2,1)}, u32[]{:S(2)}, u32[]{:S(2)}) async-start(bf16[4,4,128,256]{3,2,1,0:T(8,128)(2,1)} %broadcast_in_dim.5), calls=%async_computation.1 | async-start | bytes 2097152 | tf_op jit(solution)/shard_map/all_to_all | solution.py:149
  24.1 0.1 pad_add_fusion.info
  24.2 0.0 copy-done.3
  24.2 0.0 copy-done
  24.2 1.9 %shard_map.85 = (s32[1120]{0:T(1024)S(1)}, s32[2]{0:T(128)S(1)}) custom-call(s32[96]{0:T(128)S(1)} %bitcast.16, s32[4]{0:T(128)S(1)} %pad_add_fusion.info, bf16[96,128,128]{2,1,0:T(8,128)(2,1)S(1)} %bitcast.13), custom_call_target="tpu_custom_call" | custom-call | bytes 1048576 | tf_op jit(solution)/shard_map/pallas_call | solution.py:168
  26.1 8.2 %all-to-all-done.1 = bf16[4,4,128,256]{3,2,1,0:T(8,128)(2,1)} async-done(((bf16[4,4,128,256]{3,2,1,0:T(8,128)(2,1)}), bf16[4,4,128,256]{3,2,1,0:T(8,128)(2,1)}, u32[]{:S(2)}, u32[]{:S(2)}) %all-to-all-start.1) | async-done | bytes 1048608 | tf_op jit(solution)/shard_map/all_to_all | solution.py:149
  34.3 2.4 %shard_map.87 = bf16[16,128,256]{2,1,0:T(8,128)(2,1)S(1)} custom-call(s32[1120]{0:T(1024)S(1)} %get-tuple-element.11.lists, s32[2]{0:T(128)S(1)} %get-tuple-element.12.groups, bf16[96,128,128]{2,1,0:T(8,128)(2,1)S(1)} %bitcast.14, bf16[16,128,256]{2,1,0:T(8,128)(2,1)} %bitcast.6.nodes), custom_call_target="tpu_custom_call" | custom-call | flops 800000000 | bytes 6291456 | tf_op jit(solution)/shard_map/pallas_call | solution.py:178
  36.7 1.9 %collective-permute-start = (bf16[16,128,256]{2,1,0:T(8,128)(2,1)S(1)}, bf16[16,128,256]{2,1,0:T(8,128)(2,1)S(1)}, u32[]{:S(2)}, u32[]{:S(2)}) collective-permute-start(bf16[16,128,256]{2,1,0:T(8,128)(2,1)S(1)} %shard_map.87), channel_id=1, source_target_pairs={{0,1},{1,0},{2,3},{3,2},{4,5},{5,4},{6,7},{7,6},{8,9},{9,8},{10,11... | collective-permute-start | bytes 3145736 | tf_op jit(solution)/shard_map/ppermute | solution.py:153
  38.6 2.4 %shard_map.86 = bf16[16,128,256]{2,1,0:T(8,128)(2,1)S(1)} custom-call(s32[1120]{0:T(1024)S(1)} %get-tuple-element.11.lists, s32[2]{0:T(128)S(1)} %get-tuple-element.12.groups, bf16[96,128,128]{2,1,0:T(8,128)(2,1)S(1)} %bitcast.15, bf16[16,128,256]{2,1,0:T(8,128)(2,1)} %bitcast.6.nodes), custom_call_target="tpu_custom_call" | custom-call | flops 800000000 | bytes 6291456 | tf_op jit(solution)/shard_map/pallas_call | solution.py:178
  41.0 0.0 copy-start.1
  41.0 0.0 copy-start.2
  41.0 0.2 collective-permute-done
  41.3 0.3 add_convert_fusion
  41.6 43.8 %all_to_all.31.parts = bf16[16,128,256]{2,1,0:T(8,128)(2,1)S(1)} all-to-all(bf16[16,128,256]{2,1,0:T(8,128)(2,1)S(1)} %add_convert_fusion), channel_id=1, replica_groups=mesh['zl'=4,'x'=4,'zh'=2,'y'=8,'c'=2] {'zh','y'}, dimensions={0} | all-to-all | bytes 2097152 | tf_op jit(solution)/shard_map/all_to_all | solution.py:149
  85.4 0.0 copy-done.1
  85.4 0.0 copy-done.2
  85.4 0.9 shard_map.88
  86.3 41.1 %all_to_all.32.own = bf16[16,320,128]{2,1,0:T(8,128)(2,1)S(1)} all-to-all(bf16[16,320,128]{2,1,0:T(8,128)(2,1)S(1)} %get-tuple-element.14), channel_id=1, replica_groups=mesh['zl'=4,'x'=4,'zh'=2,'y'=8,'c'=2] {'zh','y'}, dimensions={0} | all-to-all | bytes 2621440 | tf_op jit(solution)/shard_map/all_to_all | solution.py:149
  127.4 1.9 %collective-permute-start.1 = (bf16[16,320,128]{2,1,0:T(8,128)(2,1)S(1)}, bf16[16,320,128]{2,1,0:T(8,128)(2,1)S(1)}, u32[]{:S(2)}, u32[]{:S(2)}) collective-permute-start(bf16[16,320,128]{2,1,0:T(8,128)(2,1)S(1)} %all_to_all.32.own), channel_id=1, source_target_pairs={{0,1},{1,0},{2,3},{3,2},{4,5},{5,4},{6,7},{7,6},{8,9},{9,8},{10,11... | collective-permute-start | bytes 3932168 | tf_op jit(solution)/shard_map/ppermute | solution.py:153
  129.4 2.9 %shard_map.89.begun = f32[17,256,128]{2,1,0:T(8,128)S(1)} custom-call(s32[1120]{0:T(1024)S(1)} %get-tuple-element.11.lists, s32[2]{0:T(128)S(1)} %get-tuple-element.12.groups, bf16[96,128,128]{2,1,0:T(8,128)(2,1)} %bitcast.11, bf16[16,320,128]{2,1,0:T(8,128)(2,1)S(1)} %all_to_all.32.own), custom_call_target="tpu_custom_call" | custom-call | flops 800000000 | bytes 6291456 | tf_op jit(solution)/shard_map/pallas_call | solution.py:196
  132.3 0.1 collective-permute-done.1.other
  132.4 3.9 %shard_map.90 = (bf16[16,256,128]{2,1,0:T(8,128)(2,1)}, f32[64,128]{1,0:T(8,128)S(1)}, f32[17,256,128]{2,1,0:T(8,128)S(1)}) custom-call(s32[1120]{0:T(1024)S(1)} %get-tuple-element.11.lists, s32[2]{0:T(128)S(1)} %get-tuple-element.12.groups, bf16[96,128,128]{2,1,0:T(8,128)(2,1)} %bitcast.12, ...), custom_call_target="tpu_custom_call", output_to_operand_aliasing={{2}: (5, {})} | custom-call | flops 800000000 | bytes 6291456 | tf_op jit(solution)/shard_map/pallas_call | solution.py:202
  136.2 7.5 %all-to-all-start.4 = ((bf16[16,256,128]{2,1,0:T(8,128)(2,1)}), bf16[16,256,128]{2,1,0:T(8,128)(2,1)S(1)}, u32[]{:S(2)}, u32[]{:S(2)}) async-start(bf16[16,256,128]{2,1,0:T(8,128)(2,1)} %get-tuple-element.16), calls=%async_computation.4 | async-start | bytes 2097152 | tf_op jit(solution)/shard_map/all_to_all | solution.py:149
  143.7 2.8 %collective-permute-start.2 = (f32[64,128]{1,0:T(8,128)S(1)}, f32[64,128]{1,0:T(8,128)S(1)}, u32[]{:S(2)}, u32[]{:S(2)}) collective-permute-start(f32[64,128]{1,0:T(8,128)S(1)} %get-tuple-element.15), channel_id=1, source_target_pairs={{0,32},{32,0},{64,96},{96,64},{1,33},{33,1},{65,97},{97,65},{2,34}... | collective-permute-start | bytes 98312 | tf_op jit(solution)/shard_map/ppermute | solution.py:157
  146.5 5.5 %collective-permute-done.2 = f32[64,128]{1,0:T(8,128)S(1)} collective-permute-done((f32[64,128]{1,0:T(8,128)S(1)}, f32[64,128]{1,0:T(8,128)S(1)}, u32[]{:S(2)}, u32[]{:S(2)}) %collective-permute-start.2) | collective-permute-done | bytes 32800 | tf_op jit(solution)/shard_map/ppermute | solution.py:157
  152.0 1.9 %collective-permute-start.3 = (f32[64,128]{1,0:T(8,128)S(1)}, f32[64,128]{1,0:T(8,128)S(1)}, u32[]{:S(2)}, u32[]{:S(2)}) collective-permute-start(f32[64,128]{1,0:T(8,128)S(1)} %add.16), channel_id=1, source_target_pairs={{0,64},{32,96},{64,0},{96,32},{1,65},{33,97},{65,1},{97,33},{2,66}... | collective-permute-start | bytes 98312 | tf_op jit(solution)/shard_map/ppermute | solution.py:157
  153.9 6.9 %collective-permute-done.3 = f32[64,128]{1,0:T(8,128)S(1)} collective-permute-done((f32[64,128]{1,0:T(8,128)S(1)}, f32[64,128]{1,0:T(8,128)S(1)}, u32[]{:S(2)}, u32[]{:S(2)}) %collective-permute-start.3) | collective-permute-done | bytes 32800 | tf_op jit(solution)/shard_map/ppermute | solution.py:157
  160.8 1.9 %collective-permute-start.4 = (f32[64,128]{1,0:T(8,128)S(1)}, f32[64,128]{1,0:T(8,128)S(1)}, u32[]{:S(2)}, u32[]{:S(2)}) collective-permute-start(f32[64,128]{1,0:T(8,128)S(1)} %add.17), channel_id=1, source_target_pairs={{0,128},{128,0},{256,384},{384,256},{1,129},{129,1},{257,385},{385... | collective-permute-start | bytes 98312 | tf_op jit(solution)/shard_map/ppermute | solution.py:157
  162.7 5.7 %collective-permute-done.4 = f32[64,128]{1,0:T(8,128)S(1)} collective-permute-done((f32[64,128]{1,0:T(8,128)S(1)}, f32[64,128]{1,0:T(8,128)S(1)}, u32[]{:S(2)}, u32[]{:S(2)}) %collective-permute-start.4) | collective-permute-done | bytes 32800 | tf_op jit(solution)/shard_map/ppermute | solution.py:157
  168.4 2.2 %collective-permute-start.5 = (f32[64,128]{1,0:T(8,128)S(1)}, f32[64,128]{1,0:T(8,128)S(1)}, u32[]{:S(2)}, u32[]{:S(2)}) collective-permute-start(f32[64,128]{1,0:T(8,128)S(1)} %add.18), channel_id=1, source_target_pairs={{0,256},{128,384},{256,0},{384,128},{1,257},{129,385},{257,1},{385... | collective-permute-start | bytes 98312 | tf_op jit(solution)/shard_map/ppermute | solution.py:157
  170.6 4.5 %collective-permute-done.5 = f32[64,128]{1,0:T(8,128)S(1)} collective-permute-done((f32[64,128]{1,0:T(8,128)S(1)}, f32[64,128]{1,0:T(8,128)S(1)}, u32[]{:S(2)}, u32[]{:S(2)}) %collective-permute-start.5) | collective-permute-done | bytes 32800 | tf_op jit(solution)/shard_map/ppermute | solution.py:157
  175.1 0.0 all-to-all-done.4.parts
  175.1 0.7 shard_map.91
  175.7 3.8 %all-to-all-start.5 = ((bf16[8,32,256]{2,1,0:T(8,128)(2,1)}), bf16[8,32,256]{2,1,0:T(8,128)(2,1)S(1)}, u32[]{:S(2)}, u32[]{:S(2)}) async-start(bf16[8,32,256]{2,1,0:T(8,128)(2,1)} %get-tuple-element.18), calls=%async_computation.5 | async-start | bytes 262144 | tf_op jit(solution)/shard_map/all_to_all | solution.py:149
  179.5 1.0 shard_map.92
  180.5 8.1 %all-to-all-done.5 = bf16[8,32,256]{2,1,0:T(8,128)(2,1)S(1)} async-done(((bf16[8,32,256]{2,1,0:T(8,128)(2,1)}), bf16[8,32,256]{2,1,0:T(8,128)(2,1)S(1)}, u32[]{:S(2)}, u32[]{:S(2)}) %all-to-all-start.5) | async-done | bytes 131104 | tf_op jit(solution)/shard_map/all_to_all | solution.py:149
  188.6 0.7 bitcast_convert_fusion
  (4 shorter events, 0.0 us)
Async XLA Ops:
  0.6 23.6 %copy-start.3 = (s32[1,1,96]{2,1,0:T(1,128)S(1)}, s32[1,1,96]{2,1,0:T(1,128)}, u32[]{:S(2)}) copy-start(s32[1,1,96]{2,1,0:T(1,128)} %param.10) | copy-start | bytes 1156
  0.6 23.5 %copy-start = (bf16[1,1,96,128,128]{4,3,2,1,0:T(8,128)(2,1)S(1)}, bf16[1,1,96,128,128]{4,3,2,1,0:T(8,128)(2,1)}, u32[]{:S(2)}) copy-start(bf16[1,1,96,128,128]{4,3,2,1,0:T(8,128)(2,1)} %param.9) | copy-start | bytes 9437188
  18.7 15.7 %all-to-all-start.1 = ((bf16[4,4,128,256]{3,2,1,0:T(8,128)(2,1)}), bf16[4,4,128,256]{3,2,1,0:T(8,128)(2,1)}, u32[]{:S(2)}, u32[]{:S(2)}) async-start(bf16[4,4,128,256]{3,2,1,0:T(8,128)(2,1)} %broadcast_in_dim.5), calls=%async_computation.1 | async-start | bytes 2097152 | tf_op jit(solution)/shard_map/all_to_all | solution.py:149
  36.7 4.6 %collective-permute-start = (bf16[16,128,256]{2,1,0:T(8,128)(2,1)S(1)}, bf16[16,128,256]{2,1,0:T(8,128)(2,1)S(1)}, u32[]{:S(2)}, u32[]{:S(2)}) collective-permute-start(bf16[16,128,256]{2,1,0:T(8,128)(2,1)S(1)} %shard_map.87), channel_id=1, source_target_pairs={{0,1},{1,0},{2,3},{3,2},{4,5},{5,4},{6,7},{7,6},{8,9},{9,8},{10,11... | collective-permute-start | bytes 3145736 | tf_op jit(solution)/shard_map/ppermute | solution.py:153
  41.0 44.4 %copy-start.1 = (bf16[256,256]{1,0:T(8,128)(2,1)S(1)}, bf16[256,256]{1,0:T(8,128)(2,1)}, u32[]{:S(2)}) copy-start(bf16[256,256]{1,0:T(8,128)(2,1)} %weight.3) | copy-start | bytes 393220
  41.0 44.4 %copy-start.2 = (bf16[128,256]{1,0:T(8,128)(2,1)S(1)}, bf16[128,256]{1,0:T(8,128)(2,1)}, u32[]{:S(2)}) copy-start(bf16[128,256]{1,0:T(8,128)(2,1)} %cotangent.1) | copy-start | bytes 196612
  127.4 4.9 %collective-permute-start.1 = (bf16[16,320,128]{2,1,0:T(8,128)(2,1)S(1)}, bf16[16,320,128]{2,1,0:T(8,128)(2,1)S(1)}, u32[]{:S(2)}, u32[]{:S(2)}) collective-permute-start(bf16[16,320,128]{2,1,0:T(8,128)(2,1)S(1)} %all_to_all.32.own), channel_id=1, source_target_pairs={{0,1},{1,0},{2,3},{3,2},{4,5},{5,4},{6,7},{7,6},{8,9},{9,8},{10,11... | collective-permute-start | bytes 3932168 | tf_op jit(solution)/shard_map/ppermute | solution.py:153
  136.2 38.8 %all-to-all-start.4 = ((bf16[16,256,128]{2,1,0:T(8,128)(2,1)}), bf16[16,256,128]{2,1,0:T(8,128)(2,1)S(1)}, u32[]{:S(2)}, u32[]{:S(2)}) async-start(bf16[16,256,128]{2,1,0:T(8,128)(2,1)} %get-tuple-element.16), calls=%async_computation.4 | async-start | bytes 2097152 | tf_op jit(solution)/shard_map/all_to_all | solution.py:149
  143.7 8.3 %collective-permute-start.2 = (f32[64,128]{1,0:T(8,128)S(1)}, f32[64,128]{1,0:T(8,128)S(1)}, u32[]{:S(2)}, u32[]{:S(2)}) collective-permute-start(f32[64,128]{1,0:T(8,128)S(1)} %get-tuple-element.15), channel_id=1, source_target_pairs={{0,32},{32,0},{64,96},{96,64},{1,33},{33,1},{65,97},{97,65},{2,34}... | collective-permute-start | bytes 98312 | tf_op jit(solution)/shard_map/ppermute | solution.py:157
  152.0 8.8 %collective-permute-start.3 = (f32[64,128]{1,0:T(8,128)S(1)}, f32[64,128]{1,0:T(8,128)S(1)}, u32[]{:S(2)}, u32[]{:S(2)}) collective-permute-start(f32[64,128]{1,0:T(8,128)S(1)} %add.16), channel_id=1, source_target_pairs={{0,64},{32,96},{64,0},{96,32},{1,65},{33,97},{65,1},{97,33},{2,66}... | collective-permute-start | bytes 98312 | tf_op jit(solution)/shard_map/ppermute | solution.py:157
  160.8 7.6 %collective-permute-start.4 = (f32[64,128]{1,0:T(8,128)S(1)}, f32[64,128]{1,0:T(8,128)S(1)}, u32[]{:S(2)}, u32[]{:S(2)}) collective-permute-start(f32[64,128]{1,0:T(8,128)S(1)} %add.17), channel_id=1, source_target_pairs={{0,128},{128,0},{256,384},{384,256},{1,129},{129,1},{257,385},{385... | collective-permute-start | bytes 98312 | tf_op jit(solution)/shard_map/ppermute | solution.py:157
  168.4 6.7 %collective-permute-start.5 = (f32[64,128]{1,0:T(8,128)S(1)}, f32[64,128]{1,0:T(8,128)S(1)}, u32[]{:S(2)}, u32[]{:S(2)}) collective-permute-start(f32[64,128]{1,0:T(8,128)S(1)} %add.18), channel_id=1, source_target_pairs={{0,256},{128,384},{256,0},{384,128},{1,257},{129,385},{257,1},{385... | collective-permute-start | bytes 98312 | tf_op jit(solution)/shard_map/ppermute | solution.py:157
  175.7 12.8 %all-to-all-start.5 = ((bf16[8,32,256]{2,1,0:T(8,128)(2,1)}), bf16[8,32,256]{2,1,0:T(8,128)(2,1)S(1)}, u32[]{:S(2)}, u32[]{:S(2)}) async-start(bf16[8,32,256]{2,1,0:T(8,128)(2,1)} %get-tuple-element.18), calls=%async_computation.5 | async-start | bytes 262144 | tf_op jit(solution)/shard_map/all_to_all | solution.py:149

commit v9 on v8

--- a/solution.py
+++ b/solution.py
@@ -32,13 +32,10 @@
     def step(k, held):
         p = place[k]
         t, a = p >> 4, p & 15
-        z, x = a >> 2, a & 3
         half = t >> 1
-        source = (x << 2) + z
-        target = a
         mine, theirs = held
         away = (t & 1) ^ core
-        write(jnp.where(away == 0, mine, SLOTS + theirs), k, half, source, half, target)
+        write(jnp.where(away == 0, mine, SLOTS + theirs), k, half, a, half, a)
         return mine + 1 - away, theirs + away
 
     mine, theirs = lax.fori_loop(0, count, step, (jnp.int32(0), jnp.int32(0)))
@@ -103,18 +100,19 @@
     lax.fori_loop(0, groups[which], step, 0)
 
 
-def backward_own_kernel(lists, groups, blocks, own, acc):
+def backward_own_kernel(lists, groups, blocks, own, acc, grad_out):
+    grad = own[0, 256:320, :].astype(F32)
+    for s in range(1, 16):
+        grad += own[s, 256:320, :].astype(F32)
+    grad_out[...] = grad
     acc[...] = jnp.zeros_like(acc)
     back_products(0, lists, groups, blocks, own, acc)
 
 
-def backward_other_kernel(lists, groups, blocks, own, other, begun, out, grad_out, acc):
+def backward_other_kernel(lists, groups, blocks, other, mine, theirs, begun, out, total, acc):
+    total[...] = mine[...] + theirs[...]
     back_products(1, lists, groups, blocks, other, acc)
     out[...] = acc[0:16].astype(BF)
-    grad = jnp.zeros((64, 128), F32)
-    for s in range(16):
-        grad += own[s, 256:320, :].astype(F32) + other[s, 256:320, :].astype(F32)
-    grad_out[...] = grad
 
 
 def gate_kernel(scale, total, parts, out, held):
@@ -153,8 +151,8 @@
     return lax.ppermute(value, "c", [(0, 1), (1, 0)])
 
 
-def paired_sum(value, axis, k):
-    return value + lax.ppermute(value, axis, [(i, i ^ k) for i in range(4)])
+def paired(value, axis, k):
+    return lax.ppermute(value, axis, [(i, i ^ k) for i in range(4)])
 
 
 def shards(features, weight, cotangent, blocks, block_pos, counts):
@@ -172,8 +170,7 @@
         size=2**20,
     )(block_pos[0, 0], info, tile)
 
-    line = exchange(jnp.broadcast_to(features[None], (4, 128, 256)), "zl")
-    nodes = exchange(jnp.broadcast_to(line[None], (4, 4, 128, 256)), "x").reshape(16, 128, 256)
+    nodes = exchange(jnp.broadcast_to(features[None], (16, 128, 256)), ("zl", "x"))
     send, keep = [
         call(
             functools.partial(forward_kernel, which),
@@ -193,22 +190,23 @@
     )(parts, weight, cotangent)
     own = exchange(spread, ("zh", "y"))
     other = swap(own)
-    (begun,) = call(
+    begun, total = call(
         backward_own_kernel,
-        [((17, 256, 128), F32, VMEM)],
+        [((17, 256, 128), F32, VMEM), ((64, 128), F32, VMEM)],
         [SMEM, SMEM, VMEM, VMEM],
         **heavy,
     )(lists, groups, tile, own)
     back, total, _ = call(
         backward_other_kernel,
         [((16, 256, 128), BF, VMEM), ((64, 128), F32, VMEM), ((17, 256, 128), F32, VMEM)],
-        [SMEM, SMEM] + [VMEM] * 4,
-        alias={5: 2},
+        [SMEM, SMEM] + [VMEM] * 5,
+        alias={6: 2},
         **heavy,
-    )(lists, groups, tile, own, other, begun)
+    )(lists, groups, tile, other, total, paired(total, "x", 1), begun)
     parts = exchange(back, ("zl", "x"))
-    for axis in ("x", "zl"):
-        total = paired_sum(paired_sum(total, axis, 1), axis, 2)
+    for axis, k in (("x", 2), ("zl", 1), ("zl", 2)):
+        total = total + paired(total, axis, k)
+    total = total + swap(total)
     grad, parts = call(
         functools.partial(gate_kernel, 1.0 / math.sqrt(nodes_total)),
         [((8, 32, 256), BF, VMEM), ((16, 256, 128), BF, VMEM)],

time: 190 us -> 198 us (1.042)
  starting transfers between devices: 28.6 us -> 46 us
  blocking collectives: 101 us -> 85.1 us
  waiting for transfers between devices: 39.2 us -> 46.4 us
    all_to_all x3 -> x2, blocking collectives: 101 us -> 85.1 us  [exchange(): return lax.all_to_all(value, axes, 0, 0, tiled=True)]
    all_to_all x3, waiting for transfers between devices: 16.3 us -> 29.6 us  [exchange(): return lax.all_to_all(value, axes, 0, 0, tiled=True)]
    all_to_all x3, starting transfers between devices: 16 us -> 24.6 us  [exchange(): return lax.all_to_all(value, axes, 0, 0, tiled=True)]
    ppermute x4, waiting for transfers between devices: 22.5 us -> 15 us  [paired(): return lax.ppermute(value, axis, [(i, i ^ k) for i in range(4)])]
    ppermute x4, starting transfers between devices: 8.81 us -> 15.6 us  [paired(): return lax.ppermute(value, axis, [(i, i ^ k) for i in range(4)])]
    ppermute x2 -> x3, starting transfers between devices: 3.83 us -> 5.74 us  [swap(): return lax.ppermute(value, 'c', [(0, 1), (1, 0)])]
  transfers between devices with their start and end apart: 9 -> 10, of which waited for: 8 -> 8; matrix products, arithmetic and copies ran while one was open for 0% -> 0% of each run, Pallas kernels for 4% -> 4%
where the time goes in v9:
time: 198 us; the launch traced here: 197 us
  blocking collectives  85.1 us (43%)
  waiting for transfers between devices  46.4 us (23%)
  starting transfers between devices  46 us (23%)
  Pallas kernels  15.1 us (8%)
  local copies, waits for them, and re-layouts  2.09 us (1%)
    all_to_all x2, blocking collectives, exchange(): return lax.all_to_all(value, axes, 0, 0, tiled=True)  85.1 us
    all_to_all x3, waiting for transfers between devices, exchange(): return lax.all_to_all(value, axes, 0, 0, tiled=True)  29.6 us
    all_to_all x3, starting transfers between devices, exchange(): return lax.all_to_all(value, axes, 0, 0, tiled=True)  24.6 us
    ppermute x4, starting transfers between devices, paired(): return lax.ppermute(value, axis, [(i, i ^ k) for i in range(4)])  15.6 us
    ppermute x4, waiting for transfers between devices, paired(): return lax.ppermute(value, axis, [(i, i ^ k) for i in range(4)])  15 us
    ppermute x3, starting transfers between devices, swap(): return lax.ppermute(value, 'c', [(0, 1), (1, 0)])  5.74 us
    pallas_call x2, Pallas kernels, shards(): call(functools.partial(forward_kernel, which), [((16, 128, 256), BF, VMEM...  4.27 us
  transfers between devices with their start and end apart: 10, of which 8 were waited for; matrix products, arithmetic and copies ran while one was open for 0% of the time, Pallas kernels for 4%

profile of v9, /device:TPU:6, one launch (start us, length us, event | category | flops | bytes accessed | tf_op | source)
XLA Modules:
  0.0 197.3 jit_solution(3205592193995617981)
XLA Ops:
  0.6 0.0 copy-start.3
  0.6 0.0 copy-start
  0.7 2.1 %broadcast_in_dim.2 = bf16[16,128,256]{2,1,0:T(8,128)(2,1)} broadcast(bf16[128,256]{1,0:T(8,128)(2,1)} %param.6), dimensions={1,2} | broadcast | bytes 1114112 | tf_op jit(solution)/shard_map/broadcast_in_dim | solution.py:173
  2.7 10.2 %all-to-all-start = ((bf16[16,128,256]{2,1,0:T(8,128)(2,1)}), bf16[16,128,256]{2,1,0:T(8,128)(2,1)}, u32[]{:S(2)}, u32[]{:S(2)}) async-start(bf16[16,128,256]{2,1,0:T(8,128)(2,1)} %broadcast_in_dim.2), calls=%async_computation | async-start | bytes 2097152 | tf_op jit(solution)/shard_map/all_to_all | solution.py:147
  13.6 0.1 pad_add_fusion.info
  13.7 0.0 copy-done.3
  13.7 0.0 copy-done
  13.7 1.9 shard_map.85
  15.6 21.2 %all-to-all-done.nodes = bf16[16,128,256]{2,1,0:T(8,128)(2,1)} async-done(((bf16[16,128,256]{2,1,0:T(8,128)(2,1)}), bf16[16,128,256]{2,1,0:T(8,128)(2,1)}, u32[]{:S(2)}, u32[]{:S(2)}) %all-to-all-start) | async-done | bytes 1048608 | tf_op jit(solution)/shard_map/all_to_all | solution.py:147
  36.8 2.4 %shard_map.87 = bf16[16,128,256]{2,1,0:T(8,128)(2,1)S(1)} custom-call(s32[1120]{0:T(1024)S(1)} %get-tuple-element.13.lists, s32[2]{0:T(128)S(1)} %get-tuple-element.14.groups, bf16[96,128,128]{2,1,0:T(8,128)(2,1)S(1)} %bitcast.13, bf16[16,128,256]{2,1,0:T(8,128)(2,1)} %all-to-all-done.nodes), custom_call_target="tpu_custom_call" | custom-call | flops 800000000 | bytes 6291456 | tf_op jit(solution)/shard_map/pallas_call | solution.py:175
  39.1 1.9 collective-permute-start
  41.1 1.9 shard_map.86
  43.0 0.0 copy-start.1
  43.0 0.0 copy-start.2
  43.0 0.7 collective-permute-done
  43.7 0.3 add_convert_fusion
  44.0 43.7 %all_to_all.25.parts = bf16[16,128,256]{2,1,0:T(8,128)(2,1)S(1)} all-to-all(bf16[16,128,256]{2,1,0:T(8,128)(2,1)S(1)} %add_convert_fusion), channel_id=1, replica_groups=mesh['zl'=4,'x'=4,'zh'=2,'y'=8,'c'=2] {'zh','y'}, dimensions={0} | all-to-all | bytes 2097152 | tf_op jit(solution)/shard_map/all_to_all | solution.py:147
  87.7 0.0 copy-done.1
  87.7 0.0 copy-done.2
  87.7 0.9 shard_map.88
  88.6 41.4 %all_to_all.26.own = bf16[16,320,128]{2,1,0:T(8,128)(2,1)S(1)} all-to-all(bf16[16,320,128]{2,1,0:T(8,128)(2,1)S(1)} %get-tuple-element.16), channel_id=1, replica_groups=mesh['zl'=4,'x'=4,'zh'=2,'y'=8,'c'=2] {'zh','y'}, dimensions={0} | all-to-all | bytes 2621440 | tf_op jit(solution)/shard_map/all_to_all | solution.py:147
  130.1 1.9 collective-permute-start.1
  132.0 2.5 %shard_map.89 = (f32[17,256,128]{2,1,0:T(8,128)S(1)}, f32[64,128]{1,0:T(8,128)S(1)}) custom-call(s32[1120]{0:T(1024)S(1)} %get-tuple-element.13.lists, s32[2]{0:T(128)S(1)} %get-tuple-element.14.groups, bf16[96,128,128]{2,1,0:T(8,128)(2,1)} %bitcast.10, bf16[16,320,128]{2,1,0:T(8,128)(2,1)S(1)} %all_to_all.26.own), custom_call_target="tpu_custom_call" | custom-call | flops 800000000 | bytes 6291456 | tf_op jit(solution)/shard_map/pallas_call | solution.py:193
  134.5 2.3 %collective-permute-start.2 = (f32[64,128]{1,0:T(8,128)S(1)}, f32[64,128]{1,0:T(8,128)S(1)}, u32[]{:S(2)}, u32[]{:S(2)}) collective-permute-start(f32[64,128]{1,0:T(8,128)S(1)} %get-tuple-element.17.mine), channel_id=1, source_target_pairs={{0,32},{32,0},{64,96},{96,64},{1,33},{33,1},{65,97},{97,65},{2,34}... | collective-permute-start | bytes 98312 | tf_op jit(solution)/shard_map/ppermute | solution.py:155
  136.8 3.5 %collective-permute-done.2.theirs = f32[64,128]{1,0:T(8,128)S(1)} collective-permute-done((f32[64,128]{1,0:T(8,128)S(1)}, f32[64,128]{1,0:T(8,128)S(1)}, u32[]{:S(2)}, u32[]{:S(2)}) %collective-permute-start.2) | collective-permute-done | bytes 32800 | tf_op jit(solution)/shard_map/ppermute | solution.py:155
  140.3 0.0 collective-permute-done.1.other
  140.3 3.9 %shard_map.90 = (bf16[16,256,128]{2,1,0:T(8,128)(2,1)}, f32[64,128]{1,0:T(8,128)S(1)}, f32[17,256,128]{2,1,0:T(8,128)S(1)}) custom-call(s32[1120]{0:T(1024)S(1)} %get-tuple-element.13.lists, s32[2]{0:T(128)S(1)} %get-tuple-element.14.groups, bf16[96,128,128]{2,1,0:T(8,128)(2,1)} %bitcast.11, ...), custom_call_target="tpu_custom_call", output_to_operand_aliasing={{2}: (6, {})} | custom-call | flops 800000000 | bytes 6291456 | tf_op jit(solution)/shard_map/pallas_call | solution.py:199
  144.2 7.8 %all-to-all-start.3 = ((bf16[16,256,128]{2,1,0:T(8,128)(2,1)}), bf16[16,256,128]{2,1,0:T(8,128)(2,1)S(1)}, u32[]{:S(2)}, u32[]{:S(2)}) async-start(bf16[16,256,128]{2,1,0:T(8,128)(2,1)} %get-tuple-element.20), calls=%async_computation.3 | async-start | bytes 2097152 | tf_op jit(solution)/shard_map/all_to_all | solution.py:147
  152.0 3.4 %collective-permute-start.3 = (f32[64,128]{1,0:T(8,128)S(1)}, f32[64,128]{1,0:T(8,128)S(1)}, u32[]{:S(2)}, u32[]{:S(2)}) collective-permute-start(f32[64,128]{1,0:T(8,128)S(1)} %get-tuple-element.19), channel_id=1, source_target_pairs={{0,64},{32,96},{64,0},{96,32},{1,65},{33,97},{65,1},{97,33},{2,66}... | collective-permute-start | bytes 98312 | tf_op jit(solution)/shard_map/ppermute | solution.py:155
  155.4 4.0 %collective-permute-done.3 = f32[64,128]{1,0:T(8,128)S(1)} collective-permute-done((f32[64,128]{1,0:T(8,128)S(1)}, f32[64,128]{1,0:T(8,128)S(1)}, u32[]{:S(2)}, u32[]{:S(2)}) %collective-permute-start.3) | collective-permute-done | bytes 32800 | tf_op jit(solution)/shard_map/ppermute | solution.py:155
  159.4 3.7 %collective-permute-start.4 = (f32[64,128]{1,0:T(8,128)S(1)}, f32[64,128]{1,0:T(8,128)S(1)}, u32[]{:S(2)}, u32[]{:S(2)}) collective-permute-start(f32[64,128]{1,0:T(8,128)S(1)} %add.16), channel_id=1, source_target_pairs={{0,128},{128,0},{256,384},{384,256},{1,129},{129,1},{257,385},{385... | collective-permute-start | bytes 98312 | tf_op jit(solution)/shard_map/ppermute | solution.py:155
  163.1 4.7 %collective-permute-done.4 = f32[64,128]{1,0:T(8,128)S(1)} collective-permute-done((f32[64,128]{1,0:T(8,128)S(1)}, f32[64,128]{1,0:T(8,128)S(1)}, u32[]{:S(2)}, u32[]{:S(2)}) %collective-permute-start.4) | collective-permute-done | bytes 32800 | tf_op jit(solution)/shard_map/ppermute | solution.py:155
  167.8 6.2 %collective-permute-start.5 = (f32[64,128]{1,0:T(8,128)S(1)}, f32[64,128]{1,0:T(8,128)S(1)}, u32[]{:S(2)}, u32[]{:S(2)}) collective-permute-start(f32[64,128]{1,0:T(8,128)S(1)} %add.17), channel_id=1, source_target_pairs={{0,256},{128,384},{256,0},{384,128},{1,257},{129,385},{257,1},{385... | collective-permute-start | bytes 98312 | tf_op jit(solution)/shard_map/ppermute | solution.py:155
  174.0 2.8 %collective-permute-done.5 = f32[64,128]{1,0:T(8,128)S(1)} collective-permute-done((f32[64,128]{1,0:T(8,128)S(1)}, f32[64,128]{1,0:T(8,128)S(1)}, u32[]{:S(2)}, u32[]{:S(2)}) %collective-permute-start.5) | collective-permute-done | bytes 32800 | tf_op jit(solution)/shard_map/ppermute | solution.py:155
  176.8 1.9 collective-permute-start.6
  178.8 1.2 collective-permute-done.6
  179.9 0.0 all-to-all-done.3.parts
  179.9 0.7 shard_map.91
  180.6 6.6 %all-to-all-start.4 = ((bf16[8,32,256]{2,1,0:T(8,128)(2,1)}), bf16[8,32,256]{2,1,0:T(8,128)(2,1)S(1)}, u32[]{:S(2)}, u32[]{:S(2)}) async-start(bf16[8,32,256]{2,1,0:T(8,128)(2,1)} %get-tuple-element.22), calls=%async_computation.4 | async-start | bytes 262144 | tf_op jit(solution)/shard_map/all_to_all | solution.py:147
  187.2 1.0 shard_map.92
  188.2 8.4 %all-to-all-done.4 = bf16[8,32,256]{2,1,0:T(8,128)(2,1)S(1)} async-done(((bf16[8,32,256]{2,1,0:T(8,128)(2,1)}), bf16[8,32,256]{2,1,0:T(8,128)(2,1)S(1)}, u32[]{:S(2)}, u32[]{:S(2)}) %all-to-all-start.4) | async-done | bytes 131104 | tf_op jit(solution)/shard_map/all_to_all | solution.py:147
  196.6 0.7 bitcast_convert_fusion
  (4 shorter events, 0.0 us)
Async XLA Ops:
  0.6 13.0 %copy-start.3 = (s32[1,1,96]{2,1,0:T(1,128)S(1)}, s32[1,1,96]{2,1,0:T(1,128)}, u32[]{:S(2)}) copy-start(s32[1,1,96]{2,1,0:T(1,128)} %param.10) | copy-start | bytes 1156
  0.6 13.0 %copy-start = (bf16[1,1,96,128,128]{4,3,2,1,0:T(8,128)(2,1)S(1)}, bf16[1,1,96,128,128]{4,3,2,1,0:T(8,128)(2,1)}, u32[]{:S(2)}) copy-start(bf16[1,1,96,128,128]{4,3,2,1,0:T(8,128)(2,1)} %param.9) | copy-start | bytes 9437188
  2.7 34.1 %all-to-all-start = ((bf16[16,128,256]{2,1,0:T(8,128)(2,1)}), bf16[16,128,256]{2,1,0:T(8,128)(2,1)}, u32[]{:S(2)}, u32[]{:S(2)}) async-start(bf16[16,128,256]{2,1,0:T(8,128)(2,1)} %broadcast_in_dim.2), calls=%async_computation | async-start | bytes 2097152 | tf_op jit(solution)/shard_map/all_to_all | solution.py:147
  39.1 4.6 %collective-permute-start = (bf16[16,128,256]{2,1,0:T(8,128)(2,1)S(1)}, bf16[16,128,256]{2,1,0:T(8,128)(2,1)S(1)}, u32[]{:S(2)}, u32[]{:S(2)}) collective-permute-start(bf16[16,128,256]{2,1,0:T(8,128)(2,1)S(1)} %shard_map.87), channel_id=1, source_target_pairs={{0,1},{1,0},{2,3},{3,2},{4,5},{5,4},{6,7},{7,6},{8,9},{9,8},{10,11... | collective-permute-start | bytes 3145736 | tf_op jit(solution)/shard_map/ppermute | solution.py:151
  43.0 44.7 %copy-start.1 = (bf16[256,256]{1,0:T(8,128)(2,1)S(1)}, bf16[256,256]{1,0:T(8,128)(2,1)}, u32[]{:S(2)}) copy-start(bf16[256,256]{1,0:T(8,128)(2,1)} %weight.3) | copy-start | bytes 393220
  43.0 44.7 %copy-start.2 = (bf16[128,256]{1,0:T(8,128)(2,1)S(1)}, bf16[128,256]{1,0:T(8,128)(2,1)}, u32[]{:S(2)}) copy-start(bf16[128,256]{1,0:T(8,128)(2,1)} %cotangent.1) | copy-start | bytes 196612
  130.1 10.2 %collective-permute-start.1 = (bf16[16,320,128]{2,1,0:T(8,128)(2,1)S(1)}, bf16[16,320,128]{2,1,0:T(8,128)(2,1)S(1)}, u32[]{:S(2)}, u32[]{:S(2)}) collective-permute-start(bf16[16,320,128]{2,1,0:T(8,128)(2,1)S(1)} %all_to_all.26.own), channel_id=1, source_target_pairs={{0,1},{1,0},{2,3},{3,2},{4,5},{5,4},{6,7},{7,6},{8,9},{9,8},{10,11... | collective-permute-start | bytes 3932168 | tf_op jit(solution)/shard_map/ppermute | solution.py:151
  134.5 5.8 %collective-permute-start.2 = (f32[64,128]{1,0:T(8,128)S(1)}, f32[64,128]{1,0:T(8,128)S(1)}, u32[]{:S(2)}, u32[]{:S(2)}) collective-permute-start(f32[64,128]{1,0:T(8,128)S(1)} %get-tuple-element.17.mine), channel_id=1, source_target_pairs={{0,32},{32,0},{64,96},{96,64},{1,33},{33,1},{65,97},{97,65},{2,34}... | collective-permute-start | bytes 98312 | tf_op jit(solution)/shard_map/ppermute | solution.py:155
  144.2 35.7 %all-to-all-start.3 = ((bf16[16,256,128]{2,1,0:T(8,128)(2,1)}), bf16[16,256,128]{2,1,0:T(8,128)(2,1)S(1)}, u32[]{:S(2)}, u32[]{:S(2)}) async-start(bf16[16,256,128]{2,1,0:T(8,128)(2,1)} %get-tuple-element.20), calls=%async_computation.3 | async-start | bytes 2097152 | tf_op jit(solution)/shard_map/all_to_all | solution.py:147
  152.0 7.3 %collective-permute-start.3 = (f32[64,128]{1,0:T(8,128)S(1)}, f32[64,128]{1,0:T(8,128)S(1)}, u32[]{:S(2)}, u32[]{:S(2)}) collective-permute-start(f32[64,128]{1,0:T(8,128)S(1)} %get-tuple-element.19), channel_id=1, source_target_pairs={{0,64},{32,96},{64,0},{96,32},{1,65},{33,97},{65,1},{97,33},{2,66}... | collective-permute-start | bytes 98312 | tf_op jit(solution)/shard_map/ppermute | solution.py:155
  159.4 8.4 %collective-permute-start.4 = (f32[64,128]{1,0:T(8,128)S(1)}, f32[64,128]{1,0:T(8,128)S(1)}, u32[]{:S(2)}, u32[]{:S(2)}) collective-permute-start(f32[64,128]{1,0:T(8,128)S(1)} %add.16), channel_id=1, source_target_pairs={{0,128},{128,0},{256,384},{384,256},{1,129},{129,1},{257,385},{385... | collective-permute-start | bytes 98312 | tf_op jit(solution)/shard_map/ppermute | solution.py:155
  167.8 9.1 %collective-permute-start.5 = (f32[64,128]{1,0:T(8,128)S(1)}, f32[64,128]{1,0:T(8,128)S(1)}, u32[]{:S(2)}, u32[]{:S(2)}) collective-permute-start(f32[64,128]{1,0:T(8,128)S(1)} %add.17), channel_id=1, source_target_pairs={{0,256},{128,384},{256,0},{384,128},{1,257},{129,385},{257,1},{385... | collective-permute-start | bytes 98312 | tf_op jit(solution)/shard_map/ppermute | solution.py:155
  176.8 3.1 %collective-permute-start.6 = (f32[64,128]{1,0:T(8,128)S(1)}, f32[64,128]{1,0:T(8,128)S(1)}, u32[]{:S(2)}, u32[]{:S(2)}) collective-permute-start(f32[64,128]{1,0:T(8,128)S(1)} %add.18), channel_id=1, source_target_pairs={{0,1},{1,0},{2,3},{3,2},{4,5},{5,4},{6,7},{7,6},{8,9},{9,8},{10,11... | collective-permute-start | bytes 98312 | tf_op jit(solution)/shard_map/ppermute | solution.py:151
  180.6 16.0 %all-to-all-start.4 = ((bf16[8,32,256]{2,1,0:T(8,128)(2,1)}), bf16[8,32,256]{2,1,0:T(8,128)(2,1)S(1)}, u32[]{:S(2)}, u32[]{:S(2)}) async-start(bf16[8,32,256]{2,1,0:T(8,128)(2,1)} %get-tuple-element.22), calls=%async_computation.4 | async-start | bytes 262144 | tf_op jit(solution)/shard_map/all_to_all | solution.py:147

commit v10 on v4

--- a/solution.py
+++ b/solution.py
@@ -23,7 +23,7 @@
 
 
 def plan_kernel(place, info, blocks, lists, groups):
-    count, core, xi, zi = info[0], info[1], info[2], info[3]
+    count, core, zi = info[0], info[1], info[2]
 
     def write(at, k, t, source, half, target):
         for f, value in enumerate((k, t, source, half, target)):
@@ -35,7 +35,7 @@
         z, x = a >> 2, a & 3
         half = t >> 1
         source = (x << 2) + z
-        target = (((x - xi) & 3) << 2) + ((z - zi) & 3)
+        target = (x << 2) + ((z - zi) & 3)
         mine, theirs = held
         away = (t & 1) ^ core
         write(jnp.where(away == 0, mine, SLOTS + theirs), k, half, source, half, target)
@@ -89,11 +89,6 @@
         spread[s, 288:320, :] = grad[rows, 128:256]
 
 
-def split(value):
-    high = value.astype(BF)
-    return high, (value - high.astype(F32)).astype(BF)
-
-
 def back_products(which, lists, groups, blocks, source, acc):
     def step(i, _):
         products = []
@@ -113,41 +108,36 @@
     back_products(0, lists, groups, blocks, own, acc)
 
 
-def backward_other_kernel(lists, groups, blocks, own, other, begun, b0, b1, b2, b3, acc):
+def backward_other_kernel(lists, groups, blocks, own, other, begun, out, acc):
     back_products(1, lists, groups, blocks, other, acc)
     grad = jnp.zeros((64, 128), F32)
     for s in range(16):
         grad += own[s, 256:320, :].astype(F32) + other[s, 256:320, :].astype(F32)
-    high, low = split(grad)
-    for x, out in enumerate((b0, b1, b2, b3)):
+    grad = grad.astype(BF)
+    for x in range(4):
         for z in range(4):
-            out[256 * z : 256 * z + 256, :] = acc[4 * x + z].astype(BF)
-        out[1024:1088, :] = high
-        out[1088:1152, :] = low
-
-
-def ordered_sum(me, parts, row, scratch):
-    for k, part in enumerate(parts):
-        high, low = part[row : row + 64, :], part[row + 64 : row + 128, :]
-        scratch[(me - k) & 3] = high.astype(F32) + low.astype(F32)
-    return scratch[0] + scratch[1] + scratch[2] + scratch[3]
-
-
-def fold_kernel(info, b0, b1, b2, b3, f0, f1, f2, f3, scratch):
-    parts = (b0, b1, b2, b3)
-    high, low = split(ordered_sum(info[2], parts, 1024, scratch))
+            out[x, 256 * z : 256 * z + 256, :] = acc[4 * x + z].astype(BF)
+        out[x, 1024:1088, :] = grad
+
+
+def fold_kernel(parts, f0, f1, f2, f3):
+    grad = parts[0, 1024:1088, :].astype(F32)
+    for x in range(1, 4):
+        grad += parts[x, 1024:1088, :].astype(F32)
+    grad = grad.astype(BF)
     for z, out in enumerate((f0, f1, f2, f3)):
         rows = slice(256 * z, 256 * z + 256)
-        total = parts[0][rows, :].astype(F32)
-        for part in parts[1:]:
-            total += part[rows, :].astype(F32)
+        total = parts[0, rows, :].astype(F32)
+        for x in range(1, 4):
+            total += parts[x, rows, :].astype(F32)
         out[0:256, :] = total.astype(BF)
-        out[256:320, :] = high
-        out[320:384, :] = low
+        out[256:320, :] = grad
 
 
 def grad_kernel(scale, info, f0, f1, f2, f3, grad_out, scratch):
-    grad = (ordered_sum(info[3], (f0, f1, f2, f3), 256, scratch) * scale).astype(BF)
+    for k, part in enumerate((f0, f1, f2, f3)):
+        scratch[(info[2] - k) & 3] = part[256:320, :].astype(F32)
+    grad = ((scratch[0] + scratch[1] + scratch[2] + scratch[3]) * scale).astype(BF)
     for s in range(8):
         grad_out[s, :, 0:128] = grad[0:32]
         grad_out[s, :, 128:256] = grad[32:64]
@@ -188,7 +178,7 @@
 
 def shards(features, weight, cotangent, blocks, block_pos, counts):
     tile = blocks[0, 0]
-    index = [lax.axis_index(a).astype(jnp.int32) for a in ("c", "x", "zl")]
+    index = [lax.axis_index(a).astype(jnp.int32) for a in ("c", "zl")]
     info = jnp.stack([counts[0, 0]] + index)
     nodes_total = 65536
     heavy = dict(flops=8 * 10**8, size=6 * 2**20)
@@ -228,20 +218,14 @@
         [SMEM, SMEM, VMEM, VMEM],
         **heavy,
     )(lists, groups, tile, own)
-    back = call(
+    back, _ = call(
         backward_other_kernel,
-        [((1152, 128), BF, VMEM)] * 4 + [((17, 256, 128), F32, VMEM)],
+        [((4, 1088, 128), BF, VMEM), ((17, 256, 128), F32, VMEM)],
         [SMEM, SMEM] + [VMEM] * 4,
-        alias={5: 4},
+        alias={5: 1},
         **heavy,
     )(lists, groups, tile, own, other, begun)
-    back = [back[0]] + [rotate(back[k], "x", k) for k in (1, 2, 3)]
-    folded = call(
-        fold_kernel,
-        [((384, 128), BF, VMEM)] * 4,
-        [SMEM] + [VMEM] * 4,
-        [pltpu.VMEM((4, 64, 128), F32)],
-    )(info, *back)
+    folded = call(fold_kernel, [((320, 128), BF, VMEM)] * 4, [VMEM])(exchange(back, "x"))
     folded = [folded[0]] + [rotate(folded[k], "zl", k) for k in (1, 2, 3)]
     (grad,) = call(
         functools.partial(grad_kernel, 1.0 / math.sqrt(nodes_total)),

time: 190 us -> 184 us (0.968)
  blocking collectives: 99.5 us -> 120 us
  waiting for transfers between devices: 31.4 us -> 19.1 us
  starting transfers between devices: 33.4 us -> 24 us
  Pallas kernels: 19.8 us -> 15.6 us
    all_to_all x3 -> x4, blocking collectives: 99.5 us -> 120 us  [exchange(): return lax.all_to_all(value, axes, 0, 0, tiled=True)]
    ppermute x6 -> x3, waiting for transfers between devices: 15.8 us -> 2.35 us  [rotate(): return lax.ppermute(value, axis, [(i, (i + k) % 4) for i in range(4)])]
    ppermute x6 -> x3, starting transfers between devices: 19.4 us -> 11.4 us  [rotate(): return lax.ppermute(value, axis, [(i, (i + k) % 4) for i in range(4)])]
  transfers between devices with their start and end apart: 10 -> 7, of which waited for: 7 -> 5; matrix products, arithmetic and copies ran while one was open for 0% -> 0% of each run, Pallas kernels for 6% -> 4%
where the time goes in v10:
time: 184 us; the launch traced here: 183 us
  blocking collectives  120 us (65%)
  starting transfers between devices  24 us (13%)
  waiting for transfers between devices  19.1 us (10%)
  Pallas kernels  15.6 us (8%)
  local copies, waits for them, and re-layouts  2.12 us (1%)
    all_to_all x4, blocking collectives, exchange(): return lax.all_to_all(value, axes, 0, 0, tiled=True)  120 us
    all_to_all x2, waiting for transfers between devices, exchange(): return lax.all_to_all(value, axes, 0, 0, tiled=True)  16.5 us
    ppermute x3, starting transfers between devices, rotate(): return lax.ppermute(value, axis, [(i, (i + k) % 4) for i in range(4)])  11.4 us
    all_to_all x2, starting transfers between devices, exchange(): return lax.all_to_all(value, axes, 0, 0, tiled=True)  8.72 us
    pallas_call x2, Pallas kernels, shards(): call(functools.partial(forward_kernel, which), [((16, 128, 256), BF, VMEM...  4.71 us
    ppermute x2, starting transfers between devices, swap(): return lax.ppermute(value, 'c', [(0, 1), (1, 0)])  3.83 us
  transfers between devices with their start and end apart: 7, of which 5 were waited for; matrix products, arithmetic and copies ran while one was open for 0% of the time, Pallas kernels for 4%

profile of v10, /device:TPU:6, one launch (start us, length us, event | category | flops | bytes accessed | tf_op | source)
XLA Modules:
  0.0 183.1 jit_solution(15076616787410767725)
XLA Ops:
  0.6 0.0 copy-start.3
  0.6 0.0 copy-start
  0.7 1.0 broadcast_in_dim.4
  1.7 15.9 %all_to_all.30 = bf16[4,128,256]{2,1,0:T(8,128)(2,1)S(1)} all-to-all(bf16[4,128,256]{2,1,0:T(8,128)(2,1)S(1)} %broadcast_in_dim.4), channel_id=1, replica_groups=mesh['zl'=4,'x'=4,'zh'=2,'y'=8,'c'=2] {'zl'}, dimensions={0} | all-to-all | bytes 524288 | tf_op jit(solution)/shard_map/all_to_all | solution.py:168
  17.6 1.1 broadcast_in_dim.5
  18.7 4.8 %all-to-all-start.1 = ((bf16[4,4,128,256]{3,2,1,0:T(8,128)(2,1)}), bf16[4,4,128,256]{3,2,1,0:T(8,128)(2,1)}, u32[]{:S(2)}, u32[]{:S(2)}) async-start(bf16[4,4,128,256]{3,2,1,0:T(8,128)(2,1)} %broadcast_in_dim.5), calls=%async_computation.1 | async-start | bytes 2097152 | tf_op jit(solution)/shard_map/all_to_all | solution.py:168
  24.1 0.1 pad_add_fusion.info
  24.2 0.0 copy-done.3
  24.2 0.0 copy-done
  24.2 1.9 %shard_map.85 = (s32[1120]{0:T(1024)S(1)}, s32[2]{0:T(128)S(1)}) custom-call(s32[96]{0:T(128)S(1)} %bitcast.15, s32[3]{0:T(128)S(1)} %pad_add_fusion.info, bf16[96,128,128]{2,1,0:T(8,128)(2,1)S(1)} %bitcast.12), custom_call_target="tpu_custom_call" | custom-call | bytes 1048576 | tf_op jit(solution)/shard_map/pallas_call | solution.py:187
  26.1 8.2 %all-to-all-done.1 = bf16[4,4,128,256]{3,2,1,0:T(8,128)(2,1)} async-done(((bf16[4,4,128,256]{3,2,1,0:T(8,128)(2,1)}), bf16[4,4,128,256]{3,2,1,0:T(8,128)(2,1)}, u32[]{:S(2)}, u32[]{:S(2)}) %all-to-all-start.1) | async-done | bytes 1048608 | tf_op jit(solution)/shard_map/all_to_all | solution.py:168
  34.3 2.4 %shard_map.87 = bf16[16,128,256]{2,1,0:T(8,128)(2,1)S(1)} custom-call(s32[1120]{0:T(1024)S(1)} %get-tuple-element.12.lists, s32[2]{0:T(128)S(1)} %get-tuple-element.13.groups, bf16[96,128,128]{2,1,0:T(8,128)(2,1)S(1)} %bitcast.13, bf16[16,128,256]{2,1,0:T(8,128)(2,1)} %bitcast.5.nodes), custom_call_target="tpu_custom_call" | custom-call | flops 800000000 | bytes 6291456 | tf_op jit(solution)/shard_map/pallas_call | solution.py:197
  36.7 1.9 %collective-permute-start = (bf16[16,128,256]{2,1,0:T(8,128)(2,1)S(1)}, bf16[16,128,256]{2,1,0:T(8,128)(2,1)S(1)}, u32[]{:S(2)}, u32[]{:S(2)}) collective-permute-start(bf16[16,128,256]{2,1,0:T(8,128)(2,1)S(1)} %shard_map.87), channel_id=1, source_target_pairs={{0,1},{1,0},{2,3},{3,2},{4,5},{5,4},{6,7},{7,6},{8,9},{9,8},{10,11... | collective-permute-start | bytes 3145736 | tf_op jit(solution)/shard_map/ppermute | solution.py:172
  38.6 2.4 %shard_map.86 = bf16[16,128,256]{2,1,0:T(8,128)(2,1)S(1)} custom-call(s32[1120]{0:T(1024)S(1)} %get-tuple-element.12.lists, s32[2]{0:T(128)S(1)} %get-tuple-element.13.groups, bf16[96,128,128]{2,1,0:T(8,128)(2,1)S(1)} %bitcast.14, bf16[16,128,256]{2,1,0:T(8,128)(2,1)} %bitcast.5.nodes), custom_call_target="tpu_custom_call" | custom-call | flops 800000000 | bytes 6291456 | tf_op jit(solution)/shard_map/pallas_call | solution.py:197
  41.0 0.0 copy-start.1
  41.0 0.0 copy-start.2
  41.0 0.2 collective-permute-done
  41.3 0.3 add_convert_fusion
  41.6 43.8 %all_to_all.31.parts = bf16[16,128,256]{2,1,0:T(8,128)(2,1)S(1)} all-to-all(bf16[16,128,256]{2,1,0:T(8,128)(2,1)S(1)} %add_convert_fusion), channel_id=1, replica_groups=mesh['zl'=4,'x'=4,'zh'=2,'y'=8,'c'=2] {'zh','y'}, dimensions={0} | all-to-all | bytes 2097152 | tf_op jit(solution)/shard_map/all_to_all | solution.py:168
  85.4 0.0 copy-done.1
  85.4 0.0 copy-done.2
  85.4 0.9 shard_map.88
  86.3 41.1 %all_to_all.32.own = bf16[16,320,128]{2,1,0:T(8,128)(2,1)S(1)} all-to-all(bf16[16,320,128]{2,1,0:T(8,128)(2,1)S(1)} %get-tuple-element.15), channel_id=1, replica_groups=mesh['zl'=4,'x'=4,'zh'=2,'y'=8,'c'=2] {'zh','y'}, dimensions={0} | all-to-all | bytes 2621440 | tf_op jit(solution)/shard_map/all_to_all | solution.py:168
  127.5 1.9 %collective-permute-start.1 = (bf16[16,320,128]{2,1,0:T(8,128)(2,1)S(1)}, bf16[16,320,128]{2,1,0:T(8,128)(2,1)S(1)}, u32[]{:S(2)}, u32[]{:S(2)}) collective-permute-start(bf16[16,320,128]{2,1,0:T(8,128)(2,1)S(1)} %all_to_all.32.own), channel_id=1, source_target_pairs={{0,1},{1,0},{2,3},{3,2},{4,5},{5,4},{6,7},{7,6},{8,9},{9,8},{10,11... | collective-permute-start | bytes 3932168 | tf_op jit(solution)/shard_map/ppermute | solution.py:172
  129.4 2.9 %shard_map.89.begun = f32[17,256,128]{2,1,0:T(8,128)S(1)} custom-call(s32[1120]{0:T(1024)S(1)} %get-tuple-element.12.lists, s32[2]{0:T(128)S(1)} %get-tuple-element.13.groups, bf16[96,128,128]{2,1,0:T(8,128)(2,1)} %bitcast.10, bf16[16,320,128]{2,1,0:T(8,128)(2,1)S(1)} %all_to_all.32.own), custom_call_target="tpu_custom_call" | custom-call | flops 800000000 | bytes 6291456 | tf_op jit(solution)/shard_map/pallas_call | solution.py:215
  132.3 0.1 collective-permute-done.1.other
  132.4 2.9 %shard_map.90 = (bf16[4,1088,128]{2,1,0:T(8,128)(2,1)S(1)}, f32[17,256,128]{2,1,0:T(8,128)S(1)}) custom-call(s32[1120]{0:T(1024)S(1)} %get-tuple-element.12.lists, s32[2]{0:T(128)S(1)} %get-tuple-element.13.groups, bf16[96,128,128]{2,1,0:T(8,128)(2,1)} %bitcast.11, bf16[16,320,128]{2,1,0:T(8,128)(2,1)S(1)} %all_to_all.32.own, ...), custom_call_target="tpu_custom_call", output_to_operand_aliasing={{1}: (5, {})} | custom-call | flops 800000000 | bytes 6291456 | tf_op jit(solution)/shard_map/pallas_call | solution.py:221
  135.3 18.8 %all_to_all.33.parts = bf16[4,1088,128]{2,1,0:T(8,128)(2,1)S(1)} all-to-all(bf16[4,1088,128]{2,1,0:T(8,128)(2,1)S(1)} %get-tuple-element.16), channel_id=1, replica_groups=mesh['zl'=4,'x'=4,'zh'=2,'y'=8,'c'=2] {'x'}, dimensions={0} | all-to-all | bytes 2228224 | tf_op jit(solution)/shard_map/all_to_all | solution.py:168
  154.2 0.1 shard_map.91
  154.3 2.3 %collective-permute-start.2 = (bf16[320,128]{1,0:T(8,128)(2,1)S(1)}, bf16[320,128]{1,0:T(8,128)(2,1)S(1)}, u32[]{:S(2)}, u32[]{:S(2)}) collective-permute-start(bf16[320,128]{1,0:T(8,128)(2,1)S(1)} %get-tuple-element.18), channel_id=1, source_target_pairs={{0,128},{128,256},{256,384},{384,0},{1,129},{129,257},{257,385},{3... | collective-permute-start | bytes 245768 | tf_op jit(solution)/shard_map/ppermute | solution.py:176
  156.6 5.2 %collective-permute-start.3 = (bf16[320,128]{1,0:T(8,128)(2,1)S(1)}, bf16[320,128]{1,0:T(8,128)(2,1)S(1)}, u32[]{:S(2)}, u32[]{:S(2)}) collective-permute-start(bf16[320,128]{1,0:T(8,128)(2,1)S(1)} %get-tuple-element.19), channel_id=1, source_target_pairs={{0,256},{128,384},{256,0},{384,128},{1,257},{129,385},{257,1},{385... | collective-permute-start | bytes 245768 | tf_op jit(solution)/shard_map/ppermute | solution.py:176
  161.8 4.0 %collective-permute-start.4 = (bf16[320,128]{1,0:T(8,128)(2,1)S(1)}, bf16[320,128]{1,0:T(8,128)(2,1)S(1)}, u32[]{:S(2)}, u32[]{:S(2)}) collective-permute-start(bf16[320,128]{1,0:T(8,128)(2,1)S(1)} %get-tuple-element.20), channel_id=1, source_target_pairs={{0,384},{128,0},{256,128},{384,256},{1,385},{129,1},{257,129},{385... | collective-permute-start | bytes 245768 | tf_op jit(solution)/shard_map/ppermute | solution.py:176
  165.8 0.0 collective-permute-done.2.f1
  165.8 0.0 collective-permute-done.3.f2
  165.8 2.3 %collective-permute-done.4.f3 = bf16[320,128]{1,0:T(8,128)(2,1)S(1)} collective-permute-done((bf16[320,128]{1,0:T(8,128)(2,1)S(1)}, bf16[320,128]{1,0:T(8,128)(2,1)S(1)}, u32[]{:S(2)}, u32[]{:S(2)}) %collective-permute-start.4) | collective-permute-done | bytes 81952 | tf_op jit(solution)/shard_map/ppermute | solution.py:176
  168.1 1.2 shard_map.93
  169.3 3.9 %all-to-all-start.5 = ((bf16[8,32,256]{2,1,0:T(8,128)(2,1)}), bf16[8,32,256]{2,1,0:T(8,128)(2,1)S(1)}, u32[]{:S(2)}, u32[]{:S(2)}) async-start(bf16[8,32,256]{2,1,0:T(8,128)(2,1)} %shard_map.93), calls=%async_computation.5 | async-start | bytes 262144 | tf_op jit(solution)/shard_map/all_to_all | solution.py:168
  173.3 0.9 shard_map.92
  174.2 8.2 %all-to-all-done.5 = bf16[8,32,256]{2,1,0:T(8,128)(2,1)S(1)} async-done(((bf16[8,32,256]{2,1,0:T(8,128)(2,1)}), bf16[8,32,256]{2,1,0:T(8,128)(2,1)S(1)}, u32[]{:S(2)}, u32[]{:S(2)}) %all-to-all-start.5) | async-done | bytes 131104 | tf_op jit(solution)/shard_map/all_to_all | solution.py:168
  182.4 0.7 bitcast_convert_fusion
Async XLA Ops:
  0.6 23.6 %copy-start.3 = (s32[1,1,96]{2,1,0:T(1,128)S(1)}, s32[1,1,96]{2,1,0:T(1,128)}, u32[]{:S(2)}) copy-start(s32[1,1,96]{2,1,0:T(1,128)} %param.10) | copy-start | bytes 1156
  0.6 23.6 %copy-start = (bf16[1,1,96,128,128]{4,3,2,1,0:T(8,128)(2,1)S(1)}, bf16[1,1,96,128,128]{4,3,2,1,0:T(8,128)(2,1)}, u32[]{:S(2)}) copy-start(bf16[1,1,96,128,128]{4,3,2,1,0:T(8,128)(2,1)} %param.9) | copy-start | bytes 9437188
  18.7 15.7 %all-to-all-start.1 = ((bf16[4,4,128,256]{3,2,1,0:T(8,128)(2,1)}), bf16[4,4,128,256]{3,2,1,0:T(8,128)(2,1)}, u32[]{:S(2)}, u32[]{:S(2)}) async-start(bf16[4,4,128,256]{3,2,1,0:T(8,128)(2,1)} %broadcast_in_dim.5), calls=%async_computation.1 | async-start | bytes 2097152 | tf_op jit(solution)/shard_map/all_to_all | solution.py:168
  36.7 4.6 %collective-permute-start = (bf16[16,128,256]{2,1,0:T(8,128)(2,1)S(1)}, bf16[16,128,256]{2,1,0:T(8,128)(2,1)S(1)}, u32[]{:S(2)}, u32[]{:S(2)}) collective-permute-start(bf16[16,128,256]{2,1,0:T(8,128)(2,1)S(1)} %shard_map.87), channel_id=1, source_target_pairs={{0,1},{1,0},{2,3},{3,2},{4,5},{5,4},{6,7},{7,6},{8,9},{9,8},{10,11... | collective-permute-start | bytes 3145736 | tf_op jit(solution)/shard_map/ppermute | solution.py:172
  41.0 44.4 %copy-start.1 = (bf16[256,256]{1,0:T(8,128)(2,1)S(1)}, bf16[256,256]{1,0:T(8,128)(2,1)}, u32[]{:S(2)}) copy-start(bf16[256,256]{1,0:T(8,128)(2,1)} %weight.3) | copy-start | bytes 393220
  41.0 44.4 %copy-start.2 = (bf16[128,256]{1,0:T(8,128)(2,1)S(1)}, bf16[128,256]{1,0:T(8,128)(2,1)}, u32[]{:S(2)}) copy-start(bf16[128,256]{1,0:T(8,128)(2,1)} %cotangent.1) | copy-start | bytes 196612
  127.5 4.9 %collective-permute-start.1 = (bf16[16,320,128]{2,1,0:T(8,128)(2,1)S(1)}, bf16[16,320,128]{2,1,0:T(8,128)(2,1)S(1)}, u32[]{:S(2)}, u32[]{:S(2)}) collective-permute-start(bf16[16,320,128]{2,1,0:T(8,128)(2,1)S(1)} %all_to_all.32.own), channel_id=1, source_target_pairs={{0,1},{1,0},{2,3},{3,2},{4,5},{5,4},{6,7},{7,6},{8,9},{9,8},{10,11... | collective-permute-start | bytes 3932168 | tf_op jit(solution)/shard_map/ppermute | solution.py:172
  154.3 11.4 %collective-permute-start.2 = (bf16[320,128]{1,0:T(8,128)(2,1)S(1)}, bf16[320,128]{1,0:T(8,128)(2,1)S(1)}, u32[]{:S(2)}, u32[]{:S(2)}) collective-permute-start(bf16[320,128]{1,0:T(8,128)(2,1)S(1)} %get-tuple-element.18), channel_id=1, source_target_pairs={{0,128},{128,256},{256,384},{384,0},{1,129},{129,257},{257,385},{3... | collective-permute-start | bytes 245768 | tf_op jit(solution)/shard_map/ppermute | solution.py:176
  156.6 9.2 %collective-permute-start.3 = (bf16[320,128]{1,0:T(8,128)(2,1)S(1)}, bf16[320,128]{1,0:T(8,128)(2,1)S(1)}, u32[]{:S(2)}, u32[]{:S(2)}) collective-permute-start(bf16[320,128]{1,0:T(8,128)(2,1)S(1)} %get-tuple-element.19), channel_id=1, source_target_pairs={{0,256},{128,384},{256,0},{384,128},{1,257},{129,385},{257,1},{385... | collective-permute-start | bytes 245768 | tf_op jit(solution)/shard_map/ppermute | solution.py:176
  161.8 6.3 %collective-permute-start.4 = (bf16[320,128]{1,0:T(8,128)(2,1)S(1)}, bf16[320,128]{1,0:T(8,128)(2,1)S(1)}, u32[]{:S(2)}, u32[]{:S(2)}) collective-permute-start(bf16[320,128]{1,0:T(8,128)(2,1)S(1)} %get-tuple-element.20), channel_id=1, source_target_pairs={{0,384},{128,0},{256,128},{384,256},{1,385},{129,1},{257,129},{385... | collective-permute-start | bytes 245768 | tf_op jit(solution)/shard_map/ppermute | solution.py:176
  169.3 13.0 %all-to-all-start.5 = ((bf16[8,32,256]{2,1,0:T(8,128)(2,1)}), bf16[8,32,256]{2,1,0:T(8,128)(2,1)S(1)}, u32[]{:S(2)}, u32[]{:S(2)}) async-start(bf16[8,32,256]{2,1,0:T(8,128)(2,1)} %shard_map.93), calls=%async_computation.5 | async-start | bytes 262144 | tf_op jit(solution)/shard_map/all_to_all | solution.py:168

commit v11 on v10

--- a/solution.py
+++ b/solution.py
@@ -23,7 +23,7 @@
 
 
 def plan_kernel(place, info, blocks, lists, groups):
-    count, core, zi = info[0], info[1], info[2]
+    count, core = info[0], info[1]
 
     def write(at, k, t, source, half, target):
         for f, value in enumerate((k, t, source, half, target)):
@@ -35,7 +35,7 @@
         z, x = a >> 2, a & 3
         half = t >> 1
         source = (x << 2) + z
-        target = (x << 2) + ((z - zi) & 3)
+        target = (x << 2) + z
         mine, theirs = held
         away = (t & 1) ^ core
         write(jnp.where(away == 0, mine, SLOTS + theirs), k, half, source, half, target)
@@ -120,33 +120,34 @@
         out[x, 1024:1088, :] = grad
 
 
-def fold_kernel(parts, f0, f1, f2, f3):
+def fold_kernel(parts, out):
     grad = parts[0, 1024:1088, :].astype(F32)
     for x in range(1, 4):
         grad += parts[x, 1024:1088, :].astype(F32)
     grad = grad.astype(BF)
-    for z, out in enumerate((f0, f1, f2, f3)):
+    for z in range(4):
         rows = slice(256 * z, 256 * z + 256)
         total = parts[0, rows, :].astype(F32)
         for x in range(1, 4):
             total += parts[x, rows, :].astype(F32)
-        out[0:256, :] = total.astype(BF)
-        out[256:320, :] = grad
-
-
-def grad_kernel(scale, info, f0, f1, f2, f3, grad_out, scratch):
-    for k, part in enumerate((f0, f1, f2, f3)):
-        scratch[(info[2] - k) & 3] = part[256:320, :].astype(F32)
-    grad = ((scratch[0] + scratch[1] + scratch[2] + scratch[3]) * scale).astype(BF)
+        out[z, 0:256, :] = total.astype(BF)
+        out[z, 256:320, :] = grad
+
+
+def grad_kernel(scale, parts, grad_out):
+    grad = parts[0, 256:320, :].astype(F32)
+    for z in range(1, 4):
+        grad += parts[z, 256:320, :].astype(F32)
+    grad = (grad * scale).astype(BF)
     for s in range(8):
         grad_out[s, :, 0:128] = grad[0:32]
         grad_out[s, :, 128:256] = grad[32:64]
 
 
-def last_kernel(f0, f1, f2, f3, weight, input_grad):
-    total = f0[0:256, :].astype(F32)
-    for part in (f1, f2, f3):
-        total += part[0:256, :].astype(F32)
+def last_kernel(parts, weight, input_grad):
+    total = parts[0, 0:256, :].astype(F32)
+    for z in range(1, 4):
+        total += parts[z, 0:256, :].astype(F32)
     back = total.astype(BF).astype(F32).T.astype(BF)
     input_grad[...] = dot(back, weight[...], (((1,), (1,)), ((), ()))).astype(BF)
 
@@ -172,14 +173,9 @@
     return lax.ppermute(value, "c", [(0, 1), (1, 0)])
 
 
-def rotate(value, axis, k):
-    return lax.ppermute(value, axis, [(i, (i + k) % 4) for i in range(4)])
-
-
 def shards(features, weight, cotangent, blocks, block_pos, counts):
     tile = blocks[0, 0]
-    index = [lax.axis_index(a).astype(jnp.int32) for a in ("c", "zl")]
-    info = jnp.stack([counts[0, 0]] + index)
+    info = jnp.stack([counts[0, 0], lax.axis_index("c").astype(jnp.int32)])
     nodes_total = 65536
     heavy = dict(flops=8 * 10**8, size=6 * 2**20)
     i32 = jnp.int32
@@ -225,16 +221,12 @@
         alias={5: 1},
         **heavy,
     )(lists, groups, tile, own, other, begun)
-    folded = call(fold_kernel, [((320, 128), BF, VMEM)] * 4, [VMEM])(exchange(back, "x"))
-    folded = [folded[0]] + [rotate(folded[k], "zl", k) for k in (1, 2, 3)]
-    (grad,) = call(
-        functools.partial(grad_kernel, 1.0 / math.sqrt(nodes_total)),
-        [((8, 32, 256), BF, VMEM)],
-        [SMEM] + [VMEM] * 4,
-        [pltpu.VMEM((4, 64, 128), F32)],
-    )(info, *folded)
+    (folded,) = call(fold_kernel, [((4, 320, 128), BF, VMEM)], [VMEM])(exchange(back, "x"))
+    folded = exchange(folded, "zl")
+    scale = 1.0 / math.sqrt(nodes_total)
+    (grad,) = call(functools.partial(grad_kernel, scale), [((8, 32, 256), BF, VMEM)], [VMEM])(folded)
     weight_grad = exchange(grad, "y").reshape(256, 256).astype(F32)
-    (input_grad,) = call(last_kernel, [((128, 256), BF, VMEM)], [VMEM] * 5, flops=2**24, size=2**20)(*folded, weight)
+    (input_grad,) = call(last_kernel, [((128, 256), BF, VMEM)], [VMEM] * 2, flops=2**24, size=2**20)(folded, weight)
     return (output, input_grad, weight_grad)
 
 

time: 184 us -> 185 us (level)
  blocking collectives: 120 us -> 134 us
  starting transfers between devices: 24 us -> 13.2 us
    all_to_all x4 -> x5, blocking collectives: 120 us -> 134 us  [exchange(): return lax.all_to_all(value, axes, 0, 0, tiled=True)]
    ppermute x3 -> x0, starting transfers between devices: 11.4 us -> none  [rotate(): return lax.ppermute(value, axis, [(i, (i + k) % 4) for i in range(4)])]
    ppermute x3 -> x0, waiting for transfers between devices: 2.35 us -> none  [rotate(): return lax.ppermute(value, axis, [(i, (i + k) % 4) for i in range(4)])]
  transfers between devices with their start and end apart: 7 -> 4, of which waited for: 5 -> 4; matrix products, arithmetic and copies ran while one was open for 0% -> 0% of each run, Pallas kernels for 4% -> 4%
where the time goes in v11:
time: 185 us; the launch traced here: 184 us
  blocking collectives  134 us (72%)
  waiting for transfers between devices  17.7 us (10%)
  Pallas kernels  14.2 us (8%)
  starting transfers between devices  13.2 us (7%)
  local copies, waits for them, and re-layouts  2.14 us (1%)
    all_to_all x5, blocking collectives, exchange(): return lax.all_to_all(value, axes, 0, 0, tiled=True)  134 us
    all_to_all x2, waiting for transfers between devices, exchange(): return lax.all_to_all(value, axes, 0, 0, tiled=True)  16.5 us
    all_to_all x2, starting transfers between devices, exchange(): return lax.all_to_all(value, axes, 0, 0, tiled=True)  9.38 us
    pallas_call x2, Pallas kernels, shards(): call(functools.partial(forward_kernel, which), [((16, 128, 256), BF, VMEM...  4.31 us
    ppermute x2, starting transfers between devices, swap(): return lax.ppermute(value, 'c', [(0, 1), (1, 0)])  3.83 us
  transfers between devices with their start and end apart: 4, of which 4 were waited for; matrix products, arithmetic and copies ran while one was open for 0% of the time, Pallas kernels for 4%

profile of v11, /device:TPU:6, one launch (start us, length us, event | category | flops | bytes accessed | tf_op | source)
XLA Modules:
  0.0 184.2 jit_solution(18257219114244282775)
XLA Ops:
  0.6 0.0 copy-start.3
  0.6 0.0 copy-start
  0.7 1.0 broadcast_in_dim.4
  1.7 15.9 %all_to_all.35 = bf16[4,128,256]{2,1,0:T(8,128)(2,1)S(1)} all-to-all(bf16[4,128,256]{2,1,0:T(8,128)(2,1)S(1)} %broadcast_in_dim.4), channel_id=1, replica_groups=mesh['zl'=4,'x'=4,'zh'=2,'y'=8,'c'=2] {'zl'}, dimensions={0} | all-to-all | bytes 524288 | tf_op jit(solution)/shard_map/all_to_all | solution.py:169
  17.6 1.1 broadcast_in_dim.5
  18.7 4.8 %all-to-all-start.1 = ((bf16[4,4,128,256]{3,2,1,0:T(8,128)(2,1)}), bf16[4,4,128,256]{3,2,1,0:T(8,128)(2,1)}, u32[]{:S(2)}, u32[]{:S(2)}) async-start(bf16[4,4,128,256]{3,2,1,0:T(8,128)(2,1)} %broadcast_in_dim.5), calls=%async_computation.1 | async-start | bytes 2097152 | tf_op jit(solution)/shard_map/all_to_all | solution.py:169
  24.1 0.1 pad_add_fusion.info
  24.2 0.0 copy-done.3
  24.2 0.0 copy-done
  24.2 1.8 shard_map.85
  26.0 8.3 %all-to-all-done.1 = bf16[4,4,128,256]{3,2,1,0:T(8,128)(2,1)} async-done(((bf16[4,4,128,256]{3,2,1,0:T(8,128)(2,1)}), bf16[4,4,128,256]{3,2,1,0:T(8,128)(2,1)}, u32[]{:S(2)}, u32[]{:S(2)}) %all-to-all-start.1) | async-done | bytes 1048608 | tf_op jit(solution)/shard_map/all_to_all | solution.py:169
  34.4 2.4 %shard_map.87 = bf16[16,128,256]{2,1,0:T(8,128)(2,1)S(1)} custom-call(s32[1120]{0:T(1024)S(1)} %get-tuple-element.8.lists, s32[2]{0:T(128)S(1)} %get-tuple-element.9.groups, bf16[96,128,128]{2,1,0:T(8,128)(2,1)S(1)} %bitcast.12, bf16[16,128,256]{2,1,0:T(8,128)(2,1)} %bitcast.4.nodes), custom_call_target="tpu_custom_call" | custom-call | flops 800000000 | bytes 6291456 | tf_op jit(solution)/shard_map/pallas_call | solution.py:193
  36.7 1.9 %collective-permute-start = (bf16[16,128,256]{2,1,0:T(8,128)(2,1)S(1)}, bf16[16,128,256]{2,1,0:T(8,128)(2,1)S(1)}, u32[]{:S(2)}, u32[]{:S(2)}) collective-permute-start(bf16[16,128,256]{2,1,0:T(8,128)(2,1)S(1)} %shard_map.87), channel_id=1, source_target_pairs={{0,1},{1,0},{2,3},{3,2},{4,5},{5,4},{6,7},{7,6},{8,9},{9,8},{10,11... | collective-permute-start | bytes 3145736 | tf_op jit(solution)/shard_map/ppermute | solution.py:173
  38.7 1.9 %shard_map.86 = bf16[16,128,256]{2,1,0:T(8,128)(2,1)S(1)} custom-call(s32[1120]{0:T(1024)S(1)} %get-tuple-element.8.lists, s32[2]{0:T(128)S(1)} %get-tuple-element.9.groups, bf16[96,128,128]{2,1,0:T(8,128)(2,1)S(1)} %bitcast.13, bf16[16,128,256]{2,1,0:T(8,128)(2,1)} %bitcast.4.nodes), custom_call_target="tpu_custom_call" | custom-call | flops 800000000 | bytes 6291456 | tf_op jit(solution)/shard_map/pallas_call | solution.py:193
  40.6 0.0 copy-start.1
  40.6 0.0 copy-start.2
  40.6 0.7 collective-permute-done
  41.3 0.3 add_convert_fusion
  41.6 45.2 %all_to_all.36.parts = bf16[16,128,256]{2,1,0:T(8,128)(2,1)S(1)} all-to-all(bf16[16,128,256]{2,1,0:T(8,128)(2,1)S(1)} %add_convert_fusion), channel_id=1, replica_groups=mesh['zl'=4,'x'=4,'zh'=2,'y'=8,'c'=2] {'zh','y'}, dimensions={0} | all-to-all | bytes 2097152 | tf_op jit(solution)/shard_map/all_to_all | solution.py:169
  86.9 0.0 copy-done.1
  86.9 0.0 copy-done.2
  86.9 0.9 shard_map.88
  87.8 41.1 %all_to_all.37.own = bf16[16,320,128]{2,1,0:T(8,128)(2,1)S(1)} all-to-all(bf16[16,320,128]{2,1,0:T(8,128)(2,1)S(1)} %get-tuple-element.11), channel_id=1, replica_groups=mesh['zl'=4,'x'=4,'zh'=2,'y'=8,'c'=2] {'zh','y'}, dimensions={0} | all-to-all | bytes 2621440 | tf_op jit(solution)/shard_map/all_to_all | solution.py:169
  128.9 1.9 %collective-permute-start.1 = (bf16[16,320,128]{2,1,0:T(8,128)(2,1)S(1)}, bf16[16,320,128]{2,1,0:T(8,128)(2,1)S(1)}, u32[]{:S(2)}, u32[]{:S(2)}) collective-permute-start(bf16[16,320,128]{2,1,0:T(8,128)(2,1)S(1)} %all_to_all.37.own), channel_id=1, source_target_pairs={{0,1},{1,0},{2,3},{3,2},{4,5},{5,4},{6,7},{7,6},{8,9},{9,8},{10,11... | collective-permute-start | bytes 3932168 | tf_op jit(solution)/shard_map/ppermute | solution.py:173
  130.8 2.5 %shard_map.89.begun = f32[17,256,128]{2,1,0:T(8,128)S(1)} custom-call(s32[1120]{0:T(1024)S(1)} %get-tuple-element.8.lists, s32[2]{0:T(128)S(1)} %get-tuple-element.9.groups, bf16[96,128,128]{2,1,0:T(8,128)(2,1)} %bitcast.9, bf16[16,320,128]{2,1,0:T(8,128)(2,1)S(1)} %all_to_all.37.own), custom_call_target="tpu_custom_call" | custom-call | flops 800000000 | bytes 6291456 | tf_op jit(solution)/shard_map/pallas_call | solution.py:211
  133.3 0.5 collective-permute-done.1.other
  133.8 3.0 %shard_map.90 = (bf16[4,1088,128]{2,1,0:T(8,128)(2,1)S(1)}, f32[17,256,128]{2,1,0:T(8,128)S(1)}) custom-call(s32[1120]{0:T(1024)S(1)} %get-tuple-element.8.lists, s32[2]{0:T(128)S(1)} %get-tuple-element.9.groups, bf16[96,128,128]{2,1,0:T(8,128)(2,1)} %bitcast.10, bf16[16,320,128]{2,1,0:T(8,128)(2,1)S(1)} %all_to_all.37.own, ...), custom_call_target="tpu_custom_call", output_to_operand_aliasing={{1}: (5, {})} | custom-call | flops 800000000 | bytes 6291456 | tf_op jit(solution)/shard_map/pallas_call | solution.py:217
  136.8 18.3 %all_to_all.38.parts = bf16[4,1088,128]{2,1,0:T(8,128)(2,1)S(1)} all-to-all(bf16[4,1088,128]{2,1,0:T(8,128)(2,1)S(1)} %get-tuple-element.12), channel_id=1, replica_groups=mesh['zl'=4,'x'=4,'zh'=2,'y'=8,'c'=2] {'x'}, dimensions={0} | all-to-all | bytes 2228224 | tf_op jit(solution)/shard_map/all_to_all | solution.py:169
  155.1 0.1 shard_map.91
  155.3 13.8 %all_to_all.39.parts = bf16[4,320,128]{2,1,0:T(8,128)(2,1)S(1)} all-to-all(bf16[4,320,128]{2,1,0:T(8,128)(2,1)S(1)} %shard_map.91), channel_id=1, replica_groups=mesh['zl'=4,'x'=4,'zh'=2,'y'=8,'c'=2] {'zl'}, dimensions={0} | all-to-all | bytes 655360 | tf_op jit(solution)/shard_map/all_to_all | solution.py:169
  169.1 0.7 shard_map.93
  169.8 4.6 %all-to-all-start.6 = ((bf16[8,32,256]{2,1,0:T(8,128)(2,1)}), bf16[8,32,256]{2,1,0:T(8,128)(2,1)S(1)}, u32[]{:S(2)}, u32[]{:S(2)}) async-start(bf16[8,32,256]{2,1,0:T(8,128)(2,1)} %shard_map.93), calls=%async_computation.6 | async-start | bytes 262144 | tf_op jit(solution)/shard_map/all_to_all | solution.py:169
  174.4 0.9 shard_map.92
  175.2 8.2 %all-to-all-done.6 = bf16[8,32,256]{2,1,0:T(8,128)(2,1)S(1)} async-done(((bf16[8,32,256]{2,1,0:T(8,128)(2,1)}), bf16[8,32,256]{2,1,0:T(8,128)(2,1)S(1)}, u32[]{:S(2)}, u32[]{:S(2)}) %all-to-all-start.6) | async-done | bytes 131104 | tf_op jit(solution)/shard_map/all_to_all | solution.py:169
  183.5 0.7 bitcast_convert_fusion
Async XLA Ops:
  0.6 23.6 %copy-start.3 = (s32[1,1,96]{2,1,0:T(1,128)S(1)}, s32[1,1,96]{2,1,0:T(1,128)}, u32[]{:S(2)}) copy-start(s32[1,1,96]{2,1,0:T(1,128)} %param.10) | copy-start | bytes 1156
  0.6 23.6 %copy-start = (bf16[1,1,96,128,128]{4,3,2,1,0:T(8,128)(2,1)S(1)}, bf16[1,1,96,128,128]{4,3,2,1,0:T(8,128)(2,1)}, u32[]{:S(2)}) copy-start(bf16[1,1,96,128,128]{4,3,2,1,0:T(8,128)(2,1)} %param.9) | copy-start | bytes 9437188
  18.7 15.7 %all-to-all-start.1 = ((bf16[4,4,128,256]{3,2,1,0:T(8,128)(2,1)}), bf16[4,4,128,256]{3,2,1,0:T(8,128)(2,1)}, u32[]{:S(2)}, u32[]{:S(2)}) async-start(bf16[4,4,128,256]{3,2,1,0:T(8,128)(2,1)} %broadcast_in_dim.5), calls=%async_computation.1 | async-start | bytes 2097152 | tf_op jit(solution)/shard_map/all_to_all | solution.py:169
  36.7 4.6 %collective-permute-start = (bf16[16,128,256]{2,1,0:T(8,128)(2,1)S(1)}, bf16[16,128,256]{2,1,0:T(8,128)(2,1)S(1)}, u32[]{:S(2)}, u32[]{:S(2)}) collective-permute-start(bf16[16,128,256]{2,1,0:T(8,128)(2,1)S(1)} %shard_map.87), channel_id=1, source_target_pairs={{0,1},{1,0},{2,3},{3,2},{4,5},{5,4},{6,7},{7,6},{8,9},{9,8},{10,11... | collective-permute-start | bytes 3145736 | tf_op jit(solution)/shard_map/ppermute | solution.py:173
  40.6 46.3 %copy-start.1 = (bf16[256,256]{1,0:T(8,128)(2,1)S(1)}, bf16[256,256]{1,0:T(8,128)(2,1)}, u32[]{:S(2)}) copy-start(bf16[256,256]{1,0:T(8,128)(2,1)} %weight.3) | copy-start | bytes 393220
  40.6 46.2 %copy-start.2 = (bf16[128,256]{1,0:T(8,128)(2,1)S(1)}, bf16[128,256]{1,0:T(8,128)(2,1)}, u32[]{:S(2)}) copy-start(bf16[128,256]{1,0:T(8,128)(2,1)} %cotangent.1) | copy-start | bytes 196612
  128.9 4.9 %collective-permute-start.1 = (bf16[16,320,128]{2,1,0:T(8,128)(2,1)S(1)}, bf16[16,320,128]{2,1,0:T(8,128)(2,1)S(1)}, u32[]{:S(2)}, u32[]{:S(2)}) collective-permute-start(bf16[16,320,128]{2,1,0:T(8,128)(2,1)S(1)} %all_to_all.37.own), channel_id=1, source_target_pairs={{0,1},{1,0},{2,3},{3,2},{4,5},{5,4},{6,7},{7,6},{8,9},{9,8},{10,11... | collective-permute-start | bytes 3932168 | tf_op jit(solution)/shard_map/ppermute | solution.py:173
  169.8 13.7 %all-to-all-start.6 = ((bf16[8,32,256]{2,1,0:T(8,128)(2,1)}), bf16[8,32,256]{2,1,0:T(8,128)(2,1)S(1)}, u32[]{:S(2)}, u32[]{:S(2)}) async-start(bf16[8,32,256]{2,1,0:T(8,128)(2,1)} %shard_map.93), calls=%async_computation.6 | async-start | bytes 262144 | tf_op jit(solution)/shard_map/all_to_all | solution.py:169

commit v12 on v11

--- a/solution.py
+++ b/solution.py
@@ -81,12 +81,10 @@
     slopes32 = cotangent[...].astype(F32) * slope
     slopes = slopes32.astype(BF)
     turned = slopes.astype(F32).T.astype(BF)
-    grad = dot(share.astype(F32).T.astype(BF), slopes).astype(BF)
+    columns = share.astype(F32).T.astype(BF)
     for s in range(16):
         spread[s, 0:256, :] = turned
-        rows = slice(32 * (s % 8), 32 * (s % 8) + 32)
-        spread[s, 256:288, :] = grad[rows, 0:128]
-        spread[s, 288:320, :] = grad[rows, 128:256]
+        spread[s, 256:288, :] = columns[32 * (s % 8) : 32 * (s % 8) + 32]
 
 
 def back_products(which, lists, groups, blocks, source, acc):
@@ -103,21 +101,27 @@
     lax.fori_loop(0, groups[which], step, 0)
 
 
-def backward_own_kernel(lists, groups, blocks, own, acc):
+def chunk_sum(part):
+    total = jnp.zeros((32, 256), F32)
+    for s in range(16):
+        total += dot(part[s, 256:288, :], part[s, 0:256, :], (((1,), (1,)), ((), ())))
+    return total
+
+
+def backward_own_kernel(lists, groups, blocks, own, acc, half):
+    half[...] = chunk_sum(own)
     acc[...] = jnp.zeros_like(acc)
     back_products(0, lists, groups, blocks, own, acc)
 
 
-def backward_other_kernel(lists, groups, blocks, own, other, begun, out, acc):
+def backward_other_kernel(lists, groups, blocks, other, half, begun, out, acc):
     back_products(1, lists, groups, blocks, other, acc)
-    grad = jnp.zeros((64, 128), F32)
-    for s in range(16):
-        grad += own[s, 256:320, :].astype(F32) + other[s, 256:320, :].astype(F32)
-    grad = grad.astype(BF)
+    grad = (half[...] + chunk_sum(other)).astype(BF)
     for x in range(4):
         for z in range(4):
             out[x, 256 * z : 256 * z + 256, :] = acc[4 * x + z].astype(BF)
-        out[x, 1024:1088, :] = grad
+        out[x, 1024:1056, :] = grad[:, 0:128]
+        out[x, 1056:1088, :] = grad[:, 128:256]
 
 
 def fold_kernel(parts, out):
@@ -203,14 +207,14 @@
     parts = exchange(pair, ("zh", "y"))
     output, spread = call(
         middle_kernel,
-        [((128, 256), BF, VMEM), ((16, 320, 128), BF, VMEM)],
+        [((128, 256), BF, VMEM), ((16, 288, 128), BF, VMEM)],
         [VMEM, VMEM, VMEM],
     )(parts, weight, cotangent)
     own = exchange(spread, ("zh", "y"))
     other = swap(own)
-    (begun,) = call(
+    begun, half = call(
         backward_own_kernel,
-        [((17, 256, 128), F32, VMEM)],
+        [((17, 256, 128), F32, VMEM), ((32, 256), F32, VMEM)],
         [SMEM, SMEM, VMEM, VMEM],
         **heavy,
     )(lists, groups, tile, own)
@@ -220,7 +224,7 @@
         [SMEM, SMEM] + [VMEM] * 4,
         alias={5: 1},
         **heavy,
-    )(lists, groups, tile, own, other, begun)
+    )(lists, groups, tile, other, half, begun)
     (folded,) = call(fold_kernel, [((4, 320, 128), BF, VMEM)], [VMEM])(exchange(back, "x"))
     folded = exchange(folded, "zl")
     scale = 1.0 / math.sqrt(nodes_total)

time: 185 us -> 183 us (0.989)
  transfers between devices with their start and end apart: 4 -> 4, of which waited for: 4 -> 3; matrix products, arithmetic and copies ran while one was open for 0% -> 0% of each run, Pallas kernels for 4% -> 5%
where the time goes in v12:
time: 183 us
  blocking collectives  134 us (73%)
  waiting for transfers between devices  16.5 us (9%)
  Pallas kernels  15.8 us (9%)
  starting transfers between devices  12 us (7%)
  local copies, waits for them, and re-layouts  2.14 us (1%)
    all_to_all x5, blocking collectives, exchange(): return lax.all_to_all(value, axes, 0, 0, tiled=True)  134 us
    all_to_all x2, waiting for transfers between devices, exchange(): return lax.all_to_all(value, axes, 0, 0, tiled=True)  16.3 us
    all_to_all x2, starting transfers between devices, exchange(): return lax.all_to_all(value, axes, 0, 0, tiled=True)  8.14 us
    pallas_call x2, Pallas kernels, shards(): call(functools.partial(forward_kernel, which), [((16, 128, 256), BF, VMEM...  4.7 us
    ppermute x2, starting transfers between devices, swap(): return lax.ppermute(value, 'c', [(0, 1), (1, 0)])  3.83 us
  transfers between devices with their start and end apart: 4, of which 3 were waited for; matrix products, arithmetic and copies ran while one was open for 0% of the time, Pallas kernels for 5%

profile of v12, /device:TPU:6, one launch (start us, length us, event | category | flops | bytes accessed | tf_op | source)
XLA Modules:
  0.0 182.6 jit_solution(15802544928391565669)
XLA Ops:
  0.6 0.0 copy-start.3
  0.6 0.0 copy-start
  0.7 1.0 broadcast_in_dim.4
  1.7 15.9 %all_to_all.35 = bf16[4,128,256]{2,1,0:T(8,128)(2,1)S(1)} all-to-all(bf16[4,128,256]{2,1,0:T(8,128)(2,1)S(1)} %broadcast_in_dim.4), channel_id=1, replica_groups=mesh['zl'=4,'x'=4,'zh'=2,'y'=8,'c'=2] {'zl'}, dimensions={0} | all-to-all | bytes 524288 | tf_op jit(solution)/shard_map/all_to_all | solution.py:173
  17.6 1.1 broadcast_in_dim.5
  18.7 4.8 %all-to-all-start.1 = ((bf16[4,4,128,256]{3,2,1,0:T(8,128)(2,1)}), bf16[4,4,128,256]{3,2,1,0:T(8,128)(2,1)}, u32[]{:S(2)}, u32[]{:S(2)}) async-start(bf16[4,4,128,256]{3,2,1,0:T(8,128)(2,1)} %broadcast_in_dim.5), calls=%async_computation.1 | async-start | bytes 2097152 | tf_op jit(solution)/shard_map/all_to_all | solution.py:173
  24.1 0.1 pad_add_fusion.info
  24.2 0.0 copy-done.3
  24.2 0.0 copy-done
  24.2 2.0 %shard_map.85 = (s32[1120]{0:T(1024)S(1)}, s32[2]{0:T(128)S(1)}) custom-call(s32[96]{0:T(128)S(1)} %bitcast.14, s32[2]{0:T(128)S(1)} %pad_add_fusion.info, bf16[96,128,128]{2,1,0:T(8,128)(2,1)S(1)} %bitcast.11), custom_call_target="tpu_custom_call" | custom-call | bytes 1048576 | tf_op jit(solution)/shard_map/pallas_call | solution.py:187
  26.2 8.1 %all-to-all-done.1 = bf16[4,4,128,256]{3,2,1,0:T(8,128)(2,1)} async-done(((bf16[4,4,128,256]{3,2,1,0:T(8,128)(2,1)}), bf16[4,4,128,256]{3,2,1,0:T(8,128)(2,1)}, u32[]{:S(2)}, u32[]{:S(2)}) %all-to-all-start.1) | async-done | bytes 1048608 | tf_op jit(solution)/shard_map/all_to_all | solution.py:173
  34.4 2.4 %shard_map.87 = bf16[16,128,256]{2,1,0:T(8,128)(2,1)S(1)} custom-call(s32[1120]{0:T(1024)S(1)} %get-tuple-element.10.lists, s32[2]{0:T(128)S(1)} %get-tuple-element.11.groups, bf16[96,128,128]{2,1,0:T(8,128)(2,1)S(1)} %bitcast.12, bf16[16,128,256]{2,1,0:T(8,128)(2,1)} %bitcast.4.nodes), custom_call_target="tpu_custom_call" | custom-call | flops 800000000 | bytes 6291456 | tf_op jit(solution)/shard_map/pallas_call | solution.py:197
  36.7 1.9 %collective-permute-start = (bf16[16,128,256]{2,1,0:T(8,128)(2,1)S(1)}, bf16[16,128,256]{2,1,0:T(8,128)(2,1)S(1)}, u32[]{:S(2)}, u32[]{:S(2)}) collective-permute-start(bf16[16,128,256]{2,1,0:T(8,128)(2,1)S(1)} %shard_map.87), channel_id=1, source_target_pairs={{0,1},{1,0},{2,3},{3,2},{4,5},{5,4},{6,7},{7,6},{8,9},{9,8},{10,11... | collective-permute-start | bytes 3145736 | tf_op jit(solution)/shard_map/ppermute | solution.py:177
  38.6 2.4 %shard_map.86 = bf16[16,128,256]{2,1,0:T(8,128)(2,1)S(1)} custom-call(s32[1120]{0:T(1024)S(1)} %get-tuple-element.10.lists, s32[2]{0:T(128)S(1)} %get-tuple-element.11.groups, bf16[96,128,128]{2,1,0:T(8,128)(2,1)S(1)} %bitcast.13, bf16[16,128,256]{2,1,0:T(8,128)(2,1)} %bitcast.4.nodes), custom_call_target="tpu_custom_call" | custom-call | flops 800000000 | bytes 6291456 | tf_op jit(solution)/shard_map/pallas_call | solution.py:197
  41.0 0.0 copy-start.1
  41.0 0.0 copy-start.2
  41.0 0.2 collective-permute-done
  41.3 0.3 add_convert_fusion
  41.6 44.4 %all_to_all.36.parts = bf16[16,128,256]{2,1,0:T(8,128)(2,1)S(1)} all-to-all(bf16[16,128,256]{2,1,0:T(8,128)(2,1)S(1)} %add_convert_fusion), channel_id=1, replica_groups=mesh['zl'=4,'x'=4,'zh'=2,'y'=8,'c'=2] {'zh','y'}, dimensions={0} | all-to-all | bytes 2097152 | tf_op jit(solution)/shard_map/all_to_all | solution.py:173
  86.0 0.0 copy-done.1
  86.0 0.0 copy-done.2
  86.0 0.9 shard_map.88
  86.9 38.4 %all_to_all.37.own = bf16[16,288,128]{2,1,0:T(8,128)(2,1)S(1)} all-to-all(bf16[16,288,128]{2,1,0:T(8,128)(2,1)S(1)} %get-tuple-element.13), channel_id=1, replica_groups=mesh['zl'=4,'x'=4,'zh'=2,'y'=8,'c'=2] {'zh','y'}, dimensions={0} | all-to-all | bytes 2359296 | tf_op jit(solution)/shard_map/all_to_all | solution.py:173
  125.3 1.9 %collective-permute-start.1 = (bf16[16,288,128]{2,1,0:T(8,128)(2,1)S(1)}, bf16[16,288,128]{2,1,0:T(8,128)(2,1)S(1)}, u32[]{:S(2)}, u32[]{:S(2)}) collective-permute-start(bf16[16,288,128]{2,1,0:T(8,128)(2,1)S(1)} %all_to_all.37.own), channel_id=1, source_target_pairs={{0,1},{1,0},{2,3},{3,2},{4,5},{5,4},{6,7},{7,6},{8,9},{9,8},{10,11... | collective-permute-start | bytes 3538952 | tf_op jit(solution)/shard_map/ppermute | solution.py:177
  127.2 3.2 %shard_map.89 = (f32[17,256,128]{2,1,0:T(8,128)S(1)}, f32[32,256]{1,0:T(8,128)S(1)}) custom-call(s32[1120]{0:T(1024)S(1)} %get-tuple-element.10.lists, s32[2]{0:T(128)S(1)} %get-tuple-element.11.groups, bf16[96,128,128]{2,1,0:T(8,128)(2,1)} %bitcast.9, bf16[16,288,128]{2,1,0:T(8,128)(2,1)S(1)} %all_to_all.37.own), custom_call_target="tpu_custom_call" | custom-call | flops 800000000 | bytes 6291456 | tf_op jit(solution)/shard_map/pallas_call | solution.py:215
  130.5 0.0 collective-permute-done.1.other
  130.5 3.3 %shard_map.90 = (bf16[4,1088,128]{2,1,0:T(8,128)(2,1)S(1)}, f32[17,256,128]{2,1,0:T(8,128)S(1)}) custom-call(s32[1120]{0:T(1024)S(1)} %get-tuple-element.10.lists, s32[2]{0:T(128)S(1)} %get-tuple-element.11.groups, bf16[96,128,128]{2,1,0:T(8,128)(2,1)} %bitcast.10, ...), custom_call_target="tpu_custom_call", output_to_operand_aliasing={{1}: (5, {})} | custom-call | flops 800000000 | bytes 6291456 | tf_op jit(solution)/shard_map/pallas_call | solution.py:221
  133.7 19.2 %all_to_all.38.parts = bf16[4,1088,128]{2,1,0:T(8,128)(2,1)S(1)} all-to-all(bf16[4,1088,128]{2,1,0:T(8,128)(2,1)S(1)} %get-tuple-element.16), channel_id=1, replica_groups=mesh['zl'=4,'x'=4,'zh'=2,'y'=8,'c'=2] {'x'}, dimensions={0} | all-to-all | bytes 2228224 | tf_op jit(solution)/shard_map/all_to_all | solution.py:173
  153.0 0.1 shard_map.91
  153.1 15.7 %all_to_all.39.parts = bf16[4,320,128]{2,1,0:T(8,128)(2,1)S(1)} all-to-all(bf16[4,320,128]{2,1,0:T(8,128)(2,1)S(1)} %shard_map.91), channel_id=1, replica_groups=mesh['zl'=4,'x'=4,'zh'=2,'y'=8,'c'=2] {'zl'}, dimensions={0} | all-to-all | bytes 655360 | tf_op jit(solution)/shard_map/all_to_all | solution.py:173
  168.8 0.7 shard_map.93
  169.5 3.4 %all-to-all-start.6 = ((bf16[8,32,256]{2,1,0:T(8,128)(2,1)}), bf16[8,32,256]{2,1,0:T(8,128)(2,1)S(1)}, u32[]{:S(2)}, u32[]{:S(2)}) async-start(bf16[8,32,256]{2,1,0:T(8,128)(2,1)} %shard_map.93), calls=%async_computation.6 | async-start | bytes 262144 | tf_op jit(solution)/shard_map/all_to_all | solution.py:173
  172.8 0.9 shard_map.92
  173.7 8.1 %all-to-all-done.6 = bf16[8,32,256]{2,1,0:T(8,128)(2,1)S(1)} async-done(((bf16[8,32,256]{2,1,0:T(8,128)(2,1)}), bf16[8,32,256]{2,1,0:T(8,128)(2,1)S(1)}, u32[]{:S(2)}, u32[]{:S(2)}) %all-to-all-start.6) | async-done | bytes 131104 | tf_op jit(solution)/shard_map/all_to_all | solution.py:173
  181.8 0.7 bitcast_convert_fusion
Async XLA Ops:
  0.6 23.6 %copy-start.3 = (s32[1,1,96]{2,1,0:T(1,128)S(1)}, s32[1,1,96]{2,1,0:T(1,128)}, u32[]{:S(2)}) copy-start(s32[1,1,96]{2,1,0:T(1,128)} %param.10) | copy-start | bytes 1156
  0.6 23.6 %copy-start = (bf16[1,1,96,128,128]{4,3,2,1,0:T(8,128)(2,1)S(1)}, bf16[1,1,96,128,128]{4,3,2,1,0:T(8,128)(2,1)}, u32[]{:S(2)}) copy-start(bf16[1,1,96,128,128]{4,3,2,1,0:T(8,128)(2,1)} %param.9) | copy-start | bytes 9437188
  18.7 15.7 %all-to-all-start.1 = ((bf16[4,4,128,256]{3,2,1,0:T(8,128)(2,1)}), bf16[4,4,128,256]{3,2,1,0:T(8,128)(2,1)}, u32[]{:S(2)}, u32[]{:S(2)}) async-start(bf16[4,4,128,256]{3,2,1,0:T(8,128)(2,1)} %broadcast_in_dim.5), calls=%async_computation.1 | async-start | bytes 2097152 | tf_op jit(solution)/shard_map/all_to_all | solution.py:173
  36.7 4.6 %collective-permute-start = (bf16[16,128,256]{2,1,0:T(8,128)(2,1)S(1)}, bf16[16,128,256]{2,1,0:T(8,128)(2,1)S(1)}, u32[]{:S(2)}, u32[]{:S(2)}) collective-permute-start(bf16[16,128,256]{2,1,0:T(8,128)(2,1)S(1)} %shard_map.87), channel_id=1, source_target_pairs={{0,1},{1,0},{2,3},{3,2},{4,5},{5,4},{6,7},{7,6},{8,9},{9,8},{10,11... | collective-permute-start | bytes 3145736 | tf_op jit(solution)/shard_map/ppermute | solution.py:177
  41.0 45.0 %copy-start.1 = (bf16[256,256]{1,0:T(8,128)(2,1)S(1)}, bf16[256,256]{1,0:T(8,128)(2,1)}, u32[]{:S(2)}) copy-start(bf16[256,256]{1,0:T(8,128)(2,1)} %weight.3) | copy-start | bytes 393220
  41.0 45.0 %copy-start.2 = (bf16[128,256]{1,0:T(8,128)(2,1)S(1)}, bf16[128,256]{1,0:T(8,128)(2,1)}, u32[]{:S(2)}) copy-start(bf16[128,256]{1,0:T(8,128)(2,1)} %cotangent.1) | copy-start | bytes 196612
  125.3 5.2 %collective-permute-start.1 = (bf16[16,288,128]{2,1,0:T(8,128)(2,1)S(1)}, bf16[16,288,128]{2,1,0:T(8,128)(2,1)S(1)}, u32[]{:S(2)}, u32[]{:S(2)}) collective-permute-start(bf16[16,288,128]{2,1,0:T(8,128)(2,1)S(1)} %all_to_all.37.own), channel_id=1, source_target_pairs={{0,1},{1,0},{2,3},{3,2},{4,5},{5,4},{6,7},{7,6},{8,9},{9,8},{10,11... | collective-permute-start | bytes 3538952 | tf_op jit(solution)/shard_map/ppermute | solution.py:177
  169.5 12.4 %all-to-all-start.6 = ((bf16[8,32,256]{2,1,0:T(8,128)(2,1)}), bf16[8,32,256]{2,1,0:T(8,128)(2,1)S(1)}, u32[]{:S(2)}, u32[]{:S(2)}) async-start(bf16[8,32,256]{2,1,0:T(8,128)(2,1)} %shard_map.93), calls=%async_computation.6 | async-start | bytes 262144 | tf_op jit(solution)/shard_map/all_to_all | solution.py:173
